TPU v7x, 256 devices: a whole 4x4x8 slice. The times are simulated.
256 devices in a mesh: rep: 32 (over z_hi, x, core), tp: 8 (over y, z_lo).
Axes of the slice: x: 4, y: 4, z: 8 (z_hi: 4, z_lo: 2; z = z_hi * 2 + z_lo), core: 2. Of those that a mesh axis runs over, the one named last changes fastest.
Arguments:
- queries: bfloat16 [64, 1024, 3072], P('rep', None, 'tp'), as said below
- keys: bfloat16 [64, 1024, 3072], P('rep', None, 'tp'), as said below
- values: bfloat16 [64, 1024, 3072], P('rep', None, 'tp'), may hold values from -6 to 6
- output_weight: bfloat16 [3072, 3072], P('tp'), may hold values from -0.109375 to 0.109375
- adapter_down_pool: bfloat16 [128, 3072, 64], P('rep', 'tp'), may hold values from -0.109375 to 0.109375
- adapter_up_pool: bfloat16 [128, 64, 3072], P('rep', None, 'tp'), may hold values from -0.3984375 to 0.3984375
- residual: bfloat16 [64, 1024, 3072], P('rep', None, 'tp'), may hold values from -3 to 3
- gate: bfloat16 [64, 3072], P('rep', 'tp'), may hold values from 0.5 to 1.5
- adapter_id: int32 [32], replicated, may hold values from 0 to 127
- adapter_slot: int32 [128], replicated, may hold values from 0 to 127, each once
- request_count: int32 [32], replicated, may hold values from 1 to 2, as said below
Outputs:
- updated: bfloat16 [64, 1024, 3072], P('rep', None, 'tp')
Inputs may be any that keep to these rules, and one draw needn't show every extreme that they name: `request_count`: live slots of a replica; some replica has all 2 live, some has one. `adapter_slot`: slot s of the pool lies on replica index s // 4. `queries`: entries lie between -8 and 8. `keys`: entries lie between -8 and 8.
All inputs are finite; a program needn't handle non-finite values.
Results may differ from a plain program's by a relative error of at most 0.01.
Values may be sent and summed in bfloat16 or wider, within the bound.
No kernel may reach another device: no remote copies, remote signals or barrier semaphores. Data moves between devices by JAX's collectives and lax.ppermute only.
A program may use at most 128 MiB of HBM per device.

v0:
```python
import jax
import jax.numpy as jnp
from jax import lax
from jax.sharding import PartitionSpec as P

HD = 128


def attend(query_rows, key_rows, value_rows):
    batch_n, seq_n, width = query_rows.shape
    heads_here = width // HD
    query_heads = query_rows.reshape(batch_n, seq_n, heads_here, HD)
    key_heads = key_rows.reshape(batch_n, seq_n, heads_here, HD)
    value_heads = value_rows.reshape(batch_n, seq_n, heads_here, HD)
    score_scale = HD ** (-0.5)
    scores = (
        jnp.einsum("bqhd,bkhd->bhqk", query_heads, key_heads, preferred_element_type=jnp.float32)
        * score_scale
    )
    highest = jnp.max(scores, axis=-1, keepdims=True)
    expos = jnp.exp(scores - highest)
    probs = (expos / jnp.sum(expos, axis=-1, keepdims=True)).astype(jnp.bfloat16)
    mixed = jnp.einsum("bhqk,bkhd->bqhd", probs, value_heads, preferred_element_type=jnp.float32)
    return mixed.reshape(batch_n * seq_n, width).astype(jnp.bfloat16)


def per_device(
    queries,
    keys,
    values,
    output_weight,
    adapter_down_pool,
    adapter_up_pool,
    residual,
    gate,
    adapter_id,
    adapter_slot,
    request_count,
):
    replica = lax.axis_index("rep")
    wanted = adapter_slot[adapter_id[replica]]
    pieces = (
        lax.all_gather(adapter_down_pool, "rep", axis=0, tiled=True),
        lax.all_gather(adapter_up_pool, "rep", axis=0, tiled=True),
    )
    piece_rows = pieces[0].shape[0]
    matches = (jnp.arange(piece_rows, dtype=jnp.int32) == wanted).astype(jnp.float32)
    down_part = jnp.einsum("n,nij->ij", matches, pieces[0].astype(jnp.float32))
    up_part = jnp.einsum("n,nij->ij", matches, pieces[1].astype(jnp.float32))
    lowrank_down_rows = down_part.astype(jnp.bfloat16)
    up_cols = up_part.astype(jnp.bfloat16)
    attended = attend(queries, keys, values)
    batch_n, seq_n, width = residual.shape
    complete_up_factor = lax.all_gather(up_cols, "tp", axis=1, tiled=True)
    lowrank_adapter = jnp.dot(
        lowrank_down_rows, complete_up_factor, preferred_element_type=jnp.float32
    )
    merged_rows = (output_weight.astype(jnp.float32) + lowrank_adapter).astype(jnp.bfloat16)
    partial_terms = jnp.dot(attended, merged_rows, preferred_element_type=jnp.float32)
    projected = lax.psum_scatter(partial_terms, "tp", scatter_dimension=1, tiled=True)
    active = (jnp.arange(batch_n, dtype=jnp.int32) < request_count[replica]).astype(jnp.float32)
    update = (
        gate.astype(jnp.float32)[:, None, :]
        * projected.reshape(batch_n, seq_n, width)
        * active[:, None, None]
    )
    return (residual.astype(jnp.float32) + update).astype(jnp.bfloat16)


def solution(mesh):
    placed = (
        P("rep", None, "tp"),
        P("rep", None, "tp"),
        P("rep", None, "tp"),
        P("tp", None),
        P("rep", "tp", None),
        P("rep", None, "tp"),
        P("rep", None, "tp"),
        P("rep", "tp"),
        P(),
        P(),
        P(),
    )
    return jax.shard_map(
        per_device, mesh=mesh, in_specs=placed, out_specs=P("rep", None, "tp"), check_vma=False
    )
```

profile of v0, /device:TPU:32, one launch (start us, length us, event | category | flops | bytes accessed | tf_op | source)
XLA Modules:
  0.0 669.2 jit_solution(5735290523523146548)
XLA Ops:
  6.5 0.0 copy-start
  6.5 0.0 all-gather.5.cloned.1.call-start
  6.5 0.7 all-gather.5.cloned.1.call-update
  7.3 0.0 all-gather.3.cloned.1.call-start
  7.3 0.7 all-gather.3.cloned.1.call-update
  8.0 0.0 reduce-scatter.2.cloned.1.call-start
  8.1 1.3 dynamic_slice.9
  10.6 0.0 copy-start.1
  10.6 2.7 copy.24
  13.3 0.0 copy-done
  13.3 1.6 copy.25
  14.9 0.0 copy-done.1
  14.9 0.7 copy.28
  15.7 14.2 %fusion.24 = (f32[2,3,1024]{2,1,0:T(4,128)S(1)}, f32[2,3,1024,1024]{2,3,1,0:T(8,128)}) fusion(bf16[2,1024,3,128]{1,3,2,0:T(8,128)(2,1)} %bitcast.38, bf16[2,1024,3,128]{1,3,2,0:T(8,128)(2,1)} %bitcast.39), kind=kOutput, calls=%fused_computation.29 | convolution fusion | flops 1629488128 | bytes 28336128 | tf_op jit(solution)/shard_map/sub | solution.py:21
  29.8 11.8 %fusion.14 = bf16[2,1024,3,128]{3,1,2,0:T(8,128)(2,1)} fusion(bf16[2,1024,3,128]{1,3,2,0:T(8,128)(2,1)S(1)} %bitcast.37, f32[2,3,1024,1024]{2,3,1,0:T(8,128)} %get-tuple-element.6, f32[2,3,1024]{2,1,0:T(4,128)S(1)} %get-tuple-element.5), kind=kOutput, calls=%fused_computation.16 | convolution fusion | flops 1623982080 | bytes 28336128 | tf_op jit(solution)/shard_map/bhqk,bkhd->bqhd/dot_general | solution.py:23
  41.6 0.0 copy-start.4
  41.6 4.0 copy.31
  45.6 0.4 copy.40
  46.6 0.0 copy-done.4
  46.6 0.6 dynamic_slice.10
  47.2 30.9 %all-gather.5.cloned.1.call-done = bf16[128,64,384]{2,1,0:T(8,128)(2,1)} async-done(((bf16[4,64,384]{2,1,0:T(8,128)(2,1)}), bf16[128,64,384]{2,1,0:T(8,128)(2,1)}) %all-gather.5.cloned.1.call-update) | async-done | bytes 6291472 | tf_op jit(solution)/shard_map/all_gather | solution.py:44
  78.1 9.0 %fusion.8 = bf16[1,64,384]{2,0,1:T(2,128)(2,1)S(1)} fusion(bf16[128,64,384]{2,1,0:T(8,128)(2,1)} %all-gather.5.cloned.1.call-done, s32[]{:T(128)} %bitcast.5), kind=kOutput, calls=%fused_computation.8 | convolution fusion | flops 6291584 | bytes 6340612 | tf_op jit(solution)/shard_map/n,nij->ij/dot_general | solution.py:49
  87.1 32.8 %all_gather.11 = bf16[64,3072]{1,0:T(8,128)(2,1)S(1)} all-gather(bf16[64,384]{1,0:T(8,128)(2,1)S(1)} %bitcast.40), channel_id=1, replica_groups=mesh['rep'=32,'tp'=8] {'tp'}, dimensions={1}, use_global_device_ids=true | all-gather | bytes 442368 | tf_op jit(solution)/shard_map/all_gather | solution.py:54
  120.0 29.1 %all-gather.3.cloned.1.call-done = bf16[128,384,64]{1,2,0:T(8,128)(2,1)} async-done(((bf16[4,384,64]{1,2,0:T(8,128)(2,1)}), bf16[128,384,64]{1,2,0:T(8,128)(2,1)}) %all-gather.3.cloned.1.call-update) | async-done | bytes 6291472 | tf_op jit(solution)/shard_map/all_gather | solution.py:43
  149.0 9.0 %fusion.10 = bf16[1,384,64]{1,0,2:T(2,128)(2,1)S(1)} fusion(bf16[128,384,64]{1,2,0:T(8,128)(2,1)} %all-gather.3.cloned.1.call-done, s32[]{:T(128)} %bitcast.5), kind=kOutput, calls=%fused_computation.10 | convolution fusion | flops 6291584 | bytes 6340612 | tf_op jit(solution)/shard_map/n,nij->ij/dot_general | solution.py:48
  158.0 0.2 copy.37
  158.2 12.7 %fusion.12 = f32[2048,3072]{1,0:T(8,128)} fusion(bf16[2048,384]{0,1:T(8,128)(2,1)S(1)} %bitcast.34, bf16[384,3072]{1,0:T(8,128)(2,1)} %param.14, bf16[64,3072]{1,0:T(8,128)(2,1)S(1)} %all_gather.11, bf16[1,384,64]{2,1,0:T(8,128)(2,1)S(1)} %copy.37), kind=kOutput, calls=%fused_computation.14 | convolution fusion | flops 4986372096 | bytes 29540352 | tf_op jit(solution)/shard_map/dot_general | solution.py:59
  170.9 0.0 copy-start.5
  170.9 0.0 copy-start.3
  170.9 0.0 copy-start.2
  170.9 0.0 reduce-scatter.2.cloned.1.call-update
  171.0 0.6 copy-done.5
  171.6 0.6 dynamic_slice.11
  172.2 0.0 copy-done.3
  172.2 0.6 compare_convert_fusion
  172.8 486.1 %reduce-scatter.2.cloned.1.call-done = f32[2048,384]{1,0:T(8,128)} async-done(((f32[2048,3072]{1,0:T(8,128)}), f32[2048,384]{1,0:T(8,128)}) %reduce-scatter.2.cloned.1.call-update) | async-done | bytes 3145744 | tf_op jit(solution)/shard_map/reduce_scatter | solution.py:60
  659.0 0.0 copy-done.2
  659.0 3.7 add_convert_fusion.1
  (2 shorter events, 0.0 us)
Async XLA Ops:
  6.5 6.7 %copy-start = (bf16[2,1024,384]{2,1,0:T(8,128)(2,1)S(1)}, bf16[2,1024,384]{2,1,0:T(8,128)(2,1)}, u32[]{:S(2)}) copy-start(bf16[2,1024,384]{2,1,0:T(8,128)(2,1)} %param.12) | copy-start | bytes 4718596
  6.5 71.6 %all-gather.5.cloned.1.call-start = ((), (), s32[]{:S(2)}) async-start(), calls=%async_computation.2 | async-start | bytes 6488064 | tf_op jit(solution)/shard_map/all_gather | solution.py:44
  7.3 141.8 %all-gather.3.cloned.1.call-start = ((), (), s32[]{:S(2)}) async-start(), calls=%async_computation.1 | async-start | bytes 6488064 | tf_op jit(solution)/shard_map/all_gather | solution.py:43
  8.0 651.0 %reduce-scatter.2.cloned.1.call-start = ((), (), s32[]{:S(2)}) async-start(), calls=%async_computation.3 | async-start | bytes 28311552 | tf_op jit(solution)/shard_map/reduce_scatter | solution.py:60
  10.6 4.3 copy-start.1
  41.6 5.0 copy-start.4
  170.9 0.7 copy-start.5
  170.9 1.2 copy-start.3
  170.9 488.0 %copy-start.2 = (bf16[2,1024,384]{2,1,0:T(8,128)(2,1)S(1)}, bf16[2,1024,384]{2,1,0:T(8,128)(2,1)}, u32[]{:S(2)}) copy-start(bf16[2,1024,384]{2,1,0:T(8,128)(2,1)} %param.17) | copy-start | bytes 4718596
Sparse Core Ops, SparseCore 0:
  9.9 68.1 all-gather.4
  80.7 68.3 all-gather.2
  171.1 487.8 reduce-scatter.1
where the time goes:
time: 671 us; the launch traced here: 669 us
  waiting for transfers between devices  548 us (82%)
  matrix products  56.7 us (8%)
  blocking collectives  32.8 us (5%)
  between operations  15 us (2%)
  local copies, waits for them, and re-layouts  12.7 us (2%)
    reduce_scatter x1, waiting for transfers between devices, per_device(): lax.psum_scatter(partial_terms, 'tp', scatter_dimension=1, tiled=True)  486 us
    all_gather x1, blocking collectives, per_device(): complete_up_factor = lax.all_gather(up_cols, 'tp', axis=1, tiled=True)  32.8 us
    all_gather x1, waiting for transfers between devices, per_device(): lax.all_gather(adapter_up_pool, 'rep', axis=0, tiled=True)  30.9 us
    all_gather x1, waiting for transfers between devices, per_device(): lax.all_gather(adapter_down_pool, 'rep', axis=0, tiled=True)  29.1 us
    sub x1, matrix products, attend(): expos = jnp.exp(scores - highest)  14.2 us
  transfers between devices with their start and end apart: 3, of which 3 were waited for; matrix products, arithmetic and copies ran while one was open for 7% of the time, Pallas kernels for 0%

commit v1 on v0

v1 whole, which is shorter than its diff:
```python
import functools

import jax
import jax.numpy as jnp
from jax import lax
from jax.experimental import pallas as pl
from jax.experimental.pallas import tpu as pltpu
from jax.sharding import PartitionSpec as P

HD = 128
NY, NZ, NX, NC, NH = 4, 2, 4, 2, 4
LOG2E = 1.4426950408889634
VMEM = 60 * 1024 * 1024
TILE = 256
F32 = jnp.float32
BF16 = jnp.bfloat16


def table(move):
    pairs = []
    for h in range(NH):
        for x in range(NX):
            for c in range(NC):
                for y in range(NY):
                    for z in range(NZ):
                        here = ((h * NX + x) * NC + c) * NY * NZ + y * NZ + z
                        h2, x2, c2, y2, z2 = move(h, x, c, y, z)
                        h2, x2, c2, y2, z2 = h2 % NH, x2 % NX, c2 % NC, y2 % NY, z2 % NZ
                        there = ((h2 * NX + x2) * NC + c2) * NY * NZ + y2 * NZ + z2
                        pairs.append((here, there))
    return pairs


def send(array, move):
    return lax.ppermute(array, ("rep", "tp"), table(move))


def to_y(k):
    return lambda h, x, c, y, z: (h, x, c, y + k, z)


def to_x(k):
    return lambda h, x, c, y, z: (h, x + k, c, y, z)


def to_h(k):
    return lambda h, x, c, y, z: (h + k, x, c, y, z)


def swap_z(h, x, c, y, z):
    return (h, x, c, y, 1 - z)


def swap_core(h, x, c, y, z):
    return (h, x, 1 - c, y, z)


def other_z(h, x, c, y, z):
    return (h - 1 + 2 * z, x, c, y, 1 - z)


def params():
    return pltpu.CompilerParams(vmem_limit_bytes=VMEM)


def cost(flops, moved):
    return pl.CostEstimate(flops=flops, bytes_accessed=moved, transcendentals=0)


def attend_kernel(q_ref, k_ref, v_ref, out):
    rows = out.shape[0]
    k = k_ref[0]
    v = v_ref[0]
    v_one = jnp.concatenate([v, jnp.ones_like(v)], axis=1)
    factor = LOG2E * HD ** (-0.5)
    for begin in range(0, rows, TILE):
        part = slice(begin, begin + TILE)
        q = q_ref[0, part]
        s = lax.dot_general(q, k, (((1,), (1,)), ((), ())), preferred_element_type=F32)
        top = jnp.max(s, axis=1, keepdims=True)
        p = jnp.exp2((s - top) * factor).astype(BF16)
        o = jnp.dot(p, v_one, preferred_element_type=F32)
        out[part] = (o[:, :HD] / o[:, HD:]).astype(BF16)


def attend(queries, keys, values, chunk):
    b, first, rows = chunk
    seq, width = queries.shape[1:]
    whole = pl.BlockSpec((1, seq, HD), lambda h: (b, 0, h))
    return pl.pallas_call(
        attend_kernel,
        grid=(width // HD,),
        in_specs=[pl.BlockSpec((1, rows, HD), lambda h: (b, first // rows, h)), whole, whole],
        out_specs=pl.BlockSpec((rows, HD), lambda h: (0, h)),
        out_shape=jax.ShapeDtypeStruct((rows, width), BF16),
        compiler_params=params(),
        cost_estimate=cost(4 * rows * seq * width, 4 * (rows + seq) * width),
        name="attend",
    )(queries, keys, values)


def weight_specs(shift):
    def base(i, s):
        return (0, lax.rem(s[0] + shift, NY) * NZ + s[1])

    def swapped(i, s):
        return (0, lax.rem(s[0] + shift, NY))

    return base, swapped


def product(own, other, w_own, w_other):
    total = jnp.dot(own[...], w_own[...], preferred_element_type=F32)
    return total + jnp.dot(other[...], w_other[...], preferred_element_type=F32)


def far_kernel(marks, own, other, w_own, w_other, up_half, down_half):
    total = product(own, other, w_own, w_other).astype(BF16)
    half = up_half.shape[0]
    up_half[...] = total[:half]
    down_half[...] = total[half:]


def far(marks, own, other, weight, swapped):
    rows, width = own.shape
    base_map, swap_map = weight_specs(2)
    tile = pl.BlockSpec((rows, width), lambda i, s: (0, 0))
    half = pl.BlockSpec((rows // 2, width), lambda i, s: (0, 0))
    return pl.pallas_call(
        far_kernel,
        grid_spec=pltpu.PrefetchScalarGridSpec(
            num_scalar_prefetch=1,
            grid=(1,),
            in_specs=[
                tile,
                tile,
                pl.BlockSpec((width, width), base_map),
                pl.BlockSpec((width, width), swap_map),
            ],
            out_specs=[half, half],
        ),
        out_shape=[jax.ShapeDtypeStruct((rows // 2, width), BF16)] * 2,
        compiler_params=params(),
        cost_estimate=cost(4 * rows * width * width, 6 * rows * width),
        name="far",
    )(marks, own, other, weight, swapped)


def near_kernel(marks, own, other, w_own_r, w_other_r, w_own_l, w_other_l, got_r, got_l, out_r, out_l):
    half = got_r.shape[0]
    right = product(own, other, w_own_r, w_other_r)
    out_r[:half] = (right[:half] + got_r[...].astype(F32)).astype(BF16)
    out_r[half:] = right[half:].astype(BF16)
    left = product(own, other, w_own_l, w_other_l)
    out_l[:half] = left[:half].astype(BF16)
    out_l[half:] = (left[half:] + got_l[...].astype(F32)).astype(BF16)


def near(marks, own, other, weight, swapped, got_r, got_l):
    rows, width = own.shape
    tile = pl.BlockSpec((rows, width), lambda i, s: (0, 0))
    half = pl.BlockSpec((rows // 2, width), lambda i, s: (0, 0))
    specs = []
    for shift in (1, NY - 1):
        specs += [pl.BlockSpec((width, width), m) for m in weight_specs(shift)]
    return pl.pallas_call(
        near_kernel,
        grid_spec=pltpu.PrefetchScalarGridSpec(
            num_scalar_prefetch=1,
            grid=(1,),
            in_specs=[tile, tile] + specs + [half, half],
            out_specs=[tile, tile],
        ),
        out_shape=[jax.ShapeDtypeStruct((rows, width), BF16)] * 2,
        compiler_params=params(),
        cost_estimate=cost(8 * rows * width * width, 10 * rows * width),
        name="near",
    )(marks, own, other, weight, swapped, weight, swapped, got_r, got_l)


def lowrank_kernel(down_own, down_other, *refs):
    out = refs[-1]
    n = (len(refs) - 1) // 2
    dims = (((1,), (1,)), ((), ()))
    at = 0
    for own, other in zip(refs[:n], refs[n : 2 * n]):
        t = lax.dot_general(down_own[...], own[...], dims, preferred_element_type=F32)
        t = t + lax.dot_general(down_other[...], other[...], dims, preferred_element_type=F32)
        out[:, at : at + own.shape[0]] = t.astype(BF16)
        at += own.shape[0]


def lowrank(down_own, down_other, own, other):
    tokens = sum(a.shape[0] for a in own)
    width = own[0].shape[1]
    rank = down_own.shape[0]
    return pl.pallas_call(
        lowrank_kernel,
        out_shape=jax.ShapeDtypeStruct((rank, tokens), BF16),
        compiler_params=params(),
        cost_estimate=cost(4 * tokens * width * rank, 4 * tokens * width),
        name="lowrank",
    )(down_own, down_other, *own, *other)


def home_kernel(marks, own, other, w_own, w_other, got_r, got_l, t, up, residual, gate_ref, *rest):
    out = rest[-1]
    total = product(own, other, w_own, w_other)
    total = total + got_r[...].astype(F32) + got_l[...].astype(F32)
    dims = (((0,), (0,)), ((), ()))
    total = total + lax.dot_general(t[...], up[...], dims, preferred_element_type=F32)
    b = marks[3]
    live = (b < marks[2]).astype(F32)
    gate = gate_ref[...]
    g = jnp.where(b == 0, gate[0:1].astype(F32), gate[1:2].astype(F32)) * live
    out[0] = (residual[0].astype(F32) + g * total).astype(BF16)


def home(marks, chunk, own, other, weight, swapped, got_r, got_l, t, up, residual, gate, earlier):
    b, first, rows = chunk
    batch, seq, width = residual.shape
    base_map, swap_map = weight_specs(0)
    step = TILE
    tile = pl.BlockSpec((step, width), lambda i, s: (i, 0))
    place = pl.BlockSpec((1, step, width), lambda i, s: (b, first // step + i, 0))
    extra = [] if earlier is None else [earlier]
    return pl.pallas_call(
        home_kernel,
        grid_spec=pltpu.PrefetchScalarGridSpec(
            num_scalar_prefetch=1,
            grid=(rows // step,),
            in_specs=[
                tile,
                tile,
                pl.BlockSpec((width, width), base_map),
                pl.BlockSpec((width, width), swap_map),
                tile,
                tile,
                pl.BlockSpec((t.shape[0], step), lambda i, s: (0, (b * seq + first) // step + i)),
                pl.BlockSpec(up.shape, lambda i, s: (0, 0)),
                place,
                pl.BlockSpec((batch, width), lambda i, s: (0, 0)),
            ]
            + [pl.BlockSpec(memory_space=pl.ANY)] * len(extra),
            out_specs=place,
        ),
        out_shape=jax.ShapeDtypeStruct(residual.shape, BF16),
        input_output_aliases={11: 0} if extra else {},
        compiler_params=params(),
        cost_estimate=cost(4 * rows * width * width, 12 * rows * width),
        name="home",
    )(marks, own, other, weight, swapped, got_r, got_l, t, up, residual, gate, *extra)


def pick_adapter(down_pool, up_pool, wanted, rep, x, c, h):
    pool = jnp.stack([jnp.swapaxes(down_pool, 1, 2), up_pool], axis=1)
    slots = pool.shape[0]
    hits = wanted[:, None] == rep * slots + jnp.arange(slots, dtype=jnp.int32)
    hits = hits.reshape(NH, NX, NC, slots)

    def chosen(core):
        mask = lax.dynamic_index_in_dim(hits, core, 2, keepdims=False)
        total = None
        for n in range(slots):
            term = jnp.where(mask[:, :, n, None, None, None], pool[n], jnp.zeros((), BF16))
            total = term if total is None else total + term
        return total

    got = send(chosen(1 - c), swap_core)
    held = chosen(c) + got
    parts = [
        send(lax.dynamic_index_in_dim(held, lax.rem(x + d, NX), 1, keepdims=False), to_x(d))
        for d in range(1, NX)
    ]
    held = lax.dynamic_index_in_dim(held, x, 1, keepdims=False) + parts[0] + parts[1] + parts[2]
    parts = [
        send(lax.dynamic_index_in_dim(held, lax.rem(h + d, NH), 0, keepdims=False), to_h(d))
        for d in range(1, NH)
    ]
    own = lax.dynamic_index_in_dim(held, h, 0, keepdims=False) + parts[0] + parts[1] + parts[2]
    return own[0], own[1]


def per_device(
    queries,
    keys,
    values,
    output_weight,
    adapter_down_pool,
    adapter_up_pool,
    residual,
    gate,
    adapter_id,
    adapter_slot,
    request_count,
):
    rep = lax.axis_index("rep")
    tp = lax.axis_index("tp")
    c = lax.rem(rep, NC)
    x = lax.rem(lax.div(rep, NC), NX)
    h = lax.div(rep, NC * NX)
    y = lax.div(tp, NZ)
    z = lax.rem(tp, NZ)
    batch, seq, width = residual.shape

    pieces = [
        lax.dynamic_slice_in_dim(output_weight, (k * NZ + 1 - z) * width, width, 1) for k in range(NY)
    ]
    swapped = send(jnp.concatenate(pieces, axis=1), other_z)

    chunks = [(b, 0, seq) for b in range(batch)]
    own = [attend(queries, keys, values, chunk) for chunk in chunks]
    other = [send(a, swap_z) for a in own]

    wanted = adapter_slot[adapter_id]
    down, up = pick_adapter(adapter_down_pool, adapter_up_pool, wanted, rep, x, c, h)
    t = lowrank(down, send(down, swap_z), own, other)
    t = jnp.concatenate([t] + [send(t, to_y(k)) for k in range(1, NY)], axis=0)
    up = jnp.concatenate([up] * NY, axis=0)

    count = request_count[rep]
    result = None
    for chunk, mine, theirs in zip(chunks, own, other):
        marks = jnp.stack([y, z, count, jnp.int32(chunk[0])])
        up_half, down_half = far(marks, mine, theirs, output_weight, swapped)
        got_r = send(up_half, to_y(1))
        got_l = send(down_half, to_y(-1))
        right, left = near(marks, mine, theirs, output_weight, swapped, got_r, got_l)
        got_r = send(right, to_y(1))
        got_l = send(left, to_y(-1))
        result = home(
            marks, chunk, mine, theirs, output_weight, swapped, got_r, got_l, t, up, residual, gate, result
        )
    return result


def solution(mesh):
    placed = (
        P("rep", None, "tp"),
        P("rep", None, "tp"),
        P("rep", None, "tp"),
        P("tp", None),
        P("rep", "tp", None),
        P("rep", None, "tp"),
        P("rep", None, "tp"),
        P("rep", "tp"),
        P(),
        P(),
        P(),
    )
    return jax.shard_map(
        per_device, mesh=mesh, in_specs=placed, out_specs=P("rep", None, "tp"), check_vma=False
    )
```

time: 671 us -> 153 us (0.23)
  waiting for transfers between devices: 548 us -> 39.2 us
  matrix products: 56.7 us -> 0 us
  Pallas kernels: 0 us -> 49 us
  starting transfers between devices: 0.08 us -> 38 us
  blocking collectives: 32.8 us -> 0 us
  between operations: 15 us -> 0.26 us
  other arithmetic: 4.34 us -> 11.9 us
    reduce_scatter x1 -> x0, waiting for transfers between devices: 486 us -> none  [per_device(): lax.psum_scatter(partial_terms, 'tp', scatter_dimension=1, tiled=True)]
    all_gather x2 -> x0, waiting for transfers between devices: 59.9 us -> none  [the longest x1 30.9 us: per_device(): lax.all_gather(adapter_up_pool, 'rep', axis=0, tiled=True)]
    pallas_call x0 -> x9, Pallas kernels: none -> 49 us  [the longest x2 13.8 us: attend(): pl.pallas_call(attend_kernel, grid=(width // HD,), in_specs=[pl.BlockSpec...]
    dot_general x4 -> x0, matrix products: 42.5 us -> none  [the longest x1 12.7 us: per_device(): jnp.dot(attended, merged_rows, preferred_element_type=jnp.float32)]
    ppermute x0 -> x22, waiting for transfers between devices: none -> 39.2 us  [send(): return lax.ppermute(array, ('rep', 'tp'), table(move))]
    ppermute x0 -> x22, starting transfers between devices: none -> 38 us  [send(): return lax.ppermute(array, ('rep', 'tp'), table(move))]
    all_gather x1 -> x0, blocking collectives: 32.8 us -> none  [per_device(): complete_up_factor = lax.all_gather(up_cols, 'tp', axis=1, tiled=True)]
    sub x1 -> x0, matrix products: 14.2 us -> none  [attend(): expos = jnp.exp(scores - highest)]
  transfers between devices with their start and end apart: 3 -> 22, of which waited for: 3 -> 5; matrix products, arithmetic and copies ran while one was open for 7% -> 7% of each run, Pallas kernels for 0% -> 29%
where the time goes in v1:
time: 153 us; the launch traced here: 150 us
  Pallas kernels  49 us (32%)
  waiting for transfers between devices  39.2 us (26%)
  starting transfers between devices  38 us (25%)
  other arithmetic  11.9 us (8%)
  local copies, waits for them, and re-layouts  11.8 us (8%)
    ppermute x22, waiting for transfers between devices, send(): return lax.ppermute(array, ('rep', 'tp'), table(move))  39.2 us
    ppermute x22, starting transfers between devices, send(): return lax.ppermute(array, ('rep', 'tp'), table(move))  38 us
    pallas_call x2, Pallas kernels, attend(): pl.pallas_call(attend_kernel, grid=(width // HD,), in_specs=[pl.BlockSpec...  13.8 us
    pallas_call x2, Pallas kernels, home(): pl.pallas_call(home_kernel, grid_spec=pltpu.PrefetchScalarGridSpec(num_sc...  12 us
    pallas_call x2, Pallas kernels, near(): pl.pallas_call(near_kernel, grid_spec=pltpu.PrefetchScalarGridSpec(num_sc...  11.3 us
    unnamed x36, local copies, waits for them, and re-layouts  8.78 us
    pallas_call x2, Pallas kernels, far(): pl.pallas_call(far_kernel, grid_spec=pltpu.PrefetchScalarGridSpec(num_sca...  8.28 us
    pallas_call x1, Pallas kernels, lowrank(): pl.pallas_call(lowrank_kernel, out_shape=jax.ShapeDtypeStruct((rank, toke...  3.7 us
  transfers between devices with their start and end apart: 22, of which 5 were waited for; matrix products, arithmetic and copies ran while one was open for 7% of the time, Pallas kernels for 29%

profile of v1, /device:TPU:32, one launch (start us, length us, event | category | flops | bytes accessed | tf_op | source)
XLA Modules:
  0.0 150.2 jit_solution(17113785880394886215)
XLA Ops:
  0.0 0.7 compare_select_fusion
  0.7 0.7 gather_fusion
  1.5 0.1 copy.22
  1.8 0.1 copy.35
  1.9 0.1 copy.36
  2.1 0.1 copy.37
  2.2 0.1 copy.38
  2.3 1.0 fusion.5
  3.3 1.7 %select_add_fusion = bf16[4,4,2,64,384]{4,3,2,0,1:T(8,128)(2,1)} fusion(pred[4,4]{0,1:T(4,128)(4,1)S(1)} %bitcast.63, pred[4,4]{0,1:T(4,128)(4,1)S(1)} %bitcast.62, pred[4,4]{0,1:T(4,128)(4,1)S(1)} %bitcast.61, pred[4,4]{0,1:T(4,128)(4,1)S(1)} %bitcast.60, bf16[2,64,384]{2,1,0:T(8,128)(2,1)S(1)} %get-tuple-element.35, ...), kind=kLoop, calls=%fused_computation.1 | loop fusion | flops 5505024 | bytes 1966144 | tf_op jit(solution)/shard_map/add | solution.py:266
  5.1 0.2 constant_dynamic-slice_fusion.3
  5.3 1.1 pad_maximum_fusion
  6.4 1.9 %collective-permute-start.1 = (bf16[384,1536]{1,0:T(8,128)(2,1)}, bf16[384,1536]{1,0:T(8,128)(2,1)S(1)}, u32[]{:S(2)}, u32[]{:S(2)}) collective-permute-start(bf16[384,1536]{1,0:T(8,128)(2,1)} %pad_maximum_fusion), channel_id=1, source_target_pairs={{0,193},{1,64},{2,195},{3,66},{4,197},{5,68},{6,199},{7,70},{8,201... | collective-permute-start | bytes 3538952 | tf_op jit(solution)/shard_map/ppermute | solution.py:35
  8.3 0.1 copy.33
  8.4 0.1 copy.34
  8.6 0.1 copy.31
  8.7 0.1 copy.32
  8.8 2.0 %add_add_fusion = bf16[4,4,2,64,384]{4,3,2,0,1:T(8,128)(2,1)S(1)} fusion(bf16[4,4,2,64,384]{4,3,2,0,1:T(8,128)(2,1)} %collective-permute-done.6, pred[4,4]{0,1:T(4,128)(4,1)S(1)} %bitcast.57, pred[4,4]{0,1:T(4,128)(4,1)S(1)} %bitcast.56, pred[4,4]{0,1:T(4,128)(4,1)S(1)} %bitcast.59, pred[4,4]{0,1:T(4,128)(4,1)S(1)} %bitcast.58, ...), kind=kLoop, calls=%fused_computation.2 | loop fusion | flops 6291456 | bytes 3539008 | tf_op jit(solution)/shard_map/add | solution.py:270
  10.9 1.1 copy-done.5
  12.0 0.1 dynamic-slice_bitcast_fusion.2
  12.2 1.6 %collective-permute-start.7 = (bf16[4,2,64,384]{3,2,1,0:T(8,128)(2,1)S(1)}, bf16[4,2,64,384]{3,2,1,0:T(8,128)(2,1)}, u32[]{:S(2)}, u32[]{:S(2)}) collective-permute-start(bf16[4,2,64,384]{3,2,1,0:T(8,128)(2,1)S(1)} %get-tuple-element.27), channel_id=1, source_target_pairs={{0,16},{1,17},{2,18},{3,19},{4,20},{5,21},{6,22},{7,23},{8,24},{9,... | collective-permute-start | bytes 1179656 | tf_op jit(solution)/shard_map/ppermute | solution.py:35
  13.7 6.9 %attend.3.refs_0_.own = bf16[1024,384]{1,0:T(8,128)(2,1)} custom-call(bf16[2,1024,384]{2,1,0:T(8,128)(2,1)} %q_ref.3, bf16[2,1024,384]{2,1,0:T(8,128)(2,1)} %k_ref.3, bf16[2,1024,384]{2,1,0:T(8,128)(2,1)} %v_ref.3), custom_call_target="tpu_custom_call" | custom-call | flops 1610612736 | bytes 3145728 | tf_op jit(solution)/shard_map/attend/pallas_call | solution.py:90
  20.6 4.0 %collective-permute-start.14 = (bf16[1024,384]{1,0:T(8,128)(2,1)}, bf16[1024,384]{1,0:T(8,128)(2,1)S(1)}, u32[]{:S(2)}, u32[]{:S(2)}) collective-permute-start(bf16[1024,384]{1,0:T(8,128)(2,1)} %attend.3.refs_0_.own), channel_id=1, source_target_pairs={{0,1},{1,0},{2,3},{3,2},{4,5},{5,4},{6,7},{7,6},{8,9},{9,8},{10,11... | collective-permute-start | bytes 2359304 | tf_op jit(solution)/shard_map/ppermute | solution.py:35
  24.7 2.7 %collective-permute-start.8 = (bf16[4,2,64,384]{3,2,1,0:T(8,128)(2,1)S(1)}, bf16[4,2,64,384]{3,2,1,0:T(8,128)(2,1)}, u32[]{:S(2)}, u32[]{:S(2)}) collective-permute-start(bf16[4,2,64,384]{3,2,1,0:T(8,128)(2,1)S(1)} %get-tuple-element.29), channel_id=1, source_target_pairs={{0,32},{1,33},{2,34},{3,35},{4,36},{5,37},{6,38},{7,39},{8,40},{9,... | collective-permute-start | bytes 1179656 | tf_op jit(solution)/shard_map/ppermute | solution.py:35
  27.4 1.4 collective-permute-start.9
  28.8 6.9 %attend.2.own.refs_1_ = bf16[1024,384]{1,0:T(8,128)(2,1)} custom-call(bf16[2,1024,384]{2,1,0:T(8,128)(2,1)} %q_ref.3, bf16[2,1024,384]{2,1,0:T(8,128)(2,1)} %k_ref.3, bf16[2,1024,384]{2,1,0:T(8,128)(2,1)} %v_ref.3), custom_call_target="tpu_custom_call" | custom-call | flops 1610612736 | bytes 3145728 | tf_op jit(solution)/shard_map/attend/pallas_call | solution.py:90
  35.8 0.6 dynamic_slice.48
  36.4 1.3 pad_add_fusion.2
  37.7 0.7 pad_add_fusion.marks
  38.4 6.1 %collective-permute-done.9 = bf16[4,2,64,384]{3,2,1,0:T(8,128)(2,1)} collective-permute-done((bf16[4,2,64,384]{3,2,1,0:T(8,128)(2,1)S(1)}, bf16[4,2,64,384]{3,2,1,0:T(8,128)(2,1)}, u32[]{:S(2)}, u32[]{:S(2)}) %collective-permute-start.9) | collective-permute-done | bytes 393248 | tf_op jit(solution)/shard_map/ppermute | solution.py:35
  44.5 1.4 fusion.1
  46.0 0.8 collective-permute-start.10
  46.8 3.9 %collective-permute-start.11 = (bf16[2,64,384]{2,1,0:T(8,128)(2,1)S(1)}, bf16[2,64,384]{2,1,0:T(8,128)(2,1)S(1)}, u32[]{:S(2)}, u32[]{:S(2)}) collective-permute-start(bf16[2,64,384]{2,1,0:T(8,128)(2,1)S(1)} %get-tuple-element.32), channel_id=1, source_target_pairs={{0,128},{1,129},{2,130},{3,131},{4,132},{5,133},{6,134},{7,135},{8... | collective-permute-start | bytes 294920 | tf_op jit(solution)/shard_map/ppermute | solution.py:35
  50.7 2.7 %collective-permute-start.12 = (bf16[2,64,384]{2,1,0:T(8,128)(2,1)S(1)}, bf16[2,64,384]{2,1,0:T(8,128)(2,1)S(1)}, u32[]{:S(2)}, u32[]{:S(2)}) collective-permute-start(bf16[2,64,384]{2,1,0:T(8,128)(2,1)S(1)} %get-tuple-element.31), channel_id=1, source_target_pairs={{0,192},{1,193},{2,194},{3,195},{4,196},{5,197},{6,198},{7,199},{8... | collective-permute-start | bytes 294920 | tf_op jit(solution)/shard_map/ppermute | solution.py:35
  53.4 1.0 copy-done.2
  54.4 4.1 %far.3 = (bf16[512,384]{1,0:T(8,128)(2,1)}, bf16[512,384]{1,0:T(8,128)(2,1)}) custom-call(s32[4]{0:T(128)} %get-tuple-element.21.marks, bf16[1024,384]{1,0:T(8,128)(2,1)} %attend.3.refs_0_.own, bf16[1024,384]{1,0:T(8,128)(2,1)} %copy-done.3, bf16[384,3072]{1,0:T(8,128)(2,1)} %w_own.7, bf16[384,1536]{1,0:T(8,128)(2,1)} %copy-done.2), custom_call_target="tpu_custom_call" | custom-call | flops 603979776 | bytes 2359296 | tf_op jit(solution)/shard_map/far/pallas_call | solution.py:129
  58.5 1.6 %collective-permute-start.18 = (bf16[512,384]{1,0:T(8,128)(2,1)}, bf16[512,384]{1,0:T(8,128)(2,1)S(1)}, u32[]{:S(2)}, u32[]{:S(2)}) collective-permute-start(bf16[512,384]{1,0:T(8,128)(2,1)} %get-tuple-element.17), channel_id=1, source_target_pairs={{0,2},{1,3},{2,4},{3,5},{4,6},{5,7},{6,0},{7,1},{8,10},{9,11},{10,... | collective-permute-start | bytes 1179656 | tf_op jit(solution)/shard_map/ppermute | solution.py:35
  60.1 3.2 %collective-permute-done.other.refs_3_ = bf16[1024,384]{1,0:T(8,128)(2,1)S(1)} collective-permute-done((bf16[1024,384]{1,0:T(8,128)(2,1)}, bf16[1024,384]{1,0:T(8,128)(2,1)S(1)}, u32[]{:S(2)}, u32[]{:S(2)}) %collective-permute-start) | collective-permute-done | bytes 786464 | tf_op jit(solution)/shard_map/ppermute | solution.py:35
  63.3 3.0 %collective-permute-start.19 = (bf16[512,384]{1,0:T(8,128)(2,1)}, bf16[512,384]{1,0:T(8,128)(2,1)S(1)}, u32[]{:S(2)}, u32[]{:S(2)}) collective-permute-start(bf16[512,384]{1,0:T(8,128)(2,1)} %get-tuple-element.18), channel_id=1, source_target_pairs={{0,6},{1,7},{2,0},{3,1},{4,2},{5,3},{6,4},{7,5},{8,14},{9,15},{10,... | collective-permute-start | bytes 1179656 | tf_op jit(solution)/shard_map/ppermute | solution.py:35
  66.3 4.1 %far.2 = (bf16[512,384]{1,0:T(8,128)(2,1)}, bf16[512,384]{1,0:T(8,128)(2,1)}) custom-call(s32[4]{0:T(128)} %pad_add_fusion.marks, bf16[1024,384]{1,0:T(8,128)(2,1)} %attend.2.own.refs_1_, bf16[1024,384]{1,0:T(8,128)(2,1)} %copy-done.4, bf16[384,3072]{1,0:T(8,128)(2,1)} %w_own.7, bf16[384,1536]{1,0:T(8,128)(2,1)} %copy-done.2), custom_call_target="tpu_custom_call" | custom-call | flops 603979776 | bytes 2359296 | tf_op jit(solution)/shard_map/far/pallas_call | solution.py:129
  70.5 3.2 %collective-permute-start.3 = (bf16[512,384]{1,0:T(8,128)(2,1)}, bf16[512,384]{1,0:T(8,128)(2,1)S(1)}, u32[]{:S(2)}, u32[]{:S(2)}) collective-permute-start(bf16[512,384]{1,0:T(8,128)(2,1)} %get-tuple-element.14), channel_id=1, source_target_pairs={{0,6},{1,7},{2,0},{3,1},{4,2},{5,3},{6,4},{7,5},{8,14},{9,15},{10,... | collective-permute-start | bytes 1179656 | tf_op jit(solution)/shard_map/ppermute | solution.py:35
  73.8 2.8 %collective-permute-start.13 = (bf16[64,384]{1,0:T(8,128)(2,1)S(1)}, bf16[64,384]{1,0:T(8,128)(2,1)S(1)}, u32[]{:S(2)}, u32[]{:S(2)}) collective-permute-start(bf16[64,384]{1,0:T(8,128)(2,1)S(1)} %get-tuple-element.38.down_own), channel_id=1, source_target_pairs={{0,1},{1,0},{2,3},{3,2},{4,5},{5,4},{6,7},{7,6},{8,9},{9,8},{10,11... | collective-permute-start | bytes 147464 | tf_op jit(solution)/shard_map/ppermute | solution.py:35
  76.5 2.1 %collective-permute-done.13.down_other = bf16[64,384]{1,0:T(8,128)(2,1)S(1)} collective-permute-done((bf16[64,384]{1,0:T(8,128)(2,1)S(1)}, bf16[64,384]{1,0:T(8,128)(2,1)S(1)}, u32[]{:S(2)}, u32[]{:S(2)}) %collective-permute-start.13) | collective-permute-done | bytes 49184 | tf_op jit(solution)/shard_map/ppermute | solution.py:35
  78.6 0.6 copy-done.16
  79.2 3.7 %lowrank.1 = bf16[64,2048]{1,0:T(8,128)(2,1)} custom-call(bf16[64,384]{1,0:T(8,128)(2,1)} %copy-done.15, bf16[64,384]{1,0:T(8,128)(2,1)} %copy-done.16, bf16[1024,384]{1,0:T(8,128)(2,1)} %attend.3.refs_0_.own, bf16[1024,384]{1,0:T(8,128)(2,1)} %attend.2.own.refs_1_, bf16[1024,384]{1,0:T(8,128)(2,1)} %copy-done.3, bf16[1024,384]{1,0:T(8,128)(2,1)} %copy-done.4), custom_call_target="tpu_custom_call" | custom-call | flops 201326592 | bytes 3145728 | tf_op jit(solution)/shard_map/lowrank/pallas_call | solution.py:197
  83.0 0.7 copy-done.12
  83.7 0.8 copy-done.14
  84.5 5.7 %near.3 = (bf16[1024,384]{1,0:T(8,128)(2,1)}, bf16[1024,384]{1,0:T(8,128)(2,1)}) custom-call(s32[4]{0:T(128)} %get-tuple-element.21.marks, bf16[1024,384]{1,0:T(8,128)(2,1)} %attend.3.refs_0_.own, bf16[1024,384]{1,0:T(8,128)(2,1)} %copy-done.3, bf16[384,3072]{1,0:T(8,128)(2,1)} %w_own.7, bf16[384,1536]{1,0:T(8,128)(2,1)} %copy-done.2, ...), custom_call_target="tpu_custom_call" | custom-call | flops 1207959552 | bytes 3932160 | tf_op jit(solution)/shard_map/near/pallas_call | solution.py:166
  90.1 3.2 %collective-permute-start.21 = (bf16[1024,384]{1,0:T(8,128)(2,1)}, bf16[1024,384]{1,0:T(8,128)(2,1)S(1)}, u32[]{:S(2)}, u32[]{:S(2)}) collective-permute-start(bf16[1024,384]{1,0:T(8,128)(2,1)} %get-tuple-element.20), channel_id=1, source_target_pairs={{0,6},{1,7},{2,0},{3,1},{4,2},{5,3},{6,4},{7,5},{8,14},{9,15},{10,... | collective-permute-start | bytes 2359304 | tf_op jit(solution)/shard_map/ppermute | solution.py:35
  93.4 1.8 %collective-permute-start.16 = (bf16[64,2048]{1,0:T(8,128)(2,1)S(1)}, bf16[64,2048]{1,0:T(8,128)(2,1)S(1)}, u32[]{:S(2)}, u32[]{:S(2)}) collective-permute-start(bf16[64,2048]{1,0:T(8,128)(2,1)S(1)} %copy-done.6), channel_id=1, source_target_pairs={{0,4},{1,5},{2,6},{3,7},{4,0},{5,1},{6,2},{7,3},{8,12},{9,13},{10,... | collective-permute-start | bytes 786440 | tf_op jit(solution)/shard_map/ppermute | solution.py:35
  95.2 0.8 copy-done.13
  95.9 5.6 %near.2 = (bf16[1024,384]{1,0:T(8,128)(2,1)}, bf16[1024,384]{1,0:T(8,128)(2,1)}) custom-call(s32[4]{0:T(128)} %pad_add_fusion.marks, bf16[1024,384]{1,0:T(8,128)(2,1)} %attend.2.own.refs_1_, bf16[1024,384]{1,0:T(8,128)(2,1)} %copy-done.4, bf16[384,3072]{1,0:T(8,128)(2,1)} %w_own.7, bf16[384,1536]{1,0:T(8,128)(2,1)} %copy-done.2, bf16[384,3072]{1,0:T(8,128)(2,1)} %w_own.7, ...), custom_call_target="tpu_custom_call" | custom-call | flops 1207959552 | bytes 3932160 | tf_op jit(solution)/shard_map/near/pallas_call | solution.py:166
  101.5 1.4 collective-permute-start.4
  102.9 1.8 %collective-permute-start.5 = (bf16[1024,384]{1,0:T(8,128)(2,1)}, bf16[1024,384]{1,0:T(8,128)(2,1)S(1)}, u32[]{:S(2)}, u32[]{:S(2)}) collective-permute-start(bf16[1024,384]{1,0:T(8,128)(2,1)} %get-tuple-element.16), channel_id=1, source_target_pairs={{0,6},{1,7},{2,0},{3,1},{4,2},{5,3},{6,4},{7,5},{8,14},{9,15},{10,... | collective-permute-start | bytes 2359304 | tf_op jit(solution)/shard_map/ppermute | solution.py:35
  104.8 14.3 %collective-permute-done.16 = bf16[64,2048]{1,0:T(8,128)(2,1)S(1)} collective-permute-done((bf16[64,2048]{1,0:T(8,128)(2,1)S(1)}, bf16[64,2048]{1,0:T(8,128)(2,1)S(1)}, u32[]{:S(2)}, u32[]{:S(2)}) %collective-permute-start.16) | collective-permute-done | bytes 262176 | tf_op jit(solution)/shard_map/ppermute | solution.py:35
  119.1 0.1 collective-permute-start.17
  119.2 0.7 pad_maximum_fusion.2.up
  119.9 13.5 %collective-permute-done.17 = bf16[64,2048]{1,0:T(8,128)(2,1)S(1)} collective-permute-done((bf16[64,2048]{1,0:T(8,128)(2,1)S(1)}, bf16[64,2048]{1,0:T(8,128)(2,1)S(1)}, u32[]{:S(2)}, u32[]{:S(2)}) %collective-permute-start.17) | collective-permute-done | bytes 262176 | tf_op jit(solution)/shard_map/ppermute | solution.py:35
  133.4 1.1 pad_maximum_fusion.1.t
  134.5 1.0 copy-done.7
  135.4 1.0 copy-done.8
  136.4 6.0 %home.2.rest_0_ = bf16[2,1024,384]{2,1,0:T(8,128)(2,1)} custom-call(s32[4]{0:T(128)} %get-tuple-element.21.marks, bf16[1024,384]{1,0:T(8,128)(2,1)} %attend.3.refs_0_.own, bf16[1024,384]{1,0:T(8,128)(2,1)} %copy-done.3, bf16[384,3072]{1,0:T(8,128)(2,1)} %w_own.7, bf16[384,1536]{1,0:T(8,128)(2,1)} %copy-done.2, bf16[1024,384]{1,0:T(8,128)(2,1)} %copy-done.7, ...), custom_call_target="tpu_custom_call" | custom-call | flops 603979776 | bytes 4718592 | tf_op jit(solution)/shard_map/home/pallas_call | solution.py:227
  142.4 0.9 copy-done.9
  143.3 0.9 copy-done.10
  144.2 6.0 %home.3 = bf16[2,1024,384]{2,1,0:T(8,128)(2,1)} custom-call(s32[4]{0:T(128)} %pad_add_fusion.marks, bf16[1024,384]{1,0:T(8,128)(2,1)} %attend.2.own.refs_1_, bf16[1024,384]{1,0:T(8,128)(2,1)} %copy-done.4, bf16[384,3072]{1,0:T(8,128)(2,1)} %w_own.7, bf16[384,1536]{1,0:T(8,128)(2,1)} %copy-done.2, ...), custom_call_target="tpu_custom_call", output_to_operand_aliasing={{}: (11, {})} | custom-call | flops 603979776 | bytes 4718592 | tf_op jit(solution)/shard_map/home/pallas_call | solution.py:227
  (57 shorter events, 0.5 us)
Async XLA Ops:
  0.0 0.7 copy-start
  1.4 3.7 %copy-start.1 = (bf16[384,3072]{1,0:T(8,128)(2,1)S(1)}, bf16[384,3072]{1,0:T(8,128)(2,1)}, u32[]{:S(2)}) copy-start(bf16[384,3072]{1,0:T(8,128)(2,1)} %w_own.7) | copy-start | bytes 7077892
  5.1 3.8 %collective-permute-start.6 = (bf16[4,4,2,64,384]{4,3,2,0,1:T(8,128)(2,1)}, bf16[4,4,2,64,384]{4,3,2,0,1:T(8,128)(2,1)}, u32[]{:S(2)}, u32[]{:S(2)}) collective-permute-start(bf16[4,4,2,64,384]{4,3,2,0,1:T(8,128)(2,1)} %select_add_fusion), channel_id=1, source_target_pairs={{0,8},{1,9},{2,10},{3,11},{4,12},{5,13},{6,14},{7,15},{8,0},{9,1},... | collective-permute-start | bytes 4718600 | tf_op jit(solution)/shard_map/ppermute | solution.py:35
  6.4 47.0 %collective-permute-start.1 = (bf16[384,1536]{1,0:T(8,128)(2,1)}, bf16[384,1536]{1,0:T(8,128)(2,1)S(1)}, u32[]{:S(2)}, u32[]{:S(2)}) collective-permute-start(bf16[384,1536]{1,0:T(8,128)(2,1)} %pad_maximum_fusion), channel_id=1, source_target_pairs={{0,193},{1,64},{2,195},{3,66},{4,197},{5,68},{6,199},{7,70},{8,201... | collective-permute-start | bytes 3538952 | tf_op jit(solution)/shard_map/ppermute | solution.py:35
  10.9 1.1 copy-start.5
  12.2 23.6 %collective-permute-start.7 = (bf16[4,2,64,384]{3,2,1,0:T(8,128)(2,1)S(1)}, bf16[4,2,64,384]{3,2,1,0:T(8,128)(2,1)}, u32[]{:S(2)}, u32[]{:S(2)}) collective-permute-start(bf16[4,2,64,384]{3,2,1,0:T(8,128)(2,1)S(1)} %get-tuple-element.27), channel_id=1, source_target_pairs={{0,16},{1,17},{2,18},{3,19},{4,20},{5,21},{6,22},{7,23},{8,24},{9,... | collective-permute-start | bytes 1179656 | tf_op jit(solution)/shard_map/ppermute | solution.py:35
  20.6 30.1 %collective-permute-start.14 = (bf16[1024,384]{1,0:T(8,128)(2,1)}, bf16[1024,384]{1,0:T(8,128)(2,1)S(1)}, u32[]{:S(2)}, u32[]{:S(2)}) collective-permute-start(bf16[1024,384]{1,0:T(8,128)(2,1)} %attend.3.refs_0_.own), channel_id=1, source_target_pairs={{0,1},{1,0},{2,3},{3,2},{4,5},{5,4},{6,7},{7,6},{8,9},{9,8},{10,11... | collective-permute-start | bytes 2359304 | tf_op jit(solution)/shard_map/ppermute | solution.py:35
  24.7 13.7 %collective-permute-start.8 = (bf16[4,2,64,384]{3,2,1,0:T(8,128)(2,1)S(1)}, bf16[4,2,64,384]{3,2,1,0:T(8,128)(2,1)}, u32[]{:S(2)}, u32[]{:S(2)}) collective-permute-start(bf16[4,2,64,384]{3,2,1,0:T(8,128)(2,1)S(1)} %get-tuple-element.29), channel_id=1, source_target_pairs={{0,32},{1,33},{2,34},{3,35},{4,36},{5,37},{6,38},{7,39},{8,40},{9,... | collective-permute-start | bytes 1179656 | tf_op jit(solution)/shard_map/ppermute | solution.py:35
  27.4 8.4 %copy-start.17 = (s32[32]{0:T(128)S(1)}, s32[32]{0:T(128)}, u32[]{:S(2)}) copy-start(s32[32]{0:T(128)} %param.21) | copy-start | bytes 388
  27.4 17.1 %collective-permute-start.9 = (bf16[4,2,64,384]{3,2,1,0:T(8,128)(2,1)S(1)}, bf16[4,2,64,384]{3,2,1,0:T(8,128)(2,1)}, u32[]{:S(2)}, u32[]{:S(2)}) collective-permute-start(bf16[4,2,64,384]{3,2,1,0:T(8,128)(2,1)S(1)} %get-tuple-element.28), channel_id=1, source_target_pairs={{0,48},{1,49},{2,50},{3,51},{4,52},{5,53},{6,54},{7,55},{8,56},{9,... | collective-permute-start | bytes 1179656 | tf_op jit(solution)/shard_map/ppermute | solution.py:35
  35.8 27.5 %collective-permute-start = (bf16[1024,384]{1,0:T(8,128)(2,1)}, bf16[1024,384]{1,0:T(8,128)(2,1)S(1)}, u32[]{:S(2)}, u32[]{:S(2)}) collective-permute-start(bf16[1024,384]{1,0:T(8,128)(2,1)} %attend.2.own.refs_1_), channel_id=1, source_target_pairs={{0,1},{1,0},{2,3},{3,2},{4,5},{5,4},{6,7},{7,6},{8,9},{9,8},{10,11... | collective-permute-start | bytes 2359304 | tf_op jit(solution)/shard_map/ppermute | solution.py:35
  46.0 24.5 %collective-permute-start.10 = (bf16[2,64,384]{2,1,0:T(8,128)(2,1)S(1)}, bf16[2,64,384]{2,1,0:T(8,128)(2,1)S(1)}, u32[]{:S(2)}, u32[]{:S(2)}) collective-permute-start(bf16[2,64,384]{2,1,0:T(8,128)(2,1)S(1)} %get-tuple-element.30), channel_id=1, source_target_pairs={{0,64},{1,65},{2,66},{3,67},{4,68},{5,69},{6,70},{7,71},{8,72},{9,... | collective-permute-start | bytes 294920 | tf_op jit(solution)/shard_map/ppermute | solution.py:35
  46.8 23.7 %collective-permute-start.11 = (bf16[2,64,384]{2,1,0:T(8,128)(2,1)S(1)}, bf16[2,64,384]{2,1,0:T(8,128)(2,1)S(1)}, u32[]{:S(2)}, u32[]{:S(2)}) collective-permute-start(bf16[2,64,384]{2,1,0:T(8,128)(2,1)S(1)} %get-tuple-element.32), channel_id=1, source_target_pairs={{0,128},{1,129},{2,130},{3,131},{4,132},{5,133},{6,134},{7,135},{8... | collective-permute-start | bytes 294920 | tf_op jit(solution)/shard_map/ppermute | solution.py:35
  50.7 2.7 %copy-start.3 = (bf16[1024,384]{1,0:T(8,128)(2,1)}, bf16[1024,384]{1,0:T(8,128)(2,1)S(1)}, u32[]{:S(2)}) copy-start(bf16[1024,384]{1,0:T(8,128)(2,1)S(1)} %collective-permute-done.14.refs_2_.other) | copy-start | bytes 2359300
  50.7 23.0 %collective-permute-start.12 = (bf16[2,64,384]{2,1,0:T(8,128)(2,1)S(1)}, bf16[2,64,384]{2,1,0:T(8,128)(2,1)S(1)}, u32[]{:S(2)}, u32[]{:S(2)}) collective-permute-start(bf16[2,64,384]{2,1,0:T(8,128)(2,1)S(1)} %get-tuple-element.31), channel_id=1, source_target_pairs={{0,192},{1,193},{2,194},{3,195},{4,196},{5,197},{6,198},{7,199},{8... | collective-permute-start | bytes 294920 | tf_op jit(solution)/shard_map/ppermute | solution.py:35
  53.4 1.0 copy-start.2
  58.5 24.4 %collective-permute-start.18 = (bf16[512,384]{1,0:T(8,128)(2,1)}, bf16[512,384]{1,0:T(8,128)(2,1)S(1)}, u32[]{:S(2)}, u32[]{:S(2)}) collective-permute-start(bf16[512,384]{1,0:T(8,128)(2,1)} %get-tuple-element.17), channel_id=1, source_target_pairs={{0,2},{1,3},{2,4},{3,5},{4,6},{5,7},{6,0},{7,1},{8,10},{9,11},{10,... | collective-permute-start | bytes 1179656 | tf_op jit(solution)/shard_map/ppermute | solution.py:35
  63.3 3.0 %copy-start.4 = (bf16[1024,384]{1,0:T(8,128)(2,1)}, bf16[1024,384]{1,0:T(8,128)(2,1)S(1)}, u32[]{:S(2)}) copy-start(bf16[1024,384]{1,0:T(8,128)(2,1)S(1)} %collective-permute-done.other.refs_3_) | copy-start | bytes 2359300
  63.3 19.7 %collective-permute-start.19 = (bf16[512,384]{1,0:T(8,128)(2,1)}, bf16[512,384]{1,0:T(8,128)(2,1)S(1)}, u32[]{:S(2)}, u32[]{:S(2)}) collective-permute-start(bf16[512,384]{1,0:T(8,128)(2,1)} %get-tuple-element.18), channel_id=1, source_target_pairs={{0,6},{1,7},{2,0},{3,1},{4,2},{5,3},{6,4},{7,5},{8,14},{9,15},{10,... | collective-permute-start | bytes 1179656 | tf_op jit(solution)/shard_map/ppermute | solution.py:35
  70.5 22.9 %collective-permute-start.2 = (bf16[512,384]{1,0:T(8,128)(2,1)}, bf16[512,384]{1,0:T(8,128)(2,1)S(1)}, u32[]{:S(2)}, u32[]{:S(2)}) collective-permute-start(bf16[512,384]{1,0:T(8,128)(2,1)} %get-tuple-element.13), channel_id=1, source_target_pairs={{0,2},{1,3},{2,4},{3,5},{4,6},{5,7},{6,0},{7,1},{8,10},{9,11},{10,... | collective-permute-start | bytes 1179656 | tf_op jit(solution)/shard_map/ppermute | solution.py:35
  70.5 24.7 %collective-permute-start.3 = (bf16[512,384]{1,0:T(8,128)(2,1)}, bf16[512,384]{1,0:T(8,128)(2,1)S(1)}, u32[]{:S(2)}, u32[]{:S(2)}) collective-permute-start(bf16[512,384]{1,0:T(8,128)(2,1)} %get-tuple-element.14), channel_id=1, source_target_pairs={{0,6},{1,7},{2,0},{3,1},{4,2},{5,3},{6,4},{7,5},{8,14},{9,15},{10,... | collective-permute-start | bytes 1179656 | tf_op jit(solution)/shard_map/ppermute | solution.py:35
  73.7 4.9 %copy-start.15 = (bf16[64,384]{1,0:T(8,128)(2,1)}, bf16[64,384]{1,0:T(8,128)(2,1)S(1)}, u32[]{:S(2)}) copy-start(bf16[64,384]{1,0:T(8,128)(2,1)S(1)} %get-tuple-element.38.down_own) | copy-start | bytes 147460
  73.8 4.9 %collective-permute-start.13 = (bf16[64,384]{1,0:T(8,128)(2,1)S(1)}, bf16[64,384]{1,0:T(8,128)(2,1)S(1)}, u32[]{:S(2)}, u32[]{:S(2)}) collective-permute-start(bf16[64,384]{1,0:T(8,128)(2,1)S(1)} %get-tuple-element.38.down_own), channel_id=1, source_target_pairs={{0,1},{1,0},{2,3},{3,2},{4,5},{5,4},{6,7},{7,6},{8,9},{9,8},{10,11... | collective-permute-start | bytes 147464 | tf_op jit(solution)/shard_map/ppermute | solution.py:35
  78.6 0.6 copy-start.16
  82.9 10.4 %copy-start.6 = (bf16[64,2048]{1,0:T(8,128)(2,1)S(1)}, bf16[64,2048]{1,0:T(8,128)(2,1)}, u32[]{:S(2)}) copy-start(bf16[64,2048]{1,0:T(8,128)(2,1)} %lowrank.1) | copy-start | bytes 786436
  82.9 20.0 %collective-permute-start.15 = (bf16[64,2048]{1,0:T(8,128)(2,1)}, bf16[64,2048]{1,0:T(8,128)(2,1)S(1)}, u32[]{:S(2)}, u32[]{:S(2)}) collective-permute-start(bf16[64,2048]{1,0:T(8,128)(2,1)} %lowrank.1), channel_id=1, source_target_pairs={{0,2},{1,3},{2,4},{3,5},{4,6},{5,7},{6,0},{7,1},{8,10},{9,11},{10,... | collective-permute-start | bytes 786440 | tf_op jit(solution)/shard_map/ppermute | solution.py:35
  82.9 0.7 copy-start.12
  83.7 0.8 copy-start.14
  90.1 44.3 %collective-permute-start.20 = (bf16[1024,384]{1,0:T(8,128)(2,1)}, bf16[1024,384]{1,0:T(8,128)(2,1)S(1)}, u32[]{:S(2)}, u32[]{:S(2)}) collective-permute-start(bf16[1024,384]{1,0:T(8,128)(2,1)} %get-tuple-element.19), channel_id=1, source_target_pairs={{0,2},{1,3},{2,4},{3,5},{4,6},{5,7},{6,0},{7,1},{8,10},{9,11},{10,... | collective-permute-start | bytes 2359304 | tf_op jit(solution)/shard_map/ppermute | solution.py:35
  90.1 44.3 %collective-permute-start.21 = (bf16[1024,384]{1,0:T(8,128)(2,1)}, bf16[1024,384]{1,0:T(8,128)(2,1)S(1)}, u32[]{:S(2)}, u32[]{:S(2)}) collective-permute-start(bf16[1024,384]{1,0:T(8,128)(2,1)} %get-tuple-element.20), channel_id=1, source_target_pairs={{0,6},{1,7},{2,0},{3,1},{4,2},{5,3},{6,4},{7,5},{8,14},{9,15},{10,... | collective-permute-start | bytes 2359304 | tf_op jit(solution)/shard_map/ppermute | solution.py:35
  93.4 1.8 %copy-start.11 = (bf16[512,384]{1,0:T(8,128)(2,1)}, bf16[512,384]{1,0:T(8,128)(2,1)S(1)}, u32[]{:S(2)}) copy-start(bf16[512,384]{1,0:T(8,128)(2,1)S(1)} %collective-permute-done.2.got_r) | copy-start | bytes 1179652
  93.4 25.7 %collective-permute-start.16 = (bf16[64,2048]{1,0:T(8,128)(2,1)S(1)}, bf16[64,2048]{1,0:T(8,128)(2,1)S(1)}, u32[]{:S(2)}, u32[]{:S(2)}) collective-permute-start(bf16[64,2048]{1,0:T(8,128)(2,1)S(1)} %copy-done.6), channel_id=1, source_target_pairs={{0,4},{1,5},{2,6},{3,7},{4,0},{5,1},{6,2},{7,3},{8,12},{9,13},{10,... | collective-permute-start | bytes 786440 | tf_op jit(solution)/shard_map/ppermute | solution.py:35
  95.2 0.8 copy-start.13
  101.5 40.9 %collective-permute-start.4 = (bf16[1024,384]{1,0:T(8,128)(2,1)}, bf16[1024,384]{1,0:T(8,128)(2,1)S(1)}, u32[]{:S(2)}, u32[]{:S(2)}) collective-permute-start(bf16[1024,384]{1,0:T(8,128)(2,1)} %get-tuple-element.15), channel_id=1, source_target_pairs={{0,2},{1,3},{2,4},{3,5},{4,6},{5,7},{6,0},{7,1},{8,10},{9,11},{10,... | collective-permute-start | bytes 2359304 | tf_op jit(solution)/shard_map/ppermute | solution.py:35
  102.9 39.5 %collective-permute-start.5 = (bf16[1024,384]{1,0:T(8,128)(2,1)}, bf16[1024,384]{1,0:T(8,128)(2,1)S(1)}, u32[]{:S(2)}, u32[]{:S(2)}) collective-permute-start(bf16[1024,384]{1,0:T(8,128)(2,1)} %get-tuple-element.16), channel_id=1, source_target_pairs={{0,6},{1,7},{2,0},{3,1},{4,2},{5,3},{6,4},{7,5},{8,14},{9,15},{10,... | collective-permute-start | bytes 2359304 | tf_op jit(solution)/shard_map/ppermute | solution.py:35
  119.1 14.3 %collective-permute-start.17 = (bf16[64,2048]{1,0:T(8,128)(2,1)S(1)}, bf16[64,2048]{1,0:T(8,128)(2,1)S(1)}, u32[]{:S(2)}, u32[]{:S(2)}) collective-permute-start(bf16[64,2048]{1,0:T(8,128)(2,1)S(1)} %copy-done.6), channel_id=1, source_target_pairs={{0,6},{1,7},{2,0},{3,1},{4,2},{5,3},{6,4},{7,5},{8,14},{9,15},{10,... | collective-permute-start | bytes 786440 | tf_op jit(solution)/shard_map/ppermute | solution.py:35
  134.5 1.0 copy-start.7
  135.4 1.0 copy-start.8
  142.4 0.9 copy-start.9
  143.3 0.9 copy-start.10

commit v2 on v1

v2 whole, which is shorter than its diff:
```python
import functools

import jax
import jax.numpy as jnp
from jax import lax
from jax.experimental import pallas as pl
from jax.experimental.pallas import tpu as pltpu
from jax.sharding import PartitionSpec as P

HD = 128
NY, NZ, NX, NC, NH = 4, 2, 4, 2, 4
LOG2E = 1.4426950408889634
LARGE = 60 * 1024 * 1024
SMALL = 32 * 1024 * 1024
TILE = 256
STEP = 512
F32 = jnp.float32
BF16 = jnp.bfloat16


def table(move):
    pairs = []
    for h in range(NH):
        for x in range(NX):
            for c in range(NC):
                for y in range(NY):
                    for z in range(NZ):
                        here = ((h * NX + x) * NC + c) * NY * NZ + y * NZ + z
                        h2, x2, c2, y2, z2 = move(h, x, c, y, z)
                        h2, x2, c2, y2, z2 = h2 % NH, x2 % NX, c2 % NC, y2 % NY, z2 % NZ
                        there = ((h2 * NX + x2) * NC + c2) * NY * NZ + y2 * NZ + z2
                        pairs.append((here, there))
    return pairs


def send(array, move):
    return lax.ppermute(array, ("rep", "tp"), table(move))


def to_y(k):
    return lambda h, x, c, y, z: (h, x, c, y + k, z)


def to_x(k):
    return lambda h, x, c, y, z: (h, x + k, c, y, z)


def to_h(k):
    return lambda h, x, c, y, z: (h + k, x, c, y, z)


def swap_z(h, x, c, y, z):
    return (h, x, c, y, 1 - z)


def swap_core(h, x, c, y, z):
    return (h, x, 1 - c, y, z)


def pair_y(step):
    return lambda h, x, c, y, z: (h, x, c, y ^ step, z)


def pair_x(step):
    return lambda h, x, c, y, z: (h, x ^ step, c, y, z)


def other_z(h, x, c, y, z):
    return (h - 1 + 2 * z, x, c, y, 1 - z)


def params(size=SMALL):
    return pltpu.CompilerParams(vmem_limit_bytes=size)


def cost(flops, moved):
    return pl.CostEstimate(flops=flops, bytes_accessed=moved, transcendentals=0)


def attend_kernel(q_ref, k_ref, v_ref, out):
    rows = out.shape[0]
    k = k_ref[0]
    v = v_ref[0]
    v_one = jnp.concatenate([v, jnp.ones_like(v)], axis=1)
    factor = LOG2E * HD ** (-0.5)
    for begin in range(0, rows, TILE):
        part = slice(begin, begin + TILE)
        q = q_ref[0, part]
        s = lax.dot_general(q, k, (((1,), (1,)), ((), ())), preferred_element_type=F32)
        top = jnp.max(s, axis=1, keepdims=True)
        p = jnp.exp2((s - top) * factor).astype(BF16)
        o = jnp.dot(p, v_one, preferred_element_type=F32)
        out[part] = (o[:, :HD] / o[:, HD:]).astype(BF16)


def attend(queries, keys, values, chunk):
    b, first, rows = chunk
    seq, width = queries.shape[1:]
    whole = pl.BlockSpec((1, seq, HD), lambda h: (b, 0, h))
    return pl.pallas_call(
        attend_kernel,
        grid=(width // HD,),
        in_specs=[pl.BlockSpec((1, rows, HD), lambda h: (b, first // rows, h)), whole, whole],
        out_specs=pl.BlockSpec((rows, HD), lambda h: (0, h)),
        out_shape=jax.ShapeDtypeStruct((rows, width), BF16),
        compiler_params=params(LARGE),
        cost_estimate=cost(4 * rows * seq * width, 4 * (rows + seq) * width),
        name="attend",
    )(queries, keys, values)


def own_block(shift):
    return lambda i, s: (0, lax.rem(s[0] + shift, NY) * NZ + s[1])


def joined(first, second, axis):
    return jnp.concatenate([first[...], second[...]], axis=axis)


def after(value, *earlier):
    return lax.optimization_barrier((value, *earlier))[0]


def far_kernel(marks, own, other, w_own, w_other, *outs):
    w = joined(w_own, w_other, 0)
    total = jnp.dot(joined(own, other, 1), w, preferred_element_type=F32).astype(BF16)
    at = 0
    for out in outs:
        out[...] = total[at : at + out.shape[0]]
        at += out.shape[0]


def far(marks, own, other, weight, swapped, parts):
    rows, width = own.shape
    fixed = lambda i, s: (0, 0)
    tile = pl.BlockSpec((rows, width), fixed)
    return pl.pallas_call(
        far_kernel,
        grid_spec=pltpu.PrefetchScalarGridSpec(
            num_scalar_prefetch=1,
            grid=(1,),
            in_specs=[
                tile,
                tile,
                pl.BlockSpec((width, width), own_block(2)),
                pl.BlockSpec((width, width), fixed),
            ],
            out_specs=[pl.BlockSpec((rows // parts, width), fixed)] * parts,
        ),
        out_shape=[jax.ShapeDtypeStruct((rows // parts, width), BF16)] * parts,
        compiler_params=params(),
        cost_estimate=cost(4 * rows * width * width, 6 * rows * width),
        name="far",
    )(marks, own, other, weight, swapped)


def near_kernel(places, marks, own, other, w_r, w_l, r_other, l_other, *refs):
    outs = refs[-2:]
    width = w_r.shape[1]
    w = joined(w_r, w_l, 1)
    w = jnp.concatenate([w, joined(r_other, l_other, 1)], axis=0)
    total = jnp.dot(joined(own, other, 1), w, preferred_element_type=F32)
    for side, out in enumerate(outs):
        part = total[:, side * width : (side + 1) * width]
        out[...] = part.astype(BF16)
        for got, (where, first) in zip(refs, places):
            if where == side:
                last = first + got.shape[0]
                out[first:last] = (part[first:last] + got[...].astype(F32)).astype(BF16)


def near(marks, own, other, weight, first, gots, places):
    rows, width = own.shape
    fixed = lambda i, s: (0, 0)
    tile = pl.BlockSpec((rows, width), fixed)
    return pl.pallas_call(
        functools.partial(near_kernel, places),
        grid_spec=pltpu.PrefetchScalarGridSpec(
            num_scalar_prefetch=1,
            grid=(1,),
            in_specs=[
                tile,
                tile,
                pl.BlockSpec((width, width), own_block(1)),
                pl.BlockSpec((width, width), own_block(NY - 1)),
                pl.BlockSpec((width, width), lambda i, s: (0, 1)),
                pl.BlockSpec((width, width), lambda i, s: (0, 2)),
            ]
            + [pl.BlockSpec(got.shape, fixed) for got in gots],
            out_specs=[tile, tile],
        ),
        out_shape=[jax.ShapeDtypeStruct((rows, width), BF16)] * 2,
        compiler_params=params(),
        cost_estimate=cost(8 * rows * width * width, 10 * rows * width),
        name="near",
    )(marks, own, other, weight, weight, first, first, *gots)


def lowrank_kernel(down_own, down_other, *refs):
    out = refs[-1]
    n = (len(refs) - 1) // 2
    dims = (((1,), (1,)), ((), ()))
    at = 0
    for own, other in zip(refs[:n], refs[n : 2 * n]):
        t = lax.dot_general(down_own[...], own[...], dims, preferred_element_type=F32)
        t = t + lax.dot_general(down_other[...], other[...], dims, preferred_element_type=F32)
        out[:, at : at + own.shape[0]] = t.astype(BF16)
        at += own.shape[0]


def lowrank(down_own, down_other, own, other):
    tokens = sum(a.shape[0] for a in own)
    width = own[0].shape[1]
    rank = down_own.shape[0]
    return pl.pallas_call(
        lowrank_kernel,
        out_shape=jax.ShapeDtypeStruct((rank, tokens), BF16),
        compiler_params=params(),
        cost_estimate=cost(4 * tokens * width * rank, 4 * tokens * width),
        name="lowrank",
    )(down_own, down_other, *own, *other)


def home_kernel(b, n, marks, counts, own, other, w_own, w_other, t, up, residual, gate, *rest):
    out = rest[-1]
    w = joined(w_own, w_other, 0)
    total = jnp.dot(joined(own, other, 1), w, preferred_element_type=F32)
    for got in rest[:n]:
        total = total + got[...].astype(F32)
    dims = (((0,), (0,)), ((), ()))
    total = total + lax.dot_general(t[...], up[...], dims, preferred_element_type=F32)
    g = gate[...][b : b + 1].astype(F32) * (b < counts[marks[2]]).astype(F32)
    out[0] = (residual[0].astype(F32) + g * total).astype(BF16)


def home(marks, chunk, own, other, weight, swapped, gots, t, up, residual, gate, counts, earlier):
    b, first, rows = chunk
    batch, seq, width = residual.shape
    step = min(rows, STEP)
    fixed = lambda i, s, n: (0, 0)
    tile = pl.BlockSpec((step, width), lambda i, s, n: (i, 0))
    place = pl.BlockSpec((1, step, width), lambda i, s, n: (b, first // step + i, 0))
    extra = [] if earlier is None else [earlier]
    return pl.pallas_call(
        functools.partial(home_kernel, b, len(gots)),
        grid_spec=pltpu.PrefetchScalarGridSpec(
            num_scalar_prefetch=2,
            grid=(rows // step,),
            in_specs=[
                tile,
                tile,
                pl.BlockSpec((width, width), lambda i, s, n: (0, s[0] * NZ + s[1])),
                pl.BlockSpec((width, width), lambda i, s, n: (0, 3)),
                pl.BlockSpec((up.shape[0], step), lambda i, s, n: (0, (b * seq + first) // step + i)),
                pl.BlockSpec(up.shape, fixed),
                place,
                pl.BlockSpec((batch, width), fixed),
            ]
            + [tile] * len(gots)
            + [pl.BlockSpec(memory_space=pl.ANY)] * len(extra),
            out_specs=place,
        ),
        out_shape=jax.ShapeDtypeStruct(residual.shape, BF16),
        input_output_aliases={10 + len(gots): 0} if extra else {},
        compiler_params=params(),
        cost_estimate=cost(4 * rows * width * width, 12 * rows * width),
        name="home",
    )(marks, counts, own, other, weight, swapped, t, up, residual, gate, *gots, *extra)


def adapter_place(info, ids, slots, dest, count):
    return slots[ids[dest]] - info[2] * count


def choose_kernel(info, ids, slots, down, up, away):
    n = down.shape[0]
    for place in range(NH * NX):
        wanted = adapter_place(info, ids, slots, place * NC + 1 - info[3], n)
        away[place] = jnp.zeros(away.shape[1:], BF16)
        for k in range(n):

            @pl.when(wanted == k)
            def _():
                away[place, 0] = down[k]
                away[place, 1] = up[k]


def choose(info, ids, slots, down_pool, up_pool):
    rank, width = up_pool.shape[1:]
    smem = pl.BlockSpec(memory_space=pltpu.SMEM)
    vmem = pl.BlockSpec(memory_space=pltpu.VMEM)
    shape = (NH * NX, 2, rank, width)
    return pl.pallas_call(
        choose_kernel,
        in_specs=[smem] * 3 + [vmem] * 2,
        out_specs=vmem,
        out_shape=jax.ShapeDtypeStruct(shape, BF16),
        compiler_params=params(LARGE),
        cost_estimate=cost(0, 2 * NH * NX * 2 * rank * width),
        name="choose",
    )(info, ids, slots, down_pool, up_pool)


def keep_kernel(info, ids, slots, down, up, got, mine, away):
    n = down.shape[0]
    for h in range(NH):
        for i in range(NX // 2):
            for out, bit in ((mine, info[4]), (away, 1 - info[4])):
                place = h * NX + bit * (NX // 2) + i
                wanted = adapter_place(info, ids, slots, place * NC + info[3], n)
                out[h, i] = got[place]
                for k in range(n):

                    @pl.when(wanted == k)
                    def _():
                        out[h, i, 0] = got[place, 0] + down[k]
                        out[h, i, 1] = got[place, 1] + up[k]


def keep(info, ids, slots, down_pool, up_pool, got):
    rank, width = up_pool.shape[1:]
    smem = pl.BlockSpec(memory_space=pltpu.SMEM)
    vmem = pl.BlockSpec(memory_space=pltpu.VMEM)
    half = jax.ShapeDtypeStruct((NH, NX // 2, 2, rank, width), BF16)
    return pl.pallas_call(
        keep_kernel,
        in_specs=[smem] * 3 + [vmem] * 3,
        out_specs=[vmem] * 2,
        out_shape=[half, half],
        compiler_params=params(LARGE),
        cost_estimate=cost(0, 4 * NH * NX * 2 * rank * width),
        name="keep",
    )(info, ids, slots, down_pool, up_pool, got)


def merge_kernel(at, info, a, b, mine, away):
    bit = info[at]
    for p in range(a.shape[0]):
        for q in range(a.shape[2]):
            mine[p, q] = a[p, bit, q] + b[p, bit, q]
            away[p, q] = a[p, 1 - bit, q] + b[p, 1 - bit, q]


def merge(info, at, a, b, lead):
    whole = a.shape[-3:]
    count = a.size // (whole[0] * whole[1] * whole[2])
    split = (lead, 2, count // lead // 2) + whole
    half = jax.ShapeDtypeStruct((lead, count // lead // 2) + whole, BF16)
    vmem = pl.BlockSpec(memory_space=pltpu.VMEM)
    return pl.pallas_call(
        functools.partial(merge_kernel, at),
        in_specs=[pl.BlockSpec(memory_space=pltpu.SMEM), vmem, vmem],
        out_specs=[vmem, vmem],
        out_shape=[half, half],
        compiler_params=params(),
        cost_estimate=cost(0, 6 * a.size),
        name="merge",
    )(info, a.reshape(split), b.reshape(split))


def fan_kernel(info, a, b, *outs):
    for i, out in enumerate(outs):
        h = lax.rem(2 * info[6] + info[7] + i, NH)
        out[...] = a[h] + b[h]


def fan(info, a, b):
    shape = (NH,) + a.shape[-3:]
    vmem = pl.BlockSpec(memory_space=pltpu.VMEM)
    return pl.pallas_call(
        fan_kernel,
        in_specs=[pl.BlockSpec(memory_space=pltpu.SMEM), vmem, vmem],
        out_specs=[vmem] * NH,
        out_shape=[jax.ShapeDtypeStruct(shape[1:], BF16)] * NH,
        compiler_params=params(),
        cost_estimate=cost(0, 6 * a.size),
        name="fan",
    )(info, a.reshape(shape), b.reshape(shape))


def settle_kernel(a, b, c, d, down, up):
    for i, out in enumerate((down, up)):
        out[...] = a[i] + b[i] + c[i] + d[i]


def settle(parts):
    shape = parts[0].shape[1:]
    vmem = pl.BlockSpec(memory_space=pltpu.VMEM)
    return pl.pallas_call(
        settle_kernel,
        in_specs=[vmem] * NH,
        out_specs=[vmem] * 2,
        out_shape=[jax.ShapeDtypeStruct(shape, BF16)] * 2,
        compiler_params=params(),
        cost_estimate=cost(0, 10 * parts[0].size),
        name="settle",
    )(*parts)


def cut_kernel(info, a, b, c, d, out):
    width = a.shape[1]
    for i, block in enumerate((a, b, c, d)):
        out[:, i * width : (i + 1) * width] = block[...]


def cut(info, weight, width):
    def block(shift):
        return pl.BlockSpec((width, width), lambda i, s: (0, lax.rem(s[0] + shift, NY) * NZ + 1 - s[1]))

    return pl.pallas_call(
        cut_kernel,
        grid_spec=pltpu.PrefetchScalarGridSpec(
            num_scalar_prefetch=1,
            grid=(1,),
            in_specs=[block(shift) for shift in (2, 1, NY - 1, 0)],
            out_specs=pl.BlockSpec((width, NY * width), lambda i, s: (0, 0)),
        ),
        out_shape=jax.ShapeDtypeStruct((width, NY * width), BF16),
        compiler_params=params(LARGE),
        cost_estimate=cost(0, 16 * width * width),
        name="cut",
    )(info, *[weight] * 4)


def spread_kernel(marks, own, other, w_f, w_r, w_l, w_other, *outs):
    width = w_f.shape[1]
    w = jnp.concatenate([w_f[...], w_r[...], w_l[...]], axis=1)
    w = jnp.concatenate([w, w_other[...]], axis=0)
    total = jnp.dot(joined(own, other, 1), w, preferred_element_type=F32)
    for i, out in enumerate(outs):
        out[...] = total[:, i * width : (i + 1) * width].astype(BF16)


def spread(marks, own, other, weight, first):
    rows, width = own.shape
    fixed = lambda i, s: (0, 0)
    tile = pl.BlockSpec((rows, width), fixed)
    return pl.pallas_call(
        spread_kernel,
        grid_spec=pltpu.PrefetchScalarGridSpec(
            num_scalar_prefetch=1,
            grid=(1,),
            in_specs=[tile, tile]
            + [pl.BlockSpec((width, width), own_block(shift)) for shift in (2, 1, NY - 1)]
            + [pl.BlockSpec((width, 3 * width), fixed)],
            out_specs=[tile] * 3,
        ),
        out_shape=[jax.ShapeDtypeStruct((rows, width), BF16)] * 3,
        compiler_params=params(),
        cost_estimate=cost(12 * rows * width * width, 10 * rows * width),
        name="spread",
    )(marks, own, other, weight, weight, weight, first)


def per_device(
    queries,
    keys,
    values,
    output_weight,
    adapter_down_pool,
    adapter_up_pool,
    residual,
    gate,
    adapter_id,
    adapter_slot,
    request_count,
):
    rep = lax.axis_index("rep")
    tp = lax.axis_index("tp")
    c = lax.rem(rep, NC)
    x = lax.rem(lax.div(rep, NC), NX)
    h = lax.div(rep, NC * NX)
    y = lax.div(tp, NZ)
    z = lax.rem(tp, NZ)
    batch, seq, width = residual.shape

    info = jnp.stack([y, z, rep, c, lax.div(x, 2), lax.rem(x, 2), lax.div(h, 2), lax.rem(h, 2)])
    chunks = [(0, 0, seq // 2), (1, 0, seq), (0, seq // 2, seq // 2)]
    turns = (to_y(1), to_y(-1))
    own, other = [], []

    def mix(*earlier):
        a = attend(after(queries, *earlier), keys, values, chunks[len(own)])
        own.append(a)
        other.append(send(a, swap_z))

    def first_half(i, *earlier):
        return far(after(info, *earlier), own[i], other[i], output_weight, swapped, 2)

    def pass_on(i, halves):
        return [send(part, turn) for part, turn in zip(halves, turns)]

    def second_half(i, gots, *earlier):
        places = [(side, side * gots[0].shape[0]) for side in range(2)]
        marks = after(info, *earlier)
        sums = near(marks, own[i], other[i], output_weight, swapped, gots, places)
        return sums, [send(part, turn) for part, turn in zip(sums, turns)]

    piece = cut(info, output_weight, width)
    swapped = send(piece, other_z)
    pools = adapter_id, adapter_slot, jnp.swapaxes(adapter_down_pool, 1, 2), adapter_up_pool
    away = choose(after(info, piece), *pools)
    got = send(away, swap_core)
    mix(away)
    mix(own[0])
    held, away = keep(after(info, own[1], other[0]), *pools, got)
    got = send(away, pair_x(2))
    mix(away)
    messages = spread(after(info, own[2]), own[0], other[0], output_weight, swapped)
    home0 = [send(part, turn) for part, turn in zip(messages, (to_y(2),) + turns)]
    far1 = first_half(1, *messages)
    got1 = pass_on(1, far1)
    held, away = merge(after(info, *far1), 5, held, got, NH)
    got = send(away, pair_x(1))
    far2 = first_half(2, away)
    got2 = pass_on(2, far2)
    held = fan(after(info, *far2), held, got)
    parts = [held[0]] + [send(part, to_h(d + 1)) for d, part in enumerate(held[1:])]
    near1, home1 = second_half(1, got1, *held, *home0, *got2)
    near2, home2 = second_half(2, got2, *near1)
    parts[0] = after(parts[0], *near2)
    down, up = settle(parts)
    order = (0, 2, 1)
    t = lowrank(down, send(down, swap_z), [own[i] for i in order], [other[i] for i in order])
    t = after(t + send(t, pair_y(1)), *home1, *home2)
    t = t + send(t, pair_y(2))

    result = None
    for chunk, mine, theirs, gots in zip(chunks, own, other, (home0, home1, home2)):
        result = home(
            info, chunk, mine, theirs, output_weight, swapped, gots, t, up, residual, gate, request_count, result
        )
    return result


def solution(mesh):
    placed = (
        P("rep", None, "tp"),
        P("rep", None, "tp"),
        P("rep", None, "tp"),
        P("tp", None),
        P("rep", "tp", None),
        P("rep", None, "tp"),
        P("rep", None, "tp"),
        P("rep", "tp"),
        P(),
        P(),
        P(),
    )
    return jax.shard_map(
        per_device, mesh=mesh, in_specs=placed, out_specs=P("rep", None, "tp"), check_vma=False
    )
```

time: 153 us -> 132 us (0.86); the launches traced: 150 us -> 131 us
  other arithmetic: 11.9 us -> 0.13 us
  local copies, waits for them, and re-layouts: 11.8 us -> 2.79 us
  starting transfers between devices: 38 us -> 43.9 us
  waiting for transfers between devices: 39.2 us -> 35.8 us
    unnamed x36 -> x26, local copies, waits for them, and re-layouts: 8.78 us -> 2.2 us
    ppermute x22 -> x24, starting transfers between devices: 38 us -> 43.9 us  [send(): return lax.ppermute(array, ('rep', 'tp'), table(move))]
    add x5 -> x2, other arithmetic: 5.23 us -> 0.13 us  [the longest x1 0.06 us: per_device(): t = after(t + send(t, pair_y(1)), *home1, *home2)]
    pallas_call x2, Pallas kernels: 8.28 us -> 3.78 us  [far(): pl.pallas_call(far_kernel, grid_spec=pltpu.PrefetchScalarGridSpec(num_sca...]
    ppermute x22 -> x24, waiting for transfers between devices: 39.2 us -> 35.8 us  [send(): return lax.ppermute(array, ('rep', 'tp'), table(move))]
    pallas_call x2 -> x3, Pallas kernels: 13.8 us -> 17.2 us  [attend(): pl.pallas_call(attend_kernel, grid=(width // HD,), in_specs=[pl.BlockSpec...]
    concatenate x3 -> x0, other arithmetic: 2.92 us -> none  [the longest x1 1.13 us: per_device(): swapped = send(jnp.concatenate(pieces, axis=1), other_z)]
    another operation x2 -> x0, other arithmetic: 1.94 us -> none  [per_device(): marks = jnp.stack([y, z, count, jnp.int32(chunk[0])])]
  transfers between devices with their start and end apart: 22 -> 24, of which waited for: 5 -> 11; matrix products, arithmetic and copies ran while one was open for 7% -> 0% of each run, Pallas kernels for 29% -> 24%
where the time goes in v2:
time: 132 us; the launch traced here: 131 us
  Pallas kernels  48.1 us (36%)
  starting transfers between devices  43.9 us (33%)
  waiting for transfers between devices  35.8 us (27%)
  local copies, waits for them, and re-layouts  2.79 us (2%)
    ppermute x24, starting transfers between devices, send(): return lax.ppermute(array, ('rep', 'tp'), table(move))  43.9 us
    ppermute x24, waiting for transfers between devices, send(): return lax.ppermute(array, ('rep', 'tp'), table(move))  35.8 us
    pallas_call x3, Pallas kernels, attend(): pl.pallas_call(attend_kernel, grid=(width // HD,), in_specs=[pl.BlockSpec...  17.2 us
    pallas_call x3, Pallas kernels, home(): pl.pallas_call(functools.partial(home_kernel, b, len(gots)), grid_spec=pl...  7.81 us
    pallas_call x2, Pallas kernels, near(): pl.pallas_call(functools.partial(near_kernel, places), grid_spec=pltpu.Pr...  4.43 us
    pallas_call x2, Pallas kernels, far(): pl.pallas_call(far_kernel, grid_spec=pltpu.PrefetchScalarGridSpec(num_sca...  3.78 us
    pallas_call x1, Pallas kernels, keep(): pl.pallas_call(keep_kernel, in_specs=[smem] * 3 + [vmem] * 3, out_specs=[...  3.31 us
    pallas_call x1, Pallas kernels, cut(): pl.pallas_call(cut_kernel, grid_spec=pltpu.PrefetchScalarGridSpec(num_sca...  3.05 us
  transfers between devices with their start and end apart: 24, of which 11 were waited for; matrix products, arithmetic and copies ran while one was open for 0% of the time, Pallas kernels for 24%

profile of v2, /device:TPU:32, one launch (start us, length us, event | category | flops | bytes accessed | tf_op | source)
XLA Modules:
  0.0 131.0 jit_solution(17383098502120572460)
XLA Ops:
  0.0 0.6 stack.35.info.marks
  0.6 3.0 %cut.1 = bf16[384,1536]{1,0:T(8,128)(2,1)} custom-call(s32[8]{0:T(128)} %stack.35.info.marks, bf16[384,3072]{1,0:T(8,128)(2,1)} %w_own.9, bf16[384,3072]{1,0:T(8,128)(2,1)} %w_own.9, bf16[384,3072]{1,0:T(8,128)(2,1)} %w_own.9, bf16[384,3072]{1,0:T(8,128)(2,1)} %w_own.9), custom_call_target="tpu_custom_call" | custom-call | bytes 2359296 | tf_op jit(solution)/shard_map/cut/pallas_call | solution.py:410
  3.6 2.6 %choose.1 = bf16[16,2,64,384]{3,2,1,0:T(8,128)(2,1)} custom-call(s32[8]{0:T(128)} %stack.35.info.marks, s32[32]{0:T(128)} %ids.3, s32[128]{0:T(128)} %slots.3, bf16[4,64,384]{2,1,0:T(8,128)(2,1)} %bitcast.18, bf16[4,64,384]{2,1,0:T(8,128)(2,1)} %up.3), custom_call_target="tpu_custom_call" | custom-call | bytes 1572864 | tf_op jit(solution)/shard_map/choose/pallas_call | solution.py:293
  6.3 0.0 collective-permute-start.1
  6.3 1.9 %collective-permute-start.3 = (bf16[384,1536]{1,0:T(8,128)(2,1)}, bf16[384,1536]{1,0:T(8,128)(2,1)S(1)}, u32[]{:S(2)}, u32[]{:S(2)}) collective-permute-start(bf16[384,1536]{1,0:T(8,128)(2,1)} %cut.1), channel_id=1, source_target_pairs={{0,193},{1,64},{2,195},{3,66},{4,197},{5,68},{6,199},{7,70},{8,201... | collective-permute-start | bytes 3538952 | tf_op jit(solution)/shard_map/ppermute | solution.py:37
  8.2 5.1 %attend.3.own.refs_0_ = bf16[512,384]{1,0:T(8,128)(2,1)} custom-call(bf16[2,1024,384]{2,1,0:T(8,128)(2,1)} %q_ref.2, bf16[2,1024,384]{2,1,0:T(8,128)(2,1)} %k_ref.5, bf16[2,1024,384]{2,1,0:T(8,128)(2,1)} %v_ref.5), custom_call_target="tpu_custom_call" | custom-call | flops 805306368 | bytes 2359296 | tf_op jit(solution)/shard_map/attend/pallas_call | solution.py:100
  13.3 4.0 %collective-permute-start = (bf16[512,384]{1,0:T(8,128)(2,1)}, bf16[512,384]{1,0:T(8,128)(2,1)S(1)}, u32[]{:S(2)}, u32[]{:S(2)}) collective-permute-start(bf16[512,384]{1,0:T(8,128)(2,1)} %attend.3.own.refs_0_), channel_id=1, source_target_pairs={{0,1},{1,0},{2,3},{3,2},{4,5},{5,4},{6,7},{7,6},{8,9},{9,8},{10,11... | collective-permute-start | bytes 1179656 | tf_op jit(solution)/shard_map/ppermute | solution.py:37
  17.4 6.9 %attend.4.own.refs_2_ = bf16[1024,384]{1,0:T(8,128)(2,1)} custom-call(bf16[2,1024,384]{2,1,0:T(8,128)(2,1)} %q_ref.2, bf16[2,1024,384]{2,1,0:T(8,128)(2,1)} %k_ref.5, bf16[2,1024,384]{2,1,0:T(8,128)(2,1)} %v_ref.5), custom_call_target="tpu_custom_call" | custom-call | flops 1610612736 | bytes 3145728 | tf_op jit(solution)/shard_map/attend/pallas_call | solution.py:100
  24.3 0.0 collective-permute-start.4
  24.3 2.9 %collective-permute-done.other.refs_3_ = bf16[512,384]{1,0:T(8,128)(2,1)S(1)} collective-permute-done((bf16[512,384]{1,0:T(8,128)(2,1)}, bf16[512,384]{1,0:T(8,128)(2,1)S(1)}, u32[]{:S(2)}, u32[]{:S(2)}) %collective-permute-start) | collective-permute-done | bytes 393248 | tf_op jit(solution)/shard_map/ppermute | solution.py:37
  27.2 0.0 collective-permute-done.1.got
  27.2 1.2 copy-done.12
  28.3 3.3 %keep.1 = (bf16[4,2,2,64,384]{4,3,2,1,0:T(8,128)(2,1)}, bf16[4,2,2,64,384]{4,3,2,1,0:T(8,128)(2,1)}) custom-call(s32[8]{0:T(128)} %stack.35.info.marks, s32[32]{0:T(128)} %ids.3, s32[128]{0:T(128)} %slots.3, bf16[4,64,384]{2,1,0:T(8,128)(2,1)} %bitcast.19, bf16[4,64,384]{2,1,0:T(8,128)(2,1)} %up.3, bf16[16,2,64,384]{3,2,1,0:T(8,128)(2,1)} %copy-done.12), custom_call_target="tpu_custom_call" | custom-call | bytes 3145728 | tf_op jit(solution)/shard_map/keep/pallas_call | solution.py:325
  31.7 3.1 %collective-permute-start.5 = (bf16[4,2,2,64,384]{4,3,2,1,0:T(8,128)(2,1)}, bf16[4,2,2,64,384]{4,3,2,1,0:T(8,128)(2,1)}, u32[]{:S(2)}, u32[]{:S(2)}) collective-permute-start(bf16[4,2,2,64,384]{4,3,2,1,0:T(8,128)(2,1)} %get-tuple-element.44), channel_id=1, source_target_pairs={{0,32},{1,33},{2,34},{3,35},{4,36},{5,37},{6,38},{7,39},{8,40},{9,... | collective-permute-start | bytes 2359304 | tf_op jit(solution)/shard_map/ppermute | solution.py:37
  34.8 5.1 %attend.5.own.refs_1_ = bf16[512,384]{1,0:T(8,128)(2,1)} custom-call(bf16[2,1024,384]{2,1,0:T(8,128)(2,1)} %q_ref.2, bf16[2,1024,384]{2,1,0:T(8,128)(2,1)} %k_ref.5, bf16[2,1024,384]{2,1,0:T(8,128)(2,1)} %v_ref.5), custom_call_target="tpu_custom_call" | custom-call | flops 805306368 | bytes 2359296 | tf_op jit(solution)/shard_map/attend/pallas_call | solution.py:100
  39.9 2.4 %collective-permute-start.2 = (bf16[512,384]{1,0:T(8,128)(2,1)}, bf16[512,384]{1,0:T(8,128)(2,1)S(1)}, u32[]{:S(2)}, u32[]{:S(2)}) collective-permute-start(bf16[512,384]{1,0:T(8,128)(2,1)} %attend.5.own.refs_1_), channel_id=1, source_target_pairs={{0,1},{1,0},{2,3},{3,2},{4,5},{5,4},{6,7},{7,6},{8,9},{9,8},{10,11... | collective-permute-start | bytes 1179656 | tf_op jit(solution)/shard_map/ppermute | solution.py:37
  42.3 1.0 copy-done.6
  43.3 1.8 %spread.1 = (bf16[512,384]{1,0:T(8,128)(2,1)S(1)}, bf16[512,384]{1,0:T(8,128)(2,1)S(1)}, bf16[512,384]{1,0:T(8,128)(2,1)S(1)}) custom-call(s32[8]{0:T(128)S(1)} %copy-done.9, bf16[512,384]{1,0:T(8,128)(2,1)S(1)} %copy-done.4, bf16[512,384]{1,0:T(8,128)(2,1)S(1)} %copy-done.6, bf16[384,3072]{1,0:T(8,128)(2,1)S(1)} %copy-done, bf16[384,3072]{1,0:T(8,128)(2,1)S(1)} %copy-done, ...), custom_call_target="tpu_custom_call" | custom-call | flops 905969664 | bytes 1966080 | tf_op jit(solution)/shard_map/spread/pallas_call | solution.py:438
  45.1 3.3 %collective-permute-start.7 = (bf16[512,384]{1,0:T(8,128)(2,1)S(1)}, bf16[512,384]{1,0:T(8,128)(2,1)S(1)}, u32[]{:S(2)}, u32[]{:S(2)}) collective-permute-start(bf16[512,384]{1,0:T(8,128)(2,1)S(1)} %get-tuple-element.47), channel_id=1, source_target_pairs={{0,4},{1,5},{2,6},{3,7},{4,0},{5,1},{6,2},{7,3},{8,12},{9,13},{10,... | collective-permute-start | bytes 1179656 | tf_op jit(solution)/shard_map/ppermute | solution.py:37
  48.4 0.7 collective-permute-start.8
  49.1 0.0 collective-permute-done.4.other.refs_5_
  49.1 2.6 %far.2 = (bf16[512,384]{1,0:T(8,128)(2,1)S(1)}, bf16[512,384]{1,0:T(8,128)(2,1)S(1)}) custom-call(s32[8]{0:T(128)S(1)} %copy-done.9, bf16[1024,384]{1,0:T(8,128)(2,1)S(1)} %copy-done.2, bf16[1024,384]{1,0:T(8,128)(2,1)} %collective-permute-done.4.other.refs_5_, bf16[384,3072]{1,0:T(8,128)(2,1)S(1)} %copy-done, ...), custom_call_target="tpu_custom_call" | custom-call | flops 603979776 | bytes 2359296 | tf_op jit(solution)/shard_map/far/pallas_call | solution.py:137
  51.8 0.0 copy-start.3
  51.8 0.9 collective-permute-done.5
  52.7 1.3 merge.1
  54.0 1.6 %collective-permute-start.6 = (bf16[4,1,2,64,384]{4,3,2,0,1:T(8,128)(2,1)S(1)}, bf16[4,1,2,64,384]{4,3,2,0,1:T(8,128)(2,1)S(1)}, u32[]{:S(2)}, u32[]{:S(2)}) collective-permute-start(bf16[4,1,2,64,384]{4,3,2,0,1:T(8,128)(2,1)S(1)} %bitcast.17), channel_id=1, source_target_pairs={{0,16},{1,17},{2,18},{3,19},{4,20},{5,21},{6,22},{7,23},{8,24},{9,... | collective-permute-start | bytes 1179656 | tf_op jit(solution)/shard_map/ppermute | solution.py:37
  55.5 3.0 %collective-permute-start.9 = (bf16[512,384]{1,0:T(8,128)(2,1)S(1)}, bf16[512,384]{1,0:T(8,128)(2,1)S(1)}, u32[]{:S(2)}, u32[]{:S(2)}) collective-permute-start(bf16[512,384]{1,0:T(8,128)(2,1)S(1)} %get-tuple-element.49), channel_id=1, source_target_pairs={{0,6},{1,7},{2,0},{3,1},{4,2},{5,3},{6,4},{7,5},{8,14},{9,15},{10,... | collective-permute-start | bytes 1179656 | tf_op jit(solution)/shard_map/ppermute | solution.py:37
  58.5 0.0 collective-permute-done.2.other.refs_4_
  58.5 0.3 collective-permute-done.7.rest_0_
  58.8 3.0 %collective-permute-start.13 = (bf16[512,384]{1,0:T(8,128)(2,1)S(1)}, bf16[512,384]{1,0:T(8,128)(2,1)S(1)}, u32[]{:S(2)}, u32[]{:S(2)}) collective-permute-start(bf16[512,384]{1,0:T(8,128)(2,1)S(1)} %get-tuple-element.52), channel_id=1, source_target_pairs={{0,6},{1,7},{2,0},{3,1},{4,2},{5,3},{6,4},{7,5},{8,14},{9,15},{10,... | collective-permute-start | bytes 1179656 | tf_op jit(solution)/shard_map/ppermute | solution.py:37
  61.8 1.1 far.3
  62.9 3.5 %collective-permute-done.8.rest_1_ = bf16[512,384]{1,0:T(8,128)(2,1)S(1)} collective-permute-done((bf16[512,384]{1,0:T(8,128)(2,1)S(1)}, bf16[512,384]{1,0:T(8,128)(2,1)S(1)}, u32[]{:S(2)}, u32[]{:S(2)}) %collective-permute-start.8) | collective-permute-done | bytes 393248 | tf_op jit(solution)/shard_map/ppermute | solution.py:37
  66.4 2.5 %collective-permute-start.10 = (bf16[256,384]{1,0:T(8,128)(2,1)S(1)}, bf16[256,384]{1,0:T(8,128)(2,1)S(1)}, u32[]{:S(2)}, u32[]{:S(2)}) collective-permute-start(bf16[256,384]{1,0:T(8,128)(2,1)S(1)} %get-tuple-element.57), channel_id=1, source_target_pairs={{0,2},{1,3},{2,4},{3,5},{4,6},{5,7},{6,0},{7,1},{8,10},{9,11},{10,... | collective-permute-start | bytes 589832 | tf_op jit(solution)/shard_map/ppermute | solution.py:37
  68.9 0.0 collective-permute-done.6
  68.9 0.8 collective-permute-start.11
  69.7 0.6 fan.1
  70.3 0.0 collective-permute-done.9.rest_2_
  70.3 6.7 %collective-permute-done.10.refs_0_ = bf16[256,384]{1,0:T(8,128)(2,1)S(1)} collective-permute-done((bf16[256,384]{1,0:T(8,128)(2,1)S(1)}, bf16[256,384]{1,0:T(8,128)(2,1)S(1)}, u32[]{:S(2)}, u32[]{:S(2)}) %collective-permute-start.10) | collective-permute-done | bytes 196640 | tf_op jit(solution)/shard_map/ppermute | solution.py:37
  77.0 1.2 collective-permute-done.11.refs_1_
  78.2 0.0 collective-permute-done.12.refs_0_
  78.2 0.0 collective-permute-done.13.refs_1_
  78.2 3.1 %near.2 = (bf16[1024,384]{1,0:T(8,128)(2,1)S(1)}, bf16[1024,384]{1,0:T(8,128)(2,1)S(1)}) custom-call(s32[8]{0:T(128)S(1)} %copy-done.9, bf16[1024,384]{1,0:T(8,128)(2,1)S(1)} %copy-done.2, bf16[1024,384]{1,0:T(8,128)(2,1)} %collective-permute-done.4.other.refs_5_, bf16[384,3072]{1,0:T(8,128)(2,1)S(1)} %copy-done, bf16[384,3072]{1,0:T(8,128)(2,1)S(1)} %copy-done, ...), custom_call_target="tpu_custom_call" | custom-call | flops 1207959552 | bytes 3932160 | tf_op jit(solution)/shard_map/near/pallas_call | solution.py:176
  81.3 1.1 collective-permute-start.19
  82.4 2.8 %collective-permute-start.20 = (bf16[1024,384]{1,0:T(8,128)(2,1)S(1)}, bf16[1024,384]{1,0:T(8,128)(2,1)S(1)}, u32[]{:S(2)}, u32[]{:S(2)}) collective-permute-start(bf16[1024,384]{1,0:T(8,128)(2,1)S(1)} %get-tuple-element.67), channel_id=1, source_target_pairs={{0,6},{1,7},{2,0},{3,1},{4,2},{5,3},{6,4},{7,5},{8,14},{9,15},{10,... | collective-permute-start | bytes 2359304 | tf_op jit(solution)/shard_map/ppermute | solution.py:37
  85.1 0.9 collective-permute-start.14
  86.1 2.9 %collective-permute-start.15 = (bf16[2,64,384]{2,1,0:T(8,128)(2,1)S(1)}, bf16[2,64,384]{2,1,0:T(8,128)(2,1)S(1)}, u32[]{:S(2)}, u32[]{:S(2)}) collective-permute-start(bf16[2,64,384]{2,1,0:T(8,128)(2,1)S(1)} %get-tuple-element.63), channel_id=1, source_target_pairs={{0,128},{1,129},{2,130},{3,131},{4,132},{5,133},{6,134},{7,135},{8... | collective-permute-start | bytes 294920 | tf_op jit(solution)/shard_map/ppermute | solution.py:37
  89.0 2.2 %collective-permute-start.16 = (bf16[2,64,384]{2,1,0:T(8,128)(2,1)S(1)}, bf16[2,64,384]{2,1,0:T(8,128)(2,1)S(1)}, u32[]{:S(2)}, u32[]{:S(2)}) collective-permute-start(bf16[2,64,384]{2,1,0:T(8,128)(2,1)S(1)} %get-tuple-element.64), channel_id=1, source_target_pairs={{0,192},{1,193},{2,194},{3,195},{4,196},{5,197},{6,198},{7,199},{8... | collective-permute-start | bytes 294920 | tf_op jit(solution)/shard_map/ppermute | solution.py:37
  91.1 1.4 %near.3 = (bf16[512,384]{1,0:T(8,128)(2,1)S(1)}, bf16[512,384]{1,0:T(8,128)(2,1)S(1)}) custom-call(s32[8]{0:T(128)S(1)} %copy-done.9, bf16[512,384]{1,0:T(8,128)(2,1)S(1)} %copy-done.3, bf16[512,384]{1,0:T(8,128)(2,1)S(1)} %collective-permute-done.2.other.refs_4_, bf16[384,3072]{1,0:T(8,128)(2,1)S(1)} %copy-done, bf16[384,3072]{1,0:T(8,128)(2,1)S(1)} %copy-done, ...), custom_call_target="tpu_custom_call" | custom-call | flops 603979776 | bytes 1966080 | tf_op jit(solution)/shard_map/near/pallas_call | solution.py:176
  92.5 3.6 %collective-permute-done.14.b = bf16[2,64,384]{2,1,0:T(8,128)(2,1)S(1)} collective-permute-done((bf16[2,64,384]{2,1,0:T(8,128)(2,1)S(1)}, bf16[2,64,384]{2,1,0:T(8,128)(2,1)S(1)}, u32[]{:S(2)}, u32[]{:S(2)}) %collective-permute-start.14) | collective-permute-done | bytes 98336 | tf_op jit(solution)/shard_map/ppermute | solution.py:37
  96.1 0.5 collective-permute-done.15.c
  96.6 2.8 %collective-permute-start.22 = (bf16[512,384]{1,0:T(8,128)(2,1)S(1)}, bf16[512,384]{1,0:T(8,128)(2,1)S(1)}, u32[]{:S(2)}, u32[]{:S(2)}) collective-permute-start(bf16[512,384]{1,0:T(8,128)(2,1)S(1)} %get-tuple-element.70), channel_id=1, source_target_pairs={{0,6},{1,7},{2,0},{3,1},{4,2},{5,3},{6,4},{7,5},{8,14},{9,15},{10,... | collective-permute-start | bytes 1179656 | tf_op jit(solution)/shard_map/ppermute | solution.py:37
  99.4 0.1 collective-permute-start.17
  99.5 4.1 %collective-permute-done.17.down_other = bf16[64,384]{1,0:T(8,128)(2,1)S(1)} collective-permute-done((bf16[64,384]{1,0:T(8,128)(2,1)S(1)}, bf16[64,384]{1,0:T(8,128)(2,1)S(1)}, u32[]{:S(2)}, u32[]{:S(2)}) %collective-permute-start.17) | collective-permute-done | bytes 49184 | tf_op jit(solution)/shard_map/ppermute | solution.py:37
  103.6 2.3 %lowrank.1 = bf16[64,2048]{1,0:T(8,128)(2,1)S(1)} custom-call(bf16[64,384]{1,0:T(8,128)(2,1)S(1)} %get-tuple-element.72.down_own, bf16[64,384]{1,0:T(8,128)(2,1)S(1)} %collective-permute-done.17.down_other, bf16[512,384]{1,0:T(8,128)(2,1)S(1)} %copy-done.4, bf16[512,384]{1,0:T(8,128)(2,1)S(1)} %copy-done.3, bf16[1024,384]{1,0:T(8,128)(2,1)S(1)} %copy-done.2, ...), custom_call_target="tpu_custom_call" | custom-call | flops 201326592 | bytes 3145728 | tf_op jit(solution)/shard_map/lowrank/pallas_call | solution.py:215
  105.8 0.0 copy-start.10
  105.9 0.1 collective-permute-start.18
  106.0 7.8 %collective-permute-done.18 = bf16[64,2048]{1,0:T(8,128)(2,1)S(1)} collective-permute-done((bf16[64,2048]{1,0:T(8,128)(2,1)S(1)}, bf16[64,2048]{1,0:T(8,128)(2,1)S(1)}, u32[]{:S(2)}, u32[]{:S(2)}) %collective-permute-start.18) | collective-permute-done | bytes 262176 | tf_op jit(solution)/shard_map/ppermute | solution.py:37
  113.7 0.1 add.6
  113.8 4.9 %collective-permute-start.23 = (bf16[64,2048]{1,0:T(8,128)(2,1)S(1)}, bf16[64,2048]{1,0:T(8,128)(2,1)S(1)}, u32[]{:S(2)}, u32[]{:S(2)}) collective-permute-start(bf16[64,2048]{1,0:T(8,128)(2,1)S(1)} %add.6), channel_id=1, source_target_pairs={{0,4},{1,5},{2,6},{3,7},{4,0},{5,1},{6,2},{7,3},{8,12},{9,13},{10,... | collective-permute-start | bytes 786440 | tf_op jit(solution)/shard_map/ppermute | solution.py:37
  118.7 4.4 %collective-permute-done.23 = bf16[64,2048]{1,0:T(8,128)(2,1)S(1)} collective-permute-done((bf16[64,2048]{1,0:T(8,128)(2,1)S(1)}, bf16[64,2048]{1,0:T(8,128)(2,1)S(1)}, u32[]{:S(2)}, u32[]{:S(2)}) %collective-permute-start.23) | collective-permute-done | bytes 262176 | tf_op jit(solution)/shard_map/ppermute | solution.py:37
  123.1 0.1 add.7.t
  123.2 2.0 %home.3.rest_2_ = bf16[2,1024,384]{2,1,0:T(8,128)(2,1)} custom-call(s32[8]{0:T(128)S(1)} %copy-done.9, s32[32]{0:T(128)S(1)} %copy-done.11, bf16[512,384]{1,0:T(8,128)(2,1)S(1)} %copy-done.4, bf16[512,384]{1,0:T(8,128)(2,1)S(1)} %copy-done.7, bf16[384,3072]{1,0:T(8,128)(2,1)S(1)} %copy-done, ...), custom_call_target="tpu_custom_call" | custom-call | flops 301989888 | bytes 2359296 | tf_op jit(solution)/shard_map/home/pallas_call | solution.py:244
  125.2 3.8 %home.4.rest_2_ = bf16[2,1024,384]{2,1,0:T(8,128)(2,1)} custom-call(s32[8]{0:T(128)S(1)} %copy-done.9, s32[32]{0:T(128)S(1)} %copy-done.11, bf16[1024,384]{1,0:T(8,128)(2,1)S(1)} %copy-done.2, bf16[1024,384]{1,0:T(8,128)(2,1)} %collective-permute-done.4.other.refs_5_, bf16[384,3072]{1,0:T(8,128)(2,1)S(1)} %copy-done, ...), custom_call_target="tpu_custom_call", output_to_operand_aliasing={{}: (12, {})} | custom-call | flops 603979776 | bytes 4718592 | tf_op jit(solution)/shard_map/home/pallas_call | solution.py:244
  129.0 2.0 %home.5 = bf16[2,1024,384]{2,1,0:T(8,128)(2,1)} custom-call(s32[8]{0:T(128)S(1)} %copy-done.9, s32[32]{0:T(128)S(1)} %copy-done.11, bf16[512,384]{1,0:T(8,128)(2,1)S(1)} %copy-done.3, bf16[512,384]{1,0:T(8,128)(2,1)S(1)} %collective-permute-done.2.other.refs_4_, bf16[384,3072]{1,0:T(8,128)(2,1)S(1)} %copy-done, ...), custom_call_target="tpu_custom_call", output_to_operand_aliasing={{}: (12, {})} | custom-call | flops 301989888 | bytes 2359296 | tf_op jit(solution)/shard_map/home/pallas_call | solution.py:244
  (31 shorter events, 0.1 us)
Async XLA Ops:
  6.3 20.9 %collective-permute-start.1 = (bf16[16,2,64,384]{3,2,1,0:T(8,128)(2,1)}, bf16[16,2,64,384]{3,2,1,0:T(8,128)(2,1)S(1)}, u32[]{:S(2)}, u32[]{:S(2)}) collective-permute-start(bf16[16,2,64,384]{3,2,1,0:T(8,128)(2,1)} %choose.1), channel_id=1, source_target_pairs={{0,8},{1,9},{2,10},{3,11},{4,12},{5,13},{6,14},{7,15},{8,0},{9,1},... | collective-permute-start | bytes 4718600 | tf_op jit(solution)/shard_map/ppermute | solution.py:37
  6.3 36.0 %collective-permute-start.3 = (bf16[384,1536]{1,0:T(8,128)(2,1)}, bf16[384,1536]{1,0:T(8,128)(2,1)S(1)}, u32[]{:S(2)}, u32[]{:S(2)}) collective-permute-start(bf16[384,1536]{1,0:T(8,128)(2,1)} %cut.1), channel_id=1, source_target_pairs={{0,193},{1,64},{2,195},{3,66},{4,197},{5,68},{6,199},{7,70},{8,201... | collective-permute-start | bytes 3538952 | tf_op jit(solution)/shard_map/ppermute | solution.py:37
  13.3 13.8 %collective-permute-start = (bf16[512,384]{1,0:T(8,128)(2,1)}, bf16[512,384]{1,0:T(8,128)(2,1)S(1)}, u32[]{:S(2)}, u32[]{:S(2)}) collective-permute-start(bf16[512,384]{1,0:T(8,128)(2,1)} %attend.3.own.refs_0_), channel_id=1, source_target_pairs={{0,1},{1,0},{2,3},{3,2},{4,5},{5,4},{6,7},{7,6},{8,9},{9,8},{10,11... | collective-permute-start | bytes 1179656 | tf_op jit(solution)/shard_map/ppermute | solution.py:37
  24.3 24.8 %collective-permute-start.4 = (bf16[1024,384]{1,0:T(8,128)(2,1)}, bf16[1024,384]{1,0:T(8,128)(2,1)}, u32[]{:S(2)}, u32[]{:S(2)}) collective-permute-start(bf16[1024,384]{1,0:T(8,128)(2,1)} %attend.4.own.refs_2_), channel_id=1, source_target_pairs={{0,1},{1,0},{2,3},{3,2},{4,5},{5,4},{6,7},{7,6},{8,9},{9,8},{10,11... | collective-permute-start | bytes 2359304 | tf_op jit(solution)/shard_map/ppermute | solution.py:37
  27.2 4.5 %copy-start.5 = (bf16[512,384]{1,0:T(8,128)(2,1)}, bf16[512,384]{1,0:T(8,128)(2,1)S(1)}, u32[]{:S(2)}) copy-start(bf16[512,384]{1,0:T(8,128)(2,1)S(1)} %collective-permute-done.other.refs_3_) | copy-start | bytes 1179652
  27.2 1.2 copy-start.12
  31.7 10.7 %copy-start = (bf16[384,3072]{1,0:T(8,128)(2,1)S(1)}, bf16[384,3072]{1,0:T(8,128)(2,1)}, u32[]{:S(2)}) copy-start(bf16[384,3072]{1,0:T(8,128)(2,1)} %w_own.9) | copy-start | bytes 7077892
  31.7 10.7 %copy-start.4 = (bf16[512,384]{1,0:T(8,128)(2,1)S(1)}, bf16[512,384]{1,0:T(8,128)(2,1)}, u32[]{:S(2)}) copy-start(bf16[512,384]{1,0:T(8,128)(2,1)} %attend.3.own.refs_0_) | copy-start | bytes 1179652
  31.7 10.7 %copy-start.9 = (s32[8]{0:T(128)S(1)}, s32[8]{0:T(128)}, u32[]{:S(2)}) copy-start(s32[8]{0:T(128)} %stack.35.info.marks) | copy-start | bytes 100
  31.7 21.0 %collective-permute-start.5 = (bf16[4,2,2,64,384]{4,3,2,1,0:T(8,128)(2,1)}, bf16[4,2,2,64,384]{4,3,2,1,0:T(8,128)(2,1)}, u32[]{:S(2)}, u32[]{:S(2)}) collective-permute-start(bf16[4,2,2,64,384]{4,3,2,1,0:T(8,128)(2,1)} %get-tuple-element.44), channel_id=1, source_target_pairs={{0,32},{1,33},{2,34},{3,35},{4,36},{5,37},{6,38},{7,39},{8,40},{9,... | collective-permute-start | bytes 2359304 | tf_op jit(solution)/shard_map/ppermute | solution.py:37
  39.9 9.2 %copy-start.2 = (bf16[1024,384]{1,0:T(8,128)(2,1)S(1)}, bf16[1024,384]{1,0:T(8,128)(2,1)}, u32[]{:S(2)}) copy-start(bf16[1024,384]{1,0:T(8,128)(2,1)} %attend.4.own.refs_2_) | copy-start | bytes 2359300
  39.9 18.6 %collective-permute-start.2 = (bf16[512,384]{1,0:T(8,128)(2,1)}, bf16[512,384]{1,0:T(8,128)(2,1)S(1)}, u32[]{:S(2)}, u32[]{:S(2)}) collective-permute-start(bf16[512,384]{1,0:T(8,128)(2,1)} %attend.5.own.refs_1_), channel_id=1, source_target_pairs={{0,1},{1,0},{2,3},{3,2},{4,5},{5,4},{6,7},{7,6},{8,9},{9,8},{10,11... | collective-permute-start | bytes 1179656 | tf_op jit(solution)/shard_map/ppermute | solution.py:37
  42.3 1.0 copy-start.6
  45.1 13.7 %collective-permute-start.7 = (bf16[512,384]{1,0:T(8,128)(2,1)S(1)}, bf16[512,384]{1,0:T(8,128)(2,1)S(1)}, u32[]{:S(2)}, u32[]{:S(2)}) collective-permute-start(bf16[512,384]{1,0:T(8,128)(2,1)S(1)} %get-tuple-element.47), channel_id=1, source_target_pairs={{0,4},{1,5},{2,6},{3,7},{4,0},{5,1},{6,2},{7,3},{8,12},{9,13},{10,... | collective-permute-start | bytes 1179656 | tf_op jit(solution)/shard_map/ppermute | solution.py:37
  48.4 18.0 %collective-permute-start.8 = (bf16[512,384]{1,0:T(8,128)(2,1)S(1)}, bf16[512,384]{1,0:T(8,128)(2,1)S(1)}, u32[]{:S(2)}, u32[]{:S(2)}) collective-permute-start(bf16[512,384]{1,0:T(8,128)(2,1)S(1)} %get-tuple-element.48), channel_id=1, source_target_pairs={{0,2},{1,3},{2,4},{3,5},{4,6},{5,7},{6,0},{7,1},{8,10},{9,11},{10,... | collective-permute-start | bytes 1179656 | tf_op jit(solution)/shard_map/ppermute | solution.py:37
  49.1 3.6 %copy-start.8 = (bf16[4,2,2,64,384]{4,3,2,1,0:T(8,128)(2,1)S(1)}, bf16[4,2,2,64,384]{4,3,2,1,0:T(8,128)(2,1)}, u32[]{:S(2)}) copy-start(bf16[4,2,2,64,384]{4,3,2,1,0:T(8,128)(2,1)} %get-tuple-element.54) | copy-start | bytes 2359300
  51.8 10.0 %copy-start.3 = (bf16[512,384]{1,0:T(8,128)(2,1)S(1)}, bf16[512,384]{1,0:T(8,128)(2,1)}, u32[]{:S(2)}) copy-start(bf16[512,384]{1,0:T(8,128)(2,1)} %attend.5.own.refs_1_) | copy-start | bytes 1179652
  54.0 14.9 %collective-permute-start.6 = (bf16[4,1,2,64,384]{4,3,2,0,1:T(8,128)(2,1)S(1)}, bf16[4,1,2,64,384]{4,3,2,0,1:T(8,128)(2,1)S(1)}, u32[]{:S(2)}, u32[]{:S(2)}) collective-permute-start(bf16[4,1,2,64,384]{4,3,2,0,1:T(8,128)(2,1)S(1)} %bitcast.17), channel_id=1, source_target_pairs={{0,16},{1,17},{2,18},{3,19},{4,20},{5,21},{6,22},{7,23},{8,24},{9,... | collective-permute-start | bytes 1179656 | tf_op jit(solution)/shard_map/ppermute | solution.py:37
  55.5 14.8 %collective-permute-start.9 = (bf16[512,384]{1,0:T(8,128)(2,1)S(1)}, bf16[512,384]{1,0:T(8,128)(2,1)S(1)}, u32[]{:S(2)}, u32[]{:S(2)}) collective-permute-start(bf16[512,384]{1,0:T(8,128)(2,1)S(1)} %get-tuple-element.49), channel_id=1, source_target_pairs={{0,6},{1,7},{2,0},{3,1},{4,2},{5,3},{6,4},{7,5},{8,14},{9,15},{10,... | collective-permute-start | bytes 1179656 | tf_op jit(solution)/shard_map/ppermute | solution.py:37
  58.5 19.7 %collective-permute-start.12 = (bf16[512,384]{1,0:T(8,128)(2,1)S(1)}, bf16[512,384]{1,0:T(8,128)(2,1)S(1)}, u32[]{:S(2)}, u32[]{:S(2)}) collective-permute-start(bf16[512,384]{1,0:T(8,128)(2,1)S(1)} %get-tuple-element.51), channel_id=1, source_target_pairs={{0,2},{1,3},{2,4},{3,5},{4,6},{5,7},{6,0},{7,1},{8,10},{9,11},{10,... | collective-permute-start | bytes 1179656 | tf_op jit(solution)/shard_map/ppermute | solution.py:37
  58.8 19.4 %collective-permute-start.13 = (bf16[512,384]{1,0:T(8,128)(2,1)S(1)}, bf16[512,384]{1,0:T(8,128)(2,1)S(1)}, u32[]{:S(2)}, u32[]{:S(2)}) collective-permute-start(bf16[512,384]{1,0:T(8,128)(2,1)S(1)} %get-tuple-element.52), channel_id=1, source_target_pairs={{0,6},{1,7},{2,0},{3,1},{4,2},{5,3},{6,4},{7,5},{8,14},{9,15},{10,... | collective-permute-start | bytes 1179656 | tf_op jit(solution)/shard_map/ppermute | solution.py:37
  66.4 10.6 %collective-permute-start.10 = (bf16[256,384]{1,0:T(8,128)(2,1)S(1)}, bf16[256,384]{1,0:T(8,128)(2,1)S(1)}, u32[]{:S(2)}, u32[]{:S(2)}) collective-permute-start(bf16[256,384]{1,0:T(8,128)(2,1)S(1)} %get-tuple-element.57), channel_id=1, source_target_pairs={{0,2},{1,3},{2,4},{3,5},{4,6},{5,7},{6,0},{7,1},{8,10},{9,11},{10,... | collective-permute-start | bytes 589832 | tf_op jit(solution)/shard_map/ppermute | solution.py:37
  68.9 9.3 %collective-permute-start.11 = (bf16[256,384]{1,0:T(8,128)(2,1)S(1)}, bf16[256,384]{1,0:T(8,128)(2,1)S(1)}, u32[]{:S(2)}, u32[]{:S(2)}) collective-permute-start(bf16[256,384]{1,0:T(8,128)(2,1)S(1)} %get-tuple-element.58), channel_id=1, source_target_pairs={{0,6},{1,7},{2,0},{3,1},{4,2},{5,3},{6,4},{7,5},{8,14},{9,15},{10,... | collective-permute-start | bytes 589832 | tf_op jit(solution)/shard_map/ppermute | solution.py:37
  81.3 32.5 %collective-permute-start.19 = (bf16[1024,384]{1,0:T(8,128)(2,1)S(1)}, bf16[1024,384]{1,0:T(8,128)(2,1)S(1)}, u32[]{:S(2)}, u32[]{:S(2)}) collective-permute-start(bf16[1024,384]{1,0:T(8,128)(2,1)S(1)} %get-tuple-element.66), channel_id=1, source_target_pairs={{0,2},{1,3},{2,4},{3,5},{4,6},{5,7},{6,0},{7,1},{8,10},{9,11},{10,... | collective-permute-start | bytes 2359304 | tf_op jit(solution)/shard_map/ppermute | solution.py:37
  82.4 21.2 %copy-start.7 = (bf16[512,384]{1,0:T(8,128)(2,1)S(1)}, bf16[512,384]{1,0:T(8,128)(2,1)}, u32[]{:S(2)}) copy-start(bf16[512,384]{1,0:T(8,128)(2,1)} %copy-done.5) | copy-start | bytes 1179652
  82.4 31.5 %collective-permute-start.20 = (bf16[1024,384]{1,0:T(8,128)(2,1)S(1)}, bf16[1024,384]{1,0:T(8,128)(2,1)S(1)}, u32[]{:S(2)}, u32[]{:S(2)}) collective-permute-start(bf16[1024,384]{1,0:T(8,128)(2,1)S(1)} %get-tuple-element.67), channel_id=1, source_target_pairs={{0,6},{1,7},{2,0},{3,1},{4,2},{5,3},{6,4},{7,5},{8,14},{9,15},{10,... | collective-permute-start | bytes 2359304 | tf_op jit(solution)/shard_map/ppermute | solution.py:37
  85.1 11.0 %collective-permute-start.14 = (bf16[2,64,384]{2,1,0:T(8,128)(2,1)S(1)}, bf16[2,64,384]{2,1,0:T(8,128)(2,1)S(1)}, u32[]{:S(2)}, u32[]{:S(2)}) collective-permute-start(bf16[2,64,384]{2,1,0:T(8,128)(2,1)S(1)} %get-tuple-element.62), channel_id=1, source_target_pairs={{0,64},{1,65},{2,66},{3,67},{4,68},{5,69},{6,70},{7,71},{8,72},{9,... | collective-permute-start | bytes 294920 | tf_op jit(solution)/shard_map/ppermute | solution.py:37
  86.1 10.5 %collective-permute-start.15 = (bf16[2,64,384]{2,1,0:T(8,128)(2,1)S(1)}, bf16[2,64,384]{2,1,0:T(8,128)(2,1)S(1)}, u32[]{:S(2)}, u32[]{:S(2)}) collective-permute-start(bf16[2,64,384]{2,1,0:T(8,128)(2,1)S(1)} %get-tuple-element.63), channel_id=1, source_target_pairs={{0,128},{1,129},{2,130},{3,131},{4,132},{5,133},{6,134},{7,135},{8... | collective-permute-start | bytes 294920 | tf_op jit(solution)/shard_map/ppermute | solution.py:37
  89.0 10.4 %collective-permute-start.16 = (bf16[2,64,384]{2,1,0:T(8,128)(2,1)S(1)}, bf16[2,64,384]{2,1,0:T(8,128)(2,1)S(1)}, u32[]{:S(2)}, u32[]{:S(2)}) collective-permute-start(bf16[2,64,384]{2,1,0:T(8,128)(2,1)S(1)} %get-tuple-element.64), channel_id=1, source_target_pairs={{0,192},{1,193},{2,194},{3,195},{4,196},{5,197},{6,198},{7,199},{8... | collective-permute-start | bytes 294920 | tf_op jit(solution)/shard_map/ppermute | solution.py:37
  96.1 17.7 %collective-permute-start.21 = (bf16[512,384]{1,0:T(8,128)(2,1)S(1)}, bf16[512,384]{1,0:T(8,128)(2,1)S(1)}, u32[]{:S(2)}, u32[]{:S(2)}) collective-permute-start(bf16[512,384]{1,0:T(8,128)(2,1)S(1)} %get-tuple-element.69), channel_id=1, source_target_pairs={{0,2},{1,3},{2,4},{3,5},{4,6},{5,7},{6,0},{7,1},{8,10},{9,11},{10,... | collective-permute-start | bytes 1179656 | tf_op jit(solution)/shard_map/ppermute | solution.py:37
  96.6 17.2 %collective-permute-start.22 = (bf16[512,384]{1,0:T(8,128)(2,1)S(1)}, bf16[512,384]{1,0:T(8,128)(2,1)S(1)}, u32[]{:S(2)}, u32[]{:S(2)}) collective-permute-start(bf16[512,384]{1,0:T(8,128)(2,1)S(1)} %get-tuple-element.70), channel_id=1, source_target_pairs={{0,6},{1,7},{2,0},{3,1},{4,2},{5,3},{6,4},{7,5},{8,14},{9,15},{10,... | collective-permute-start | bytes 1179656 | tf_op jit(solution)/shard_map/ppermute | solution.py:37
  99.4 4.2 %collective-permute-start.17 = (bf16[64,384]{1,0:T(8,128)(2,1)S(1)}, bf16[64,384]{1,0:T(8,128)(2,1)S(1)}, u32[]{:S(2)}, u32[]{:S(2)}) collective-permute-start(bf16[64,384]{1,0:T(8,128)(2,1)S(1)} %get-tuple-element.72.down_own), channel_id=1, source_target_pairs={{0,1},{1,0},{2,3},{3,2},{4,5},{5,4},{6,7},{7,6},{8,9},{9,8},{10,11... | collective-permute-start | bytes 147464 | tf_op jit(solution)/shard_map/ppermute | solution.py:37
  103.6 19.6 %copy-start.11 = (s32[32]{0:T(128)S(1)}, s32[32]{0:T(128)}, u32[]{:S(2)}) copy-start(s32[32]{0:T(128)} %counts.5) | copy-start | bytes 388
  105.8 17.3 %copy-start.1 = (bf16[2,1024,384]{2,1,0:T(8,128)(2,1)S(1)}, bf16[2,1024,384]{2,1,0:T(8,128)(2,1)}, u32[]{:S(2)}) copy-start(bf16[2,1024,384]{2,1,0:T(8,128)(2,1)} %residual.5) | copy-start | bytes 4718596
  105.8 17.3 %copy-start.10 = (bf16[2,384]{1,0:T(2,128)(2,1)S(1)}, bf16[2,384]{1,0:T(2,128)(2,1)}, u32[]{:S(2)}) copy-start(bf16[2,384]{1,0:T(2,128)(2,1)} %gate.5) | copy-start | bytes 4612
  105.9 7.9 %collective-permute-start.18 = (bf16[64,2048]{1,0:T(8,128)(2,1)S(1)}, bf16[64,2048]{1,0:T(8,128)(2,1)S(1)}, u32[]{:S(2)}, u32[]{:S(2)}) collective-permute-start(bf16[64,2048]{1,0:T(8,128)(2,1)S(1)} %lowrank.1), channel_id=1, source_target_pairs={{0,2},{1,3},{2,0},{3,1},{4,6},{5,7},{6,4},{7,5},{8,10},{9,11},{10,... | collective-permute-start | bytes 786440 | tf_op jit(solution)/shard_map/ppermute | solution.py:37
  113.8 9.2 %collective-permute-start.23 = (bf16[64,2048]{1,0:T(8,128)(2,1)S(1)}, bf16[64,2048]{1,0:T(8,128)(2,1)S(1)}, u32[]{:S(2)}, u32[]{:S(2)}) collective-permute-start(bf16[64,2048]{1,0:T(8,128)(2,1)S(1)} %add.6), channel_id=1, source_target_pairs={{0,4},{1,5},{2,6},{3,7},{4,0},{5,1},{6,2},{7,3},{8,12},{9,13},{10,... | collective-permute-start | bytes 786440 | tf_op jit(solution)/shard_map/ppermute | solution.py:37

commit v3 on v2

--- a/solution.py
+++ b/solution.py
@@ -522,8 +522,8 @@
     down, up = settle(parts)
     order = (0, 2, 1)
     t = lowrank(down, send(down, swap_z), [own[i] for i in order], [other[i] for i in order])
-    t = after(t + send(t, pair_y(1)), *home1, *home2)
-    t = t + send(t, pair_y(2))
+    late = after(t, *home1, *home2)
+    t = t + send(t, to_y(1)) + send(t, to_y(-1)) + send(late, to_y(2))
 
     result = None
     for chunk, mine, theirs, gots in zip(chunks, own, other, (home0, home1, home2)):

time: 132 us -> 141 us (1.068)
  waiting for transfers between devices: 35.8 us -> 49.2 us
  starting transfers between devices: 43.9 us -> 39.6 us
    ppermute x24 -> x25, waiting for transfers between devices: 35.8 us -> 49.2 us  [send(): return lax.ppermute(array, ('rep', 'tp'), table(move))]
    ppermute x24 -> x25, starting transfers between devices: 43.9 us -> 39.6 us  [send(): return lax.ppermute(array, ('rep', 'tp'), table(move))]
  transfers between devices with their start and end apart: 24 -> 25, of which waited for: 11 -> 12; matrix products, arithmetic and copies ran while one was open for 0% -> 0% of each run, Pallas kernels for 24% -> 23%
where the time goes in v3:
time: 141 us; the launch traced here: 140 us
  waiting for transfers between devices  49.2 us (35%)
  Pallas kernels  48.1 us (34%)
  starting transfers between devices  39.6 us (28%)
  local copies, waits for them, and re-layouts  2.89 us (2%)
    ppermute x25, waiting for transfers between devices, send(): return lax.ppermute(array, ('rep', 'tp'), table(move))  49.2 us
    ppermute x25, starting transfers between devices, send(): return lax.ppermute(array, ('rep', 'tp'), table(move))  39.6 us
    pallas_call x3, Pallas kernels, attend(): pl.pallas_call(attend_kernel, grid=(width // HD,), in_specs=[pl.BlockSpec...  17.2 us
    pallas_call x3, Pallas kernels, home(): pl.pallas_call(functools.partial(home_kernel, b, len(gots)), grid_spec=pl...  7.81 us
    pallas_call x2, Pallas kernels, near(): pl.pallas_call(functools.partial(near_kernel, places), grid_spec=pltpu.Pr...  4.43 us
    pallas_call x2, Pallas kernels, far(): pl.pallas_call(far_kernel, grid_spec=pltpu.PrefetchScalarGridSpec(num_sca...  3.78 us
    pallas_call x1, Pallas kernels, keep(): pl.pallas_call(keep_kernel, in_specs=[smem] * 3 + [vmem] * 3, out_specs=[...  3.3 us
    pallas_call x1, Pallas kernels, cut(): pl.pallas_call(cut_kernel, grid_spec=pltpu.PrefetchScalarGridSpec(num_sca...  3.04 us
  transfers between devices with their start and end apart: 25, of which 12 were waited for; matrix products, arithmetic and copies ran while one was open for 0% of the time, Pallas kernels for 23%

profile of v3, /device:TPU:32, one launch (start us, length us, event | category | flops | bytes accessed | tf_op | source)
XLA Modules:
  0.0 140.2 jit_solution(4443771887238327254)
XLA Ops:
  0.0 0.7 stack.35.info.marks
  0.7 3.0 %cut.1 = bf16[384,1536]{1,0:T(8,128)(2,1)} custom-call(s32[8]{0:T(128)} %stack.35.info.marks, bf16[384,3072]{1,0:T(8,128)(2,1)} %w_own.9, bf16[384,3072]{1,0:T(8,128)(2,1)} %w_own.9, bf16[384,3072]{1,0:T(8,128)(2,1)} %w_own.9, bf16[384,3072]{1,0:T(8,128)(2,1)} %w_own.9), custom_call_target="tpu_custom_call" | custom-call | bytes 2359296 | tf_op jit(solution)/shard_map/cut/pallas_call | solution.py:410
  3.7 2.7 %choose.1 = bf16[16,2,64,384]{3,2,1,0:T(8,128)(2,1)} custom-call(s32[8]{0:T(128)} %stack.35.info.marks, s32[32]{0:T(128)} %ids.3, s32[128]{0:T(128)} %slots.3, bf16[4,64,384]{2,1,0:T(8,128)(2,1)} %bitcast.18, bf16[4,64,384]{2,1,0:T(8,128)(2,1)} %up.3), custom_call_target="tpu_custom_call" | custom-call | bytes 1572864 | tf_op jit(solution)/shard_map/choose/pallas_call | solution.py:293
  6.4 1.9 %collective-permute-start.3 = (bf16[384,1536]{1,0:T(8,128)(2,1)}, bf16[384,1536]{1,0:T(8,128)(2,1)S(1)}, u32[]{:S(2)}, u32[]{:S(2)}) collective-permute-start(bf16[384,1536]{1,0:T(8,128)(2,1)} %cut.1), channel_id=1, source_target_pairs={{0,193},{1,64},{2,195},{3,66},{4,197},{5,68},{6,199},{7,70},{8,201... | collective-permute-start | bytes 3538952 | tf_op jit(solution)/shard_map/ppermute | solution.py:37
  8.3 5.2 %attend.3.own.refs_0_ = bf16[512,384]{1,0:T(8,128)(2,1)} custom-call(bf16[2,1024,384]{2,1,0:T(8,128)(2,1)} %q_ref.2, bf16[2,1024,384]{2,1,0:T(8,128)(2,1)} %k_ref.5, bf16[2,1024,384]{2,1,0:T(8,128)(2,1)} %v_ref.5), custom_call_target="tpu_custom_call" | custom-call | flops 805306368 | bytes 2359296 | tf_op jit(solution)/shard_map/attend/pallas_call | solution.py:100
  13.5 4.0 %collective-permute-start = (bf16[512,384]{1,0:T(8,128)(2,1)}, bf16[512,384]{1,0:T(8,128)(2,1)S(1)}, u32[]{:S(2)}, u32[]{:S(2)}) collective-permute-start(bf16[512,384]{1,0:T(8,128)(2,1)} %attend.3.own.refs_0_), channel_id=1, source_target_pairs={{0,1},{1,0},{2,3},{3,2},{4,5},{5,4},{6,7},{7,6},{8,9},{9,8},{10,11... | collective-permute-start | bytes 1179656 | tf_op jit(solution)/shard_map/ppermute | solution.py:37
  17.5 6.9 %attend.4.own.refs_2_ = bf16[1024,384]{1,0:T(8,128)(2,1)} custom-call(bf16[2,1024,384]{2,1,0:T(8,128)(2,1)} %q_ref.2, bf16[2,1024,384]{2,1,0:T(8,128)(2,1)} %k_ref.5, bf16[2,1024,384]{2,1,0:T(8,128)(2,1)} %v_ref.5), custom_call_target="tpu_custom_call" | custom-call | flops 1610612736 | bytes 3145728 | tf_op jit(solution)/shard_map/attend/pallas_call | solution.py:100
  24.4 0.0 collective-permute-start.4
  24.4 2.9 %collective-permute-done.other.refs_3_ = bf16[512,384]{1,0:T(8,128)(2,1)S(1)} collective-permute-done((bf16[512,384]{1,0:T(8,128)(2,1)}, bf16[512,384]{1,0:T(8,128)(2,1)S(1)}, u32[]{:S(2)}, u32[]{:S(2)}) %collective-permute-start) | collective-permute-done | bytes 393248 | tf_op jit(solution)/shard_map/ppermute | solution.py:37
  27.3 1.2 copy-done.12
  28.5 3.3 %keep.1 = (bf16[4,2,2,64,384]{4,3,2,1,0:T(8,128)(2,1)}, bf16[4,2,2,64,384]{4,3,2,1,0:T(8,128)(2,1)}) custom-call(s32[8]{0:T(128)} %stack.35.info.marks, s32[32]{0:T(128)} %ids.3, s32[128]{0:T(128)} %slots.3, bf16[4,64,384]{2,1,0:T(8,128)(2,1)} %bitcast.19, bf16[4,64,384]{2,1,0:T(8,128)(2,1)} %up.3, bf16[16,2,64,384]{3,2,1,0:T(8,128)(2,1)} %copy-done.12), custom_call_target="tpu_custom_call" | custom-call | bytes 3145728 | tf_op jit(solution)/shard_map/keep/pallas_call | solution.py:325
  31.8 3.1 %collective-permute-start.5 = (bf16[4,2,2,64,384]{4,3,2,1,0:T(8,128)(2,1)}, bf16[4,2,2,64,384]{4,3,2,1,0:T(8,128)(2,1)}, u32[]{:S(2)}, u32[]{:S(2)}) collective-permute-start(bf16[4,2,2,64,384]{4,3,2,1,0:T(8,128)(2,1)} %get-tuple-element.44), channel_id=1, source_target_pairs={{0,32},{1,33},{2,34},{3,35},{4,36},{5,37},{6,38},{7,39},{8,40},{9,... | collective-permute-start | bytes 2359304 | tf_op jit(solution)/shard_map/ppermute | solution.py:37
  34.9 5.1 %attend.5.own.refs_1_ = bf16[512,384]{1,0:T(8,128)(2,1)} custom-call(bf16[2,1024,384]{2,1,0:T(8,128)(2,1)} %q_ref.2, bf16[2,1024,384]{2,1,0:T(8,128)(2,1)} %k_ref.5, bf16[2,1024,384]{2,1,0:T(8,128)(2,1)} %v_ref.5), custom_call_target="tpu_custom_call" | custom-call | flops 805306368 | bytes 2359296 | tf_op jit(solution)/shard_map/attend/pallas_call | solution.py:100
  40.1 2.4 %collective-permute-start.2 = (bf16[512,384]{1,0:T(8,128)(2,1)}, bf16[512,384]{1,0:T(8,128)(2,1)S(1)}, u32[]{:S(2)}, u32[]{:S(2)}) collective-permute-start(bf16[512,384]{1,0:T(8,128)(2,1)} %attend.5.own.refs_1_), channel_id=1, source_target_pairs={{0,1},{1,0},{2,3},{3,2},{4,5},{5,4},{6,7},{7,6},{8,9},{9,8},{10,11... | collective-permute-start | bytes 1179656 | tf_op jit(solution)/shard_map/ppermute | solution.py:37
  42.5 1.0 copy-done.6
  43.5 1.8 %spread.1 = (bf16[512,384]{1,0:T(8,128)(2,1)S(1)}, bf16[512,384]{1,0:T(8,128)(2,1)S(1)}, bf16[512,384]{1,0:T(8,128)(2,1)S(1)}) custom-call(s32[8]{0:T(128)S(1)} %copy-done.9, bf16[512,384]{1,0:T(8,128)(2,1)S(1)} %copy-done.4, bf16[512,384]{1,0:T(8,128)(2,1)S(1)} %copy-done.6, bf16[384,3072]{1,0:T(8,128)(2,1)S(1)} %copy-done, bf16[384,3072]{1,0:T(8,128)(2,1)S(1)} %copy-done, ...), custom_call_target="tpu_custom_call" | custom-call | flops 905969664 | bytes 1966080 | tf_op jit(solution)/shard_map/spread/pallas_call | solution.py:438
  45.3 3.3 %collective-permute-start.7 = (bf16[512,384]{1,0:T(8,128)(2,1)S(1)}, bf16[512,384]{1,0:T(8,128)(2,1)S(1)}, u32[]{:S(2)}, u32[]{:S(2)}) collective-permute-start(bf16[512,384]{1,0:T(8,128)(2,1)S(1)} %get-tuple-element.47), channel_id=1, source_target_pairs={{0,4},{1,5},{2,6},{3,7},{4,0},{5,1},{6,2},{7,3},{8,12},{9,13},{10,... | collective-permute-start | bytes 1179656 | tf_op jit(solution)/shard_map/ppermute | solution.py:37
  48.5 0.7 collective-permute-start.8
  49.2 0.0 collective-permute-done.4.other.refs_5_
  49.2 2.6 %far.2 = (bf16[512,384]{1,0:T(8,128)(2,1)S(1)}, bf16[512,384]{1,0:T(8,128)(2,1)S(1)}) custom-call(s32[8]{0:T(128)S(1)} %copy-done.9, bf16[1024,384]{1,0:T(8,128)(2,1)S(1)} %copy-done.2, bf16[1024,384]{1,0:T(8,128)(2,1)} %collective-permute-done.4.other.refs_5_, bf16[384,3072]{1,0:T(8,128)(2,1)S(1)} %copy-done, ...), custom_call_target="tpu_custom_call" | custom-call | flops 603979776 | bytes 2359296 | tf_op jit(solution)/shard_map/far/pallas_call | solution.py:137
  51.9 0.0 copy-start.3
  51.9 0.9 collective-permute-done.5
  52.8 1.3 merge.1
  54.1 1.6 %collective-permute-start.6 = (bf16[4,1,2,64,384]{4,3,2,0,1:T(8,128)(2,1)S(1)}, bf16[4,1,2,64,384]{4,3,2,0,1:T(8,128)(2,1)S(1)}, u32[]{:S(2)}, u32[]{:S(2)}) collective-permute-start(bf16[4,1,2,64,384]{4,3,2,0,1:T(8,128)(2,1)S(1)} %bitcast.17), channel_id=1, source_target_pairs={{0,16},{1,17},{2,18},{3,19},{4,20},{5,21},{6,22},{7,23},{8,24},{9,... | collective-permute-start | bytes 1179656 | tf_op jit(solution)/shard_map/ppermute | solution.py:37
  55.7 3.0 %collective-permute-start.9 = (bf16[512,384]{1,0:T(8,128)(2,1)S(1)}, bf16[512,384]{1,0:T(8,128)(2,1)S(1)}, u32[]{:S(2)}, u32[]{:S(2)}) collective-permute-start(bf16[512,384]{1,0:T(8,128)(2,1)S(1)} %get-tuple-element.49), channel_id=1, source_target_pairs={{0,6},{1,7},{2,0},{3,1},{4,2},{5,3},{6,4},{7,5},{8,14},{9,15},{10,... | collective-permute-start | bytes 1179656 | tf_op jit(solution)/shard_map/ppermute | solution.py:37
  58.7 0.0 collective-permute-done.2.other.refs_4_
  58.7 0.0 collective-permute-start.12
  58.7 0.3 collective-permute-done.7.rest_0_
  58.9 3.0 %collective-permute-start.13 = (bf16[512,384]{1,0:T(8,128)(2,1)S(1)}, bf16[512,384]{1,0:T(8,128)(2,1)S(1)}, u32[]{:S(2)}, u32[]{:S(2)}) collective-permute-start(bf16[512,384]{1,0:T(8,128)(2,1)S(1)} %get-tuple-element.52), channel_id=1, source_target_pairs={{0,6},{1,7},{2,0},{3,1},{4,2},{5,3},{6,4},{7,5},{8,14},{9,15},{10,... | collective-permute-start | bytes 1179656 | tf_op jit(solution)/shard_map/ppermute | solution.py:37
  61.9 1.1 far.3
  63.0 3.5 %collective-permute-done.8.rest_1_ = bf16[512,384]{1,0:T(8,128)(2,1)S(1)} collective-permute-done((bf16[512,384]{1,0:T(8,128)(2,1)S(1)}, bf16[512,384]{1,0:T(8,128)(2,1)S(1)}, u32[]{:S(2)}, u32[]{:S(2)}) %collective-permute-start.8) | collective-permute-done | bytes 393248 | tf_op jit(solution)/shard_map/ppermute | solution.py:37
  66.5 2.5 %collective-permute-start.10 = (bf16[256,384]{1,0:T(8,128)(2,1)S(1)}, bf16[256,384]{1,0:T(8,128)(2,1)S(1)}, u32[]{:S(2)}, u32[]{:S(2)}) collective-permute-start(bf16[256,384]{1,0:T(8,128)(2,1)S(1)} %get-tuple-element.57), channel_id=1, source_target_pairs={{0,2},{1,3},{2,4},{3,5},{4,6},{5,7},{6,0},{7,1},{8,10},{9,11},{10,... | collective-permute-start | bytes 589832 | tf_op jit(solution)/shard_map/ppermute | solution.py:37
  69.0 0.0 collective-permute-done.6
  69.0 0.8 collective-permute-start.11
  69.8 0.6 fan.1
  70.4 0.0 collective-permute-done.9.rest_2_
  70.4 6.7 %collective-permute-done.10.refs_0_ = bf16[256,384]{1,0:T(8,128)(2,1)S(1)} collective-permute-done((bf16[256,384]{1,0:T(8,128)(2,1)S(1)}, bf16[256,384]{1,0:T(8,128)(2,1)S(1)}, u32[]{:S(2)}, u32[]{:S(2)}) %collective-permute-start.10) | collective-permute-done | bytes 196640 | tf_op jit(solution)/shard_map/ppermute | solution.py:37
  77.1 1.2 collective-permute-done.11.refs_1_
  78.3 3.1 %near.2 = (bf16[1024,384]{1,0:T(8,128)(2,1)S(1)}, bf16[1024,384]{1,0:T(8,128)(2,1)S(1)}) custom-call(s32[8]{0:T(128)S(1)} %copy-done.9, bf16[1024,384]{1,0:T(8,128)(2,1)S(1)} %copy-done.2, bf16[1024,384]{1,0:T(8,128)(2,1)} %collective-permute-done.4.other.refs_5_, bf16[384,3072]{1,0:T(8,128)(2,1)S(1)} %copy-done, bf16[384,3072]{1,0:T(8,128)(2,1)S(1)} %copy-done, ...), custom_call_target="tpu_custom_call" | custom-call | flops 1207959552 | bytes 3932160 | tf_op jit(solution)/shard_map/near/pallas_call | solution.py:176
  81.4 1.1 collective-permute-start.20
  82.5 2.7 %collective-permute-start.21 = (bf16[1024,384]{1,0:T(8,128)(2,1)S(1)}, bf16[1024,384]{1,0:T(8,128)(2,1)S(1)}, u32[]{:S(2)}, u32[]{:S(2)}) collective-permute-start(bf16[1024,384]{1,0:T(8,128)(2,1)S(1)} %get-tuple-element.67), channel_id=1, source_target_pairs={{0,6},{1,7},{2,0},{3,1},{4,2},{5,3},{6,4},{7,5},{8,14},{9,15},{10,... | collective-permute-start | bytes 2359304 | tf_op jit(solution)/shard_map/ppermute | solution.py:37
  85.2 1.4 near.3
  86.6 0.1 collective-permute-start.22
  86.7 3.2 %collective-permute-start.23 = (bf16[512,384]{1,0:T(8,128)(2,1)S(1)}, bf16[512,384]{1,0:T(8,128)(2,1)S(1)}, u32[]{:S(2)}, u32[]{:S(2)}) collective-permute-start(bf16[512,384]{1,0:T(8,128)(2,1)S(1)} %get-tuple-element.70), channel_id=1, source_target_pairs={{0,6},{1,7},{2,0},{3,1},{4,2},{5,3},{6,4},{7,5},{8,14},{9,15},{10,... | collective-permute-start | bytes 1179656 | tf_op jit(solution)/shard_map/ppermute | solution.py:37
  89.9 0.9 collective-permute-start.14
  90.9 6.8 %collective-permute-done.14.b = bf16[2,64,384]{2,1,0:T(8,128)(2,1)S(1)} collective-permute-done((bf16[2,64,384]{2,1,0:T(8,128)(2,1)S(1)}, bf16[2,64,384]{2,1,0:T(8,128)(2,1)S(1)}, u32[]{:S(2)}, u32[]{:S(2)}) %collective-permute-start.14) | collective-permute-done | bytes 98336 | tf_op jit(solution)/shard_map/ppermute | solution.py:37
  97.7 0.9 collective-permute-start.15
  98.7 7.8 %collective-permute-done.15.c = bf16[2,64,384]{2,1,0:T(8,128)(2,1)S(1)} collective-permute-done((bf16[2,64,384]{2,1,0:T(8,128)(2,1)S(1)}, bf16[2,64,384]{2,1,0:T(8,128)(2,1)S(1)}, u32[]{:S(2)}, u32[]{:S(2)}) %collective-permute-start.15) | collective-permute-done | bytes 98336 | tf_op jit(solution)/shard_map/ppermute | solution.py:37
  106.4 0.2 collective-permute-start.16
  106.6 6.4 %collective-permute-done.16.d = bf16[2,64,384]{2,1,0:T(8,128)(2,1)S(1)} collective-permute-done((bf16[2,64,384]{2,1,0:T(8,128)(2,1)S(1)}, bf16[2,64,384]{2,1,0:T(8,128)(2,1)S(1)}, u32[]{:S(2)}, u32[]{:S(2)}) %collective-permute-start.16) | collective-permute-done | bytes 98336 | tf_op jit(solution)/shard_map/ppermute | solution.py:37
  113.0 0.0 copy-start.1
  113.0 0.0 copy-start.10
  113.1 0.0 copy-start.11
  113.1 0.1 collective-permute-start.17
  113.2 4.0 %collective-permute-done.17.down_other = bf16[64,384]{1,0:T(8,128)(2,1)S(1)} collective-permute-done((bf16[64,384]{1,0:T(8,128)(2,1)S(1)}, bf16[64,384]{1,0:T(8,128)(2,1)S(1)}, u32[]{:S(2)}, u32[]{:S(2)}) %collective-permute-start.17) | collective-permute-done | bytes 49184 | tf_op jit(solution)/shard_map/ppermute | solution.py:37
  117.2 2.2 %lowrank.1 = bf16[64,2048]{1,0:T(8,128)(2,1)S(1)} custom-call(bf16[64,384]{1,0:T(8,128)(2,1)S(1)} %get-tuple-element.72.down_own, bf16[64,384]{1,0:T(8,128)(2,1)S(1)} %collective-permute-done.17.down_other, bf16[512,384]{1,0:T(8,128)(2,1)S(1)} %copy-done.4, bf16[512,384]{1,0:T(8,128)(2,1)S(1)} %copy-done.3, bf16[1024,384]{1,0:T(8,128)(2,1)S(1)} %copy-done.2, ...), custom_call_target="tpu_custom_call" | custom-call | flops 201326592 | bytes 3145728 | tf_op jit(solution)/shard_map/lowrank/pallas_call | solution.py:215
  119.5 2.4 %collective-permute-start.19 = (bf16[64,2048]{1,0:T(8,128)(2,1)S(1)}, bf16[64,2048]{1,0:T(8,128)(2,1)S(1)}, u32[]{:S(2)}, u32[]{:S(2)}) collective-permute-start(bf16[64,2048]{1,0:T(8,128)(2,1)S(1)} %lowrank.1), channel_id=1, source_target_pairs={{0,6},{1,7},{2,0},{3,1},{4,2},{5,3},{6,4},{7,5},{8,14},{9,15},{10,... | collective-permute-start | bytes 786440 | tf_op jit(solution)/shard_map/ppermute | solution.py:37
  121.9 1.6 %collective-permute-start.24 = (bf16[64,2048]{1,0:T(8,128)(2,1)S(1)}, bf16[64,2048]{1,0:T(8,128)(2,1)S(1)}, u32[]{:S(2)}, u32[]{:S(2)}) collective-permute-start(bf16[64,2048]{1,0:T(8,128)(2,1)S(1)} %lowrank.1), channel_id=1, source_target_pairs={{0,4},{1,5},{2,6},{3,7},{4,0},{5,1},{6,2},{7,3},{8,12},{9,13},{10,... | collective-permute-start | bytes 786440 | tf_op jit(solution)/shard_map/ppermute | solution.py:37
  123.5 2.4 %collective-permute-done.19 = bf16[64,2048]{1,0:T(8,128)(2,1)S(1)} collective-permute-done((bf16[64,2048]{1,0:T(8,128)(2,1)S(1)}, bf16[64,2048]{1,0:T(8,128)(2,1)S(1)}, u32[]{:S(2)}, u32[]{:S(2)}) %collective-permute-start.19) | collective-permute-done | bytes 262176 | tf_op jit(solution)/shard_map/ppermute | solution.py:37
  125.9 6.3 %collective-permute-done.18 = bf16[64,2048]{1,0:T(8,128)(2,1)S(1)} collective-permute-done((bf16[64,2048]{1,0:T(8,128)(2,1)S(1)}, bf16[64,2048]{1,0:T(8,128)(2,1)S(1)}, u32[]{:S(2)}, u32[]{:S(2)}) %collective-permute-start.18) | collective-permute-done | bytes 262176 | tf_op jit(solution)/shard_map/ppermute | solution.py:37
  132.3 0.1 add_add_fusion.t
  132.4 2.0 %home.3.rest_2_ = bf16[2,1024,384]{2,1,0:T(8,128)(2,1)} custom-call(s32[8]{0:T(128)S(1)} %copy-done.9, s32[32]{0:T(128)S(1)} %copy-done.11, bf16[512,384]{1,0:T(8,128)(2,1)S(1)} %copy-done.4, bf16[512,384]{1,0:T(8,128)(2,1)S(1)} %copy-done.7, bf16[384,3072]{1,0:T(8,128)(2,1)S(1)} %copy-done, ...), custom_call_target="tpu_custom_call" | custom-call | flops 301989888 | bytes 2359296 | tf_op jit(solution)/shard_map/home/pallas_call | solution.py:244
  134.4 3.8 %home.4.rest_2_ = bf16[2,1024,384]{2,1,0:T(8,128)(2,1)} custom-call(s32[8]{0:T(128)S(1)} %copy-done.9, s32[32]{0:T(128)S(1)} %copy-done.11, bf16[1024,384]{1,0:T(8,128)(2,1)S(1)} %copy-done.2, bf16[1024,384]{1,0:T(8,128)(2,1)} %collective-permute-done.4.other.refs_5_, bf16[384,3072]{1,0:T(8,128)(2,1)S(1)} %copy-done, ...), custom_call_target="tpu_custom_call", output_to_operand_aliasing={{}: (12, {})} | custom-call | flops 603979776 | bytes 4718592 | tf_op jit(solution)/shard_map/home/pallas_call | solution.py:244
  138.2 2.0 %home.5 = bf16[2,1024,384]{2,1,0:T(8,128)(2,1)} custom-call(s32[8]{0:T(128)S(1)} %copy-done.9, s32[32]{0:T(128)S(1)} %copy-done.11, bf16[512,384]{1,0:T(8,128)(2,1)S(1)} %copy-done.3, bf16[512,384]{1,0:T(8,128)(2,1)S(1)} %collective-permute-done.2.other.refs_4_, bf16[384,3072]{1,0:T(8,128)(2,1)S(1)} %copy-done, ...), custom_call_target="tpu_custom_call", output_to_operand_aliasing={{}: (12, {})} | custom-call | flops 301989888 | bytes 2359296 | tf_op jit(solution)/shard_map/home/pallas_call | solution.py:244
  (32 shorter events, 0.1 us)
Async XLA Ops:
  6.4 20.9 %collective-permute-start.1 = (bf16[16,2,64,384]{3,2,1,0:T(8,128)(2,1)}, bf16[16,2,64,384]{3,2,1,0:T(8,128)(2,1)S(1)}, u32[]{:S(2)}, u32[]{:S(2)}) collective-permute-start(bf16[16,2,64,384]{3,2,1,0:T(8,128)(2,1)} %choose.1), channel_id=1, source_target_pairs={{0,8},{1,9},{2,10},{3,11},{4,12},{5,13},{6,14},{7,15},{8,0},{9,1},... | collective-permute-start | bytes 4718600 | tf_op jit(solution)/shard_map/ppermute | solution.py:37
  6.4 36.1 %collective-permute-start.3 = (bf16[384,1536]{1,0:T(8,128)(2,1)}, bf16[384,1536]{1,0:T(8,128)(2,1)S(1)}, u32[]{:S(2)}, u32[]{:S(2)}) collective-permute-start(bf16[384,1536]{1,0:T(8,128)(2,1)} %cut.1), channel_id=1, source_target_pairs={{0,193},{1,64},{2,195},{3,66},{4,197},{5,68},{6,199},{7,70},{8,201... | collective-permute-start | bytes 3538952 | tf_op jit(solution)/shard_map/ppermute | solution.py:37
  13.5 13.8 %collective-permute-start = (bf16[512,384]{1,0:T(8,128)(2,1)}, bf16[512,384]{1,0:T(8,128)(2,1)S(1)}, u32[]{:S(2)}, u32[]{:S(2)}) collective-permute-start(bf16[512,384]{1,0:T(8,128)(2,1)} %attend.3.own.refs_0_), channel_id=1, source_target_pairs={{0,1},{1,0},{2,3},{3,2},{4,5},{5,4},{6,7},{7,6},{8,9},{9,8},{10,11... | collective-permute-start | bytes 1179656 | tf_op jit(solution)/shard_map/ppermute | solution.py:37
  24.4 24.8 %collective-permute-start.4 = (bf16[1024,384]{1,0:T(8,128)(2,1)}, bf16[1024,384]{1,0:T(8,128)(2,1)}, u32[]{:S(2)}, u32[]{:S(2)}) collective-permute-start(bf16[1024,384]{1,0:T(8,128)(2,1)} %attend.4.own.refs_2_), channel_id=1, source_target_pairs={{0,1},{1,0},{2,3},{3,2},{4,5},{5,4},{6,7},{7,6},{8,9},{9,8},{10,11... | collective-permute-start | bytes 2359304 | tf_op jit(solution)/shard_map/ppermute | solution.py:37
  27.3 4.5 %copy-start.5 = (bf16[512,384]{1,0:T(8,128)(2,1)}, bf16[512,384]{1,0:T(8,128)(2,1)S(1)}, u32[]{:S(2)}) copy-start(bf16[512,384]{1,0:T(8,128)(2,1)S(1)} %collective-permute-done.other.refs_3_) | copy-start | bytes 1179652
  27.3 1.2 copy-start.12
  31.8 10.7 %copy-start = (bf16[384,3072]{1,0:T(8,128)(2,1)S(1)}, bf16[384,3072]{1,0:T(8,128)(2,1)}, u32[]{:S(2)}) copy-start(bf16[384,3072]{1,0:T(8,128)(2,1)} %w_own.9) | copy-start | bytes 7077892
  31.8 10.7 %copy-start.4 = (bf16[512,384]{1,0:T(8,128)(2,1)S(1)}, bf16[512,384]{1,0:T(8,128)(2,1)}, u32[]{:S(2)}) copy-start(bf16[512,384]{1,0:T(8,128)(2,1)} %attend.3.own.refs_0_) | copy-start | bytes 1179652
  31.8 10.7 %copy-start.9 = (s32[8]{0:T(128)S(1)}, s32[8]{0:T(128)}, u32[]{:S(2)}) copy-start(s32[8]{0:T(128)} %stack.35.info.marks) | copy-start | bytes 100
  31.8 21.0 %collective-permute-start.5 = (bf16[4,2,2,64,384]{4,3,2,1,0:T(8,128)(2,1)}, bf16[4,2,2,64,384]{4,3,2,1,0:T(8,128)(2,1)}, u32[]{:S(2)}, u32[]{:S(2)}) collective-permute-start(bf16[4,2,2,64,384]{4,3,2,1,0:T(8,128)(2,1)} %get-tuple-element.44), channel_id=1, source_target_pairs={{0,32},{1,33},{2,34},{3,35},{4,36},{5,37},{6,38},{7,39},{8,40},{9,... | collective-permute-start | bytes 2359304 | tf_op jit(solution)/shard_map/ppermute | solution.py:37
  40.1 9.2 %copy-start.2 = (bf16[1024,384]{1,0:T(8,128)(2,1)S(1)}, bf16[1024,384]{1,0:T(8,128)(2,1)}, u32[]{:S(2)}) copy-start(bf16[1024,384]{1,0:T(8,128)(2,1)} %attend.4.own.refs_2_) | copy-start | bytes 2359300
  40.1 18.6 %collective-permute-start.2 = (bf16[512,384]{1,0:T(8,128)(2,1)}, bf16[512,384]{1,0:T(8,128)(2,1)S(1)}, u32[]{:S(2)}, u32[]{:S(2)}) collective-permute-start(bf16[512,384]{1,0:T(8,128)(2,1)} %attend.5.own.refs_1_), channel_id=1, source_target_pairs={{0,1},{1,0},{2,3},{3,2},{4,5},{5,4},{6,7},{7,6},{8,9},{9,8},{10,11... | collective-permute-start | bytes 1179656 | tf_op jit(solution)/shard_map/ppermute | solution.py:37
  42.5 1.0 copy-start.6
  45.3 13.7 %collective-permute-start.7 = (bf16[512,384]{1,0:T(8,128)(2,1)S(1)}, bf16[512,384]{1,0:T(8,128)(2,1)S(1)}, u32[]{:S(2)}, u32[]{:S(2)}) collective-permute-start(bf16[512,384]{1,0:T(8,128)(2,1)S(1)} %get-tuple-element.47), channel_id=1, source_target_pairs={{0,4},{1,5},{2,6},{3,7},{4,0},{5,1},{6,2},{7,3},{8,12},{9,13},{10,... | collective-permute-start | bytes 1179656 | tf_op jit(solution)/shard_map/ppermute | solution.py:37
  48.5 18.0 %collective-permute-start.8 = (bf16[512,384]{1,0:T(8,128)(2,1)S(1)}, bf16[512,384]{1,0:T(8,128)(2,1)S(1)}, u32[]{:S(2)}, u32[]{:S(2)}) collective-permute-start(bf16[512,384]{1,0:T(8,128)(2,1)S(1)} %get-tuple-element.48), channel_id=1, source_target_pairs={{0,2},{1,3},{2,4},{3,5},{4,6},{5,7},{6,0},{7,1},{8,10},{9,11},{10,... | collective-permute-start | bytes 1179656 | tf_op jit(solution)/shard_map/ppermute | solution.py:37
  49.2 3.6 %copy-start.8 = (bf16[4,2,2,64,384]{4,3,2,1,0:T(8,128)(2,1)S(1)}, bf16[4,2,2,64,384]{4,3,2,1,0:T(8,128)(2,1)}, u32[]{:S(2)}) copy-start(bf16[4,2,2,64,384]{4,3,2,1,0:T(8,128)(2,1)} %get-tuple-element.54) | copy-start | bytes 2359300
  51.9 10.0 %copy-start.3 = (bf16[512,384]{1,0:T(8,128)(2,1)S(1)}, bf16[512,384]{1,0:T(8,128)(2,1)}, u32[]{:S(2)}) copy-start(bf16[512,384]{1,0:T(8,128)(2,1)} %attend.5.own.refs_1_) | copy-start | bytes 1179652
  54.1 14.9 %collective-permute-start.6 = (bf16[4,1,2,64,384]{4,3,2,0,1:T(8,128)(2,1)S(1)}, bf16[4,1,2,64,384]{4,3,2,0,1:T(8,128)(2,1)S(1)}, u32[]{:S(2)}, u32[]{:S(2)}) collective-permute-start(bf16[4,1,2,64,384]{4,3,2,0,1:T(8,128)(2,1)S(1)} %bitcast.17), channel_id=1, source_target_pairs={{0,16},{1,17},{2,18},{3,19},{4,20},{5,21},{6,22},{7,23},{8,24},{9,... | collective-permute-start | bytes 1179656 | tf_op jit(solution)/shard_map/ppermute | solution.py:37
  55.7 14.7 %collective-permute-start.9 = (bf16[512,384]{1,0:T(8,128)(2,1)S(1)}, bf16[512,384]{1,0:T(8,128)(2,1)S(1)}, u32[]{:S(2)}, u32[]{:S(2)}) collective-permute-start(bf16[512,384]{1,0:T(8,128)(2,1)S(1)} %get-tuple-element.49), channel_id=1, source_target_pairs={{0,6},{1,7},{2,0},{3,1},{4,2},{5,3},{6,4},{7,5},{8,14},{9,15},{10,... | collective-permute-start | bytes 1179656 | tf_op jit(solution)/shard_map/ppermute | solution.py:37
  58.7 19.6 %collective-permute-start.12 = (bf16[512,384]{1,0:T(8,128)(2,1)S(1)}, bf16[512,384]{1,0:T(8,128)(2,1)S(1)}, u32[]{:S(2)}, u32[]{:S(2)}) collective-permute-start(bf16[512,384]{1,0:T(8,128)(2,1)S(1)} %get-tuple-element.51), channel_id=1, source_target_pairs={{0,2},{1,3},{2,4},{3,5},{4,6},{5,7},{6,0},{7,1},{8,10},{9,11},{10,... | collective-permute-start | bytes 1179656 | tf_op jit(solution)/shard_map/ppermute | solution.py:37
  58.9 19.4 %collective-permute-start.13 = (bf16[512,384]{1,0:T(8,128)(2,1)S(1)}, bf16[512,384]{1,0:T(8,128)(2,1)S(1)}, u32[]{:S(2)}, u32[]{:S(2)}) collective-permute-start(bf16[512,384]{1,0:T(8,128)(2,1)S(1)} %get-tuple-element.52), channel_id=1, source_target_pairs={{0,6},{1,7},{2,0},{3,1},{4,2},{5,3},{6,4},{7,5},{8,14},{9,15},{10,... | collective-permute-start | bytes 1179656 | tf_op jit(solution)/shard_map/ppermute | solution.py:37
  66.5 10.5 %collective-permute-start.10 = (bf16[256,384]{1,0:T(8,128)(2,1)S(1)}, bf16[256,384]{1,0:T(8,128)(2,1)S(1)}, u32[]{:S(2)}, u32[]{:S(2)}) collective-permute-start(bf16[256,384]{1,0:T(8,128)(2,1)S(1)} %get-tuple-element.57), channel_id=1, source_target_pairs={{0,2},{1,3},{2,4},{3,5},{4,6},{5,7},{6,0},{7,1},{8,10},{9,11},{10,... | collective-permute-start | bytes 589832 | tf_op jit(solution)/shard_map/ppermute | solution.py:37
  69.0 9.3 %collective-permute-start.11 = (bf16[256,384]{1,0:T(8,128)(2,1)S(1)}, bf16[256,384]{1,0:T(8,128)(2,1)S(1)}, u32[]{:S(2)}, u32[]{:S(2)}) collective-permute-start(bf16[256,384]{1,0:T(8,128)(2,1)S(1)} %get-tuple-element.58), channel_id=1, source_target_pairs={{0,6},{1,7},{2,0},{3,1},{4,2},{5,3},{6,4},{7,5},{8,14},{9,15},{10,... | collective-permute-start | bytes 589832 | tf_op jit(solution)/shard_map/ppermute | solution.py:37
  81.4 40.5 %collective-permute-start.20 = (bf16[1024,384]{1,0:T(8,128)(2,1)S(1)}, bf16[1024,384]{1,0:T(8,128)(2,1)S(1)}, u32[]{:S(2)}, u32[]{:S(2)}) collective-permute-start(bf16[1024,384]{1,0:T(8,128)(2,1)S(1)} %get-tuple-element.66), channel_id=1, source_target_pairs={{0,2},{1,3},{2,4},{3,5},{4,6},{5,7},{6,0},{7,1},{8,10},{9,11},{10,... | collective-permute-start | bytes 2359304 | tf_op jit(solution)/shard_map/ppermute | solution.py:37
  82.5 34.7 %copy-start.7 = (bf16[512,384]{1,0:T(8,128)(2,1)S(1)}, bf16[512,384]{1,0:T(8,128)(2,1)}, u32[]{:S(2)}) copy-start(bf16[512,384]{1,0:T(8,128)(2,1)} %copy-done.5) | copy-start | bytes 1179652
  82.5 39.4 %collective-permute-start.21 = (bf16[1024,384]{1,0:T(8,128)(2,1)S(1)}, bf16[1024,384]{1,0:T(8,128)(2,1)S(1)}, u32[]{:S(2)}, u32[]{:S(2)}) collective-permute-start(bf16[1024,384]{1,0:T(8,128)(2,1)S(1)} %get-tuple-element.67), channel_id=1, source_target_pairs={{0,6},{1,7},{2,0},{3,1},{4,2},{5,3},{6,4},{7,5},{8,14},{9,15},{10,... | collective-permute-start | bytes 2359304 | tf_op jit(solution)/shard_map/ppermute | solution.py:37
  86.6 35.3 %collective-permute-start.22 = (bf16[512,384]{1,0:T(8,128)(2,1)S(1)}, bf16[512,384]{1,0:T(8,128)(2,1)S(1)}, u32[]{:S(2)}, u32[]{:S(2)}) collective-permute-start(bf16[512,384]{1,0:T(8,128)(2,1)S(1)} %get-tuple-element.69), channel_id=1, source_target_pairs={{0,2},{1,3},{2,4},{3,5},{4,6},{5,7},{6,0},{7,1},{8,10},{9,11},{10,... | collective-permute-start | bytes 1179656 | tf_op jit(solution)/shard_map/ppermute | solution.py:37
  86.7 35.2 %collective-permute-start.23 = (bf16[512,384]{1,0:T(8,128)(2,1)S(1)}, bf16[512,384]{1,0:T(8,128)(2,1)S(1)}, u32[]{:S(2)}, u32[]{:S(2)}) collective-permute-start(bf16[512,384]{1,0:T(8,128)(2,1)S(1)} %get-tuple-element.70), channel_id=1, source_target_pairs={{0,6},{1,7},{2,0},{3,1},{4,2},{5,3},{6,4},{7,5},{8,14},{9,15},{10,... | collective-permute-start | bytes 1179656 | tf_op jit(solution)/shard_map/ppermute | solution.py:37
  89.9 7.8 %collective-permute-start.14 = (bf16[2,64,384]{2,1,0:T(8,128)(2,1)S(1)}, bf16[2,64,384]{2,1,0:T(8,128)(2,1)S(1)}, u32[]{:S(2)}, u32[]{:S(2)}) collective-permute-start(bf16[2,64,384]{2,1,0:T(8,128)(2,1)S(1)} %get-tuple-element.62), channel_id=1, source_target_pairs={{0,64},{1,65},{2,66},{3,67},{4,68},{5,69},{6,70},{7,71},{8,72},{9,... | collective-permute-start | bytes 294920 | tf_op jit(solution)/shard_map/ppermute | solution.py:37
  97.7 8.7 %collective-permute-start.15 = (bf16[2,64,384]{2,1,0:T(8,128)(2,1)S(1)}, bf16[2,64,384]{2,1,0:T(8,128)(2,1)S(1)}, u32[]{:S(2)}, u32[]{:S(2)}) collective-permute-start(bf16[2,64,384]{2,1,0:T(8,128)(2,1)S(1)} %get-tuple-element.63), channel_id=1, source_target_pairs={{0,128},{1,129},{2,130},{3,131},{4,132},{5,133},{6,134},{7,135},{8... | collective-permute-start | bytes 294920 | tf_op jit(solution)/shard_map/ppermute | solution.py:37
  106.4 6.6 %collective-permute-start.16 = (bf16[2,64,384]{2,1,0:T(8,128)(2,1)S(1)}, bf16[2,64,384]{2,1,0:T(8,128)(2,1)S(1)}, u32[]{:S(2)}, u32[]{:S(2)}) collective-permute-start(bf16[2,64,384]{2,1,0:T(8,128)(2,1)S(1)} %get-tuple-element.64), channel_id=1, source_target_pairs={{0,192},{1,193},{2,194},{3,195},{4,196},{5,197},{6,198},{7,199},{8... | collective-permute-start | bytes 294920 | tf_op jit(solution)/shard_map/ppermute | solution.py:37
  113.0 19.3 %copy-start.1 = (bf16[2,1024,384]{2,1,0:T(8,128)(2,1)S(1)}, bf16[2,1024,384]{2,1,0:T(8,128)(2,1)}, u32[]{:S(2)}) copy-start(bf16[2,1024,384]{2,1,0:T(8,128)(2,1)} %residual.5) | copy-start | bytes 4718596
  113.0 19.3 %copy-start.10 = (bf16[2,384]{1,0:T(2,128)(2,1)S(1)}, bf16[2,384]{1,0:T(2,128)(2,1)}, u32[]{:S(2)}) copy-start(bf16[2,384]{1,0:T(2,128)(2,1)} %gate.5) | copy-start | bytes 4612
  113.1 19.3 %copy-start.11 = (s32[32]{0:T(128)S(1)}, s32[32]{0:T(128)}, u32[]{:S(2)}) copy-start(s32[32]{0:T(128)} %counts.5) | copy-start | bytes 388
  113.1 4.2 %collective-permute-start.17 = (bf16[64,384]{1,0:T(8,128)(2,1)S(1)}, bf16[64,384]{1,0:T(8,128)(2,1)S(1)}, u32[]{:S(2)}, u32[]{:S(2)}) collective-permute-start(bf16[64,384]{1,0:T(8,128)(2,1)S(1)} %get-tuple-element.72.down_own), channel_id=1, source_target_pairs={{0,1},{1,0},{2,3},{3,2},{4,5},{5,4},{6,7},{7,6},{8,9},{9,8},{10,11... | collective-permute-start | bytes 147464 | tf_op jit(solution)/shard_map/ppermute | solution.py:37
  119.5 6.4 %collective-permute-start.19 = (bf16[64,2048]{1,0:T(8,128)(2,1)S(1)}, bf16[64,2048]{1,0:T(8,128)(2,1)S(1)}, u32[]{:S(2)}, u32[]{:S(2)}) collective-permute-start(bf16[64,2048]{1,0:T(8,128)(2,1)S(1)} %lowrank.1), channel_id=1, source_target_pairs={{0,6},{1,7},{2,0},{3,1},{4,2},{5,3},{6,4},{7,5},{8,14},{9,15},{10,... | collective-permute-start | bytes 786440 | tf_op jit(solution)/shard_map/ppermute | solution.py:37
  121.9 10.4 %collective-permute-start.18 = (bf16[64,2048]{1,0:T(8,128)(2,1)S(1)}, bf16[64,2048]{1,0:T(8,128)(2,1)S(1)}, u32[]{:S(2)}, u32[]{:S(2)}) collective-permute-start(bf16[64,2048]{1,0:T(8,128)(2,1)S(1)} %lowrank.1), channel_id=1, source_target_pairs={{0,2},{1,3},{2,4},{3,5},{4,6},{5,7},{6,0},{7,1},{8,10},{9,11},{10,... | collective-permute-start | bytes 786440 | tf_op jit(solution)/shard_map/ppermute | solution.py:37
  121.9 10.4 %collective-permute-start.24 = (bf16[64,2048]{1,0:T(8,128)(2,1)S(1)}, bf16[64,2048]{1,0:T(8,128)(2,1)S(1)}, u32[]{:S(2)}, u32[]{:S(2)}) collective-permute-start(bf16[64,2048]{1,0:T(8,128)(2,1)S(1)} %lowrank.1), channel_id=1, source_target_pairs={{0,4},{1,5},{2,6},{3,7},{4,0},{5,1},{6,2},{7,3},{8,12},{9,13},{10,... | collective-permute-start | bytes 786440 | tf_op jit(solution)/shard_map/ppermute | solution.py:37

commit v4 on v2

--- a/solution.py
+++ b/solution.py
@@ -512,13 +512,12 @@
     got1 = pass_on(1, far1)
     held, away = merge(after(info, *far1), 5, held, got, NH)
     got = send(away, pair_x(1))
-    far2 = first_half(2, away)
-    got2 = pass_on(2, far2)
-    held = fan(after(info, *far2), held, got)
+    last = spread(after(info, away), own[2], other[2], output_weight, swapped)
+    home2 = [send(part, turn) for part, turn in zip(last, (to_y(2),) + turns)]
+    held = fan(after(info, *last), held, got)
     parts = [held[0]] + [send(part, to_h(d + 1)) for d, part in enumerate(held[1:])]
-    near1, home1 = second_half(1, got1, *held, *home0, *got2)
-    near2, home2 = second_half(2, got2, *near1)
-    parts[0] = after(parts[0], *near2)
+    near1, home1 = second_half(1, got1, *held, *home0)
+    parts[0] = after(parts[0], *near1)
     down, up = settle(parts)
     order = (0, 2, 1)
     t = lowrank(down, send(down, swap_z), [own[i] for i in order], [other[i] for i in order])

time: 132 us -> 148 us (1.12)
  waiting for transfers between devices: 35.8 us -> 55.4 us
  starting transfers between devices: 43.9 us -> 40.5 us
    ppermute x24 -> x23, waiting for transfers between devices: 35.8 us -> 55.4 us  [send(): return lax.ppermute(array, ('rep', 'tp'), table(move))]
    ppermute x24 -> x23, starting transfers between devices: 43.9 us -> 40.5 us  [send(): return lax.ppermute(array, ('rep', 'tp'), table(move))]
    pallas_call x1 -> x2, Pallas kernels: 1.79 us -> 3.57 us  [spread(): pl.pallas_call(spread_kernel, grid_spec=pltpu.PrefetchScalarGridSpec(num_...]
    pallas_call x2 -> x1, Pallas kernels: 4.43 us -> 3.06 us  [near(): pl.pallas_call(functools.partial(near_kernel, places), grid_spec=pltpu.Pr...]
    pallas_call x2 -> x1, Pallas kernels: 3.78 us -> 2.64 us  [far(): pl.pallas_call(far_kernel, grid_spec=pltpu.PrefetchScalarGridSpec(num_sca...]
  transfers between devices with their start and end apart: 24 -> 23, of which waited for: 11 -> 12; matrix products, arithmetic and copies ran while one was open for 0% -> 0% of each run, Pallas kernels for 24% -> 23%
where the time goes in v4:
time: 148 us; the launch traced here: 147 us
  waiting for transfers between devices  55.4 us (37%)
  Pallas kernels  47.5 us (32%)
  starting transfers between devices  40.5 us (27%)
  local copies, waits for them, and re-layouts  2.82 us (2%)
    ppermute x23, waiting for transfers between devices, send(): return lax.ppermute(array, ('rep', 'tp'), table(move))  55.4 us
    ppermute x23, starting transfers between devices, send(): return lax.ppermute(array, ('rep', 'tp'), table(move))  40.5 us
    pallas_call x3, Pallas kernels, attend(): pl.pallas_call(attend_kernel, grid=(width // HD,), in_specs=[pl.BlockSpec...  17.2 us
    pallas_call x3, Pallas kernels, home(): pl.pallas_call(functools.partial(home_kernel, b, len(gots)), grid_spec=pl...  7.83 us
    pallas_call x2, Pallas kernels, spread(): pl.pallas_call(spread_kernel, grid_spec=pltpu.PrefetchScalarGridSpec(num_...  3.57 us
    pallas_call x1, Pallas kernels, keep(): pl.pallas_call(keep_kernel, in_specs=[smem] * 3 + [vmem] * 3, out_specs=[...  3.3 us
    pallas_call x1, Pallas kernels, near(): pl.pallas_call(functools.partial(near_kernel, places), grid_spec=pltpu.Pr...  3.06 us
    pallas_call x1, Pallas kernels, cut(): pl.pallas_call(cut_kernel, grid_spec=pltpu.PrefetchScalarGridSpec(num_sca...  3.04 us
  transfers between devices with their start and end apart: 23, of which 12 were waited for; matrix products, arithmetic and copies ran while one was open for 0% of the time, Pallas kernels for 23%

profile of v4, /device:TPU:32, one launch (start us, length us, event | category | flops | bytes accessed | tf_op | source)
XLA Modules:
  0.0 146.5 jit_solution(12922242019029349825)
XLA Ops:
  0.0 0.6 stack.35.info.marks
  0.6 3.0 %cut.1 = bf16[384,1536]{1,0:T(8,128)(2,1)} custom-call(s32[8]{0:T(128)} %stack.35.info.marks, bf16[384,3072]{1,0:T(8,128)(2,1)} %w_own.7, bf16[384,3072]{1,0:T(8,128)(2,1)} %w_own.7, bf16[384,3072]{1,0:T(8,128)(2,1)} %w_own.7, bf16[384,3072]{1,0:T(8,128)(2,1)} %w_own.7), custom_call_target="tpu_custom_call" | custom-call | bytes 2359296 | tf_op jit(solution)/shard_map/cut/pallas_call | solution.py:410
  3.7 2.6 %choose.1 = bf16[16,2,64,384]{3,2,1,0:T(8,128)(2,1)} custom-call(s32[8]{0:T(128)} %stack.35.info.marks, s32[32]{0:T(128)} %ids.3, s32[128]{0:T(128)} %slots.3, bf16[4,64,384]{2,1,0:T(8,128)(2,1)} %bitcast.18, bf16[4,64,384]{2,1,0:T(8,128)(2,1)} %up.3), custom_call_target="tpu_custom_call" | custom-call | bytes 1572864 | tf_op jit(solution)/shard_map/choose/pallas_call | solution.py:293
  6.3 0.0 collective-permute-start.1
  6.3 1.9 %collective-permute-start.3 = (bf16[384,1536]{1,0:T(8,128)(2,1)}, bf16[384,1536]{1,0:T(8,128)(2,1)S(1)}, u32[]{:S(2)}, u32[]{:S(2)}) collective-permute-start(bf16[384,1536]{1,0:T(8,128)(2,1)} %cut.1), channel_id=1, source_target_pairs={{0,193},{1,64},{2,195},{3,66},{4,197},{5,68},{6,199},{7,70},{8,201... | collective-permute-start | bytes 3538952 | tf_op jit(solution)/shard_map/ppermute | solution.py:37
  8.2 5.2 %attend.3.own.refs_0_ = bf16[512,384]{1,0:T(8,128)(2,1)} custom-call(bf16[2,1024,384]{2,1,0:T(8,128)(2,1)} %q_ref.2, bf16[2,1024,384]{2,1,0:T(8,128)(2,1)} %k_ref.5, bf16[2,1024,384]{2,1,0:T(8,128)(2,1)} %v_ref.5), custom_call_target="tpu_custom_call" | custom-call | flops 805306368 | bytes 2359296 | tf_op jit(solution)/shard_map/attend/pallas_call | solution.py:100
  13.4 4.0 %collective-permute-start = (bf16[512,384]{1,0:T(8,128)(2,1)}, bf16[512,384]{1,0:T(8,128)(2,1)S(1)}, u32[]{:S(2)}, u32[]{:S(2)}) collective-permute-start(bf16[512,384]{1,0:T(8,128)(2,1)} %attend.3.own.refs_0_), channel_id=1, source_target_pairs={{0,1},{1,0},{2,3},{3,2},{4,5},{5,4},{6,7},{7,6},{8,9},{9,8},{10,11... | collective-permute-start | bytes 1179656 | tf_op jit(solution)/shard_map/ppermute | solution.py:37
  17.5 6.9 %attend.4.own.refs_2_ = bf16[1024,384]{1,0:T(8,128)(2,1)} custom-call(bf16[2,1024,384]{2,1,0:T(8,128)(2,1)} %q_ref.2, bf16[2,1024,384]{2,1,0:T(8,128)(2,1)} %k_ref.5, bf16[2,1024,384]{2,1,0:T(8,128)(2,1)} %v_ref.5), custom_call_target="tpu_custom_call" | custom-call | flops 1610612736 | bytes 3145728 | tf_op jit(solution)/shard_map/attend/pallas_call | solution.py:100
  24.4 0.0 collective-permute-start.4
  24.4 2.9 %collective-permute-done.other.refs_3_ = bf16[512,384]{1,0:T(8,128)(2,1)S(1)} collective-permute-done((bf16[512,384]{1,0:T(8,128)(2,1)}, bf16[512,384]{1,0:T(8,128)(2,1)S(1)}, u32[]{:S(2)}, u32[]{:S(2)}) %collective-permute-start) | collective-permute-done | bytes 393248 | tf_op jit(solution)/shard_map/ppermute | solution.py:37
  27.2 0.0 collective-permute-done.1.got
  27.2 1.2 copy-done.12
  28.4 3.3 %keep.1 = (bf16[4,2,2,64,384]{4,3,2,1,0:T(8,128)(2,1)}, bf16[4,2,2,64,384]{4,3,2,1,0:T(8,128)(2,1)}) custom-call(s32[8]{0:T(128)} %stack.35.info.marks, s32[32]{0:T(128)} %ids.3, s32[128]{0:T(128)} %slots.3, bf16[4,64,384]{2,1,0:T(8,128)(2,1)} %bitcast.19, bf16[4,64,384]{2,1,0:T(8,128)(2,1)} %up.3, bf16[16,2,64,384]{3,2,1,0:T(8,128)(2,1)} %copy-done.12), custom_call_target="tpu_custom_call" | custom-call | bytes 3145728 | tf_op jit(solution)/shard_map/keep/pallas_call | solution.py:325
  31.7 3.1 %collective-permute-start.5 = (bf16[4,2,2,64,384]{4,3,2,1,0:T(8,128)(2,1)}, bf16[4,2,2,64,384]{4,3,2,1,0:T(8,128)(2,1)}, u32[]{:S(2)}, u32[]{:S(2)}) collective-permute-start(bf16[4,2,2,64,384]{4,3,2,1,0:T(8,128)(2,1)} %get-tuple-element.42), channel_id=1, source_target_pairs={{0,32},{1,33},{2,34},{3,35},{4,36},{5,37},{6,38},{7,39},{8,40},{9,... | collective-permute-start | bytes 2359304 | tf_op jit(solution)/shard_map/ppermute | solution.py:37
  34.8 5.1 %attend.5.own.refs_1_ = bf16[512,384]{1,0:T(8,128)(2,1)} custom-call(bf16[2,1024,384]{2,1,0:T(8,128)(2,1)} %q_ref.2, bf16[2,1024,384]{2,1,0:T(8,128)(2,1)} %k_ref.5, bf16[2,1024,384]{2,1,0:T(8,128)(2,1)} %v_ref.5), custom_call_target="tpu_custom_call" | custom-call | flops 805306368 | bytes 2359296 | tf_op jit(solution)/shard_map/attend/pallas_call | solution.py:100
  40.0 2.4 %collective-permute-start.2 = (bf16[512,384]{1,0:T(8,128)(2,1)}, bf16[512,384]{1,0:T(8,128)(2,1)S(1)}, u32[]{:S(2)}, u32[]{:S(2)}) collective-permute-start(bf16[512,384]{1,0:T(8,128)(2,1)} %attend.5.own.refs_1_), channel_id=1, source_target_pairs={{0,1},{1,0},{2,3},{3,2},{4,5},{5,4},{6,7},{7,6},{8,9},{9,8},{10,11... | collective-permute-start | bytes 1179656 | tf_op jit(solution)/shard_map/ppermute | solution.py:37
  42.4 0.0 collective-permute-done.3.w_other.r_other.l_other
  42.4 1.0 copy-done.6
  43.4 1.8 %spread.2 = (bf16[512,384]{1,0:T(8,128)(2,1)S(1)}, bf16[512,384]{1,0:T(8,128)(2,1)S(1)}, bf16[512,384]{1,0:T(8,128)(2,1)S(1)}) custom-call(s32[8]{0:T(128)S(1)} %copy-done.9, bf16[512,384]{1,0:T(8,128)(2,1)S(1)} %copy-done.3, bf16[512,384]{1,0:T(8,128)(2,1)S(1)} %copy-done.6, bf16[384,3072]{1,0:T(8,128)(2,1)S(1)} %copy-done, bf16[384,3072]{1,0:T(8,128)(2,1)S(1)} %copy-done, ...), custom_call_target="tpu_custom_call" | custom-call | flops 905969664 | bytes 1966080 | tf_op jit(solution)/shard_map/spread/pallas_call | solution.py:438
  45.2 0.0 collective-permute-done.4.other.refs_5_
  45.2 2.6 %far.1 = (bf16[512,384]{1,0:T(8,128)(2,1)S(1)}, bf16[512,384]{1,0:T(8,128)(2,1)S(1)}) custom-call(s32[8]{0:T(128)S(1)} %copy-done.9, bf16[1024,384]{1,0:T(8,128)(2,1)S(1)} %copy-done.2, bf16[1024,384]{1,0:T(8,128)(2,1)} %collective-permute-done.4.other.refs_5_, bf16[384,3072]{1,0:T(8,128)(2,1)S(1)} %copy-done, ...), custom_call_target="tpu_custom_call" | custom-call | flops 603979776 | bytes 2359296 | tf_op jit(solution)/shard_map/far/pallas_call | solution.py:137
  47.9 0.0 copy-start.4
  47.9 4.9 %collective-permute-done.5 = bf16[4,2,2,64,384]{4,3,2,1,0:T(8,128)(2,1)} collective-permute-done((bf16[4,2,2,64,384]{4,3,2,1,0:T(8,128)(2,1)}, bf16[4,2,2,64,384]{4,3,2,1,0:T(8,128)(2,1)}, u32[]{:S(2)}, u32[]{:S(2)}) %collective-permute-start.5) | collective-permute-done | bytes 786464 | tf_op jit(solution)/shard_map/ppermute | solution.py:37
  52.8 1.3 merge.1
  54.0 1.6 %collective-permute-start.6 = (bf16[4,1,2,64,384]{4,3,2,0,1:T(8,128)(2,1)S(1)}, bf16[4,1,2,64,384]{4,3,2,0,1:T(8,128)(2,1)S(1)}, u32[]{:S(2)}, u32[]{:S(2)}) collective-permute-start(bf16[4,1,2,64,384]{4,3,2,0,1:T(8,128)(2,1)S(1)} %bitcast.17), channel_id=1, source_target_pairs={{0,16},{1,17},{2,18},{3,19},{4,20},{5,21},{6,22},{7,23},{8,24},{9,... | collective-permute-start | bytes 1179656 | tf_op jit(solution)/shard_map/ppermute | solution.py:37
  55.6 3.2 %collective-permute-start.7 = (bf16[512,384]{1,0:T(8,128)(2,1)S(1)}, bf16[512,384]{1,0:T(8,128)(2,1)S(1)}, u32[]{:S(2)}, u32[]{:S(2)}) collective-permute-start(bf16[512,384]{1,0:T(8,128)(2,1)S(1)} %get-tuple-element.45), channel_id=1, source_target_pairs={{0,4},{1,5},{2,6},{3,7},{4,0},{5,1},{6,2},{7,3},{8,12},{9,13},{10,... | collective-permute-start | bytes 1179656 | tf_op jit(solution)/shard_map/ppermute | solution.py:37
  58.8 0.7 collective-permute-start.8
  59.5 2.6 %collective-permute-start.9 = (bf16[512,384]{1,0:T(8,128)(2,1)S(1)}, bf16[512,384]{1,0:T(8,128)(2,1)S(1)}, u32[]{:S(2)}, u32[]{:S(2)}) collective-permute-start(bf16[512,384]{1,0:T(8,128)(2,1)S(1)} %get-tuple-element.47), channel_id=1, source_target_pairs={{0,6},{1,7},{2,0},{3,1},{4,2},{5,3},{6,4},{7,5},{8,14},{9,15},{10,... | collective-permute-start | bytes 1179656 | tf_op jit(solution)/shard_map/ppermute | solution.py:37
  62.1 0.0 collective-permute-done.2.other.refs_4_
  62.1 0.0 collective-permute-start.10
  62.1 1.8 %collective-permute-done.6 = bf16[4,1,2,64,384]{4,3,2,0,1:T(8,128)(2,1)S(1)} collective-permute-done((bf16[4,1,2,64,384]{4,3,2,0,1:T(8,128)(2,1)S(1)}, bf16[4,1,2,64,384]{4,3,2,0,1:T(8,128)(2,1)S(1)}, u32[]{:S(2)}, u32[]{:S(2)}) %collective-permute-start.6) | collective-permute-done | bytes 393248 | tf_op jit(solution)/shard_map/ppermute | solution.py:37
  63.9 3.0 %collective-permute-start.11 = (bf16[512,384]{1,0:T(8,128)(2,1)S(1)}, bf16[512,384]{1,0:T(8,128)(2,1)S(1)}, u32[]{:S(2)}, u32[]{:S(2)}) collective-permute-start(bf16[512,384]{1,0:T(8,128)(2,1)S(1)} %get-tuple-element.50), channel_id=1, source_target_pairs={{0,6},{1,7},{2,0},{3,1},{4,2},{5,3},{6,4},{7,5},{8,14},{9,15},{10,... | collective-permute-start | bytes 1179656 | tf_op jit(solution)/shard_map/ppermute | solution.py:37
  66.9 1.8 %spread.3 = (bf16[512,384]{1,0:T(8,128)(2,1)S(1)}, bf16[512,384]{1,0:T(8,128)(2,1)S(1)}, bf16[512,384]{1,0:T(8,128)(2,1)S(1)}) custom-call(s32[8]{0:T(128)S(1)} %copy-done.9, bf16[512,384]{1,0:T(8,128)(2,1)S(1)} %copy-done.4, bf16[512,384]{1,0:T(8,128)(2,1)S(1)} %collective-permute-done.2.other.refs_4_, bf16[384,3072]{1,0:T(8,128)(2,1)S(1)} %copy-done, ...), custom_call_target="tpu_custom_call" | custom-call | flops 905969664 | bytes 1966080 | tf_op jit(solution)/shard_map/spread/pallas_call | solution.py:438
  68.7 0.6 fan.1
  69.3 1.7 %collective-permute-start.12 = (bf16[2,64,384]{2,1,0:T(8,128)(2,1)S(1)}, bf16[2,64,384]{2,1,0:T(8,128)(2,1)S(1)}, u32[]{:S(2)}, u32[]{:S(2)}) collective-permute-start(bf16[2,64,384]{2,1,0:T(8,128)(2,1)S(1)} %get-tuple-element.61), channel_id=1, source_target_pairs={{0,64},{1,65},{2,66},{3,67},{4,68},{5,69},{6,70},{7,71},{8,72},{9,... | collective-permute-start | bytes 294920 | tf_op jit(solution)/shard_map/ppermute | solution.py:37
  71.0 5.8 %collective-permute-done.8.rest_1_ = bf16[512,384]{1,0:T(8,128)(2,1)S(1)} collective-permute-done((bf16[512,384]{1,0:T(8,128)(2,1)S(1)}, bf16[512,384]{1,0:T(8,128)(2,1)S(1)}, u32[]{:S(2)}, u32[]{:S(2)}) %collective-permute-start.8) | collective-permute-done | bytes 393248 | tf_op jit(solution)/shard_map/ppermute | solution.py:37
  76.8 2.7 %collective-permute-start.13 = (bf16[2,64,384]{2,1,0:T(8,128)(2,1)S(1)}, bf16[2,64,384]{2,1,0:T(8,128)(2,1)S(1)}, u32[]{:S(2)}, u32[]{:S(2)}) collective-permute-start(bf16[2,64,384]{2,1,0:T(8,128)(2,1)S(1)} %get-tuple-element.62), channel_id=1, source_target_pairs={{0,128},{1,129},{2,130},{3,131},{4,132},{5,133},{6,134},{7,135},{8... | collective-permute-start | bytes 294920 | tf_op jit(solution)/shard_map/ppermute | solution.py:37
  79.6 0.0 collective-permute-done.9.rest_2_
  79.6 2.7 %collective-permute-start.14 = (bf16[2,64,384]{2,1,0:T(8,128)(2,1)S(1)}, bf16[2,64,384]{2,1,0:T(8,128)(2,1)S(1)}, u32[]{:S(2)}, u32[]{:S(2)}) collective-permute-start(bf16[2,64,384]{2,1,0:T(8,128)(2,1)S(1)} %get-tuple-element.63), channel_id=1, source_target_pairs={{0,192},{1,193},{2,194},{3,195},{4,196},{5,197},{6,198},{7,199},{8... | collective-permute-start | bytes 294920 | tf_op jit(solution)/shard_map/ppermute | solution.py:37
  82.2 1.3 collective-permute-done.10.refs_0_
  83.5 0.4 collective-permute-done.11.refs_1_
  83.9 3.1 %near.1 = (bf16[1024,384]{1,0:T(8,128)(2,1)S(1)}, bf16[1024,384]{1,0:T(8,128)(2,1)S(1)}) custom-call(s32[8]{0:T(128)S(1)} %copy-done.9, bf16[1024,384]{1,0:T(8,128)(2,1)S(1)} %copy-done.2, bf16[1024,384]{1,0:T(8,128)(2,1)} %collective-permute-done.4.other.refs_5_, bf16[384,3072]{1,0:T(8,128)(2,1)S(1)} %copy-done, bf16[384,3072]{1,0:T(8,128)(2,1)S(1)} %copy-done, ...), custom_call_target="tpu_custom_call" | custom-call | flops 1207959552 | bytes 3932160 | tf_op jit(solution)/shard_map/near/pallas_call | solution.py:176
  87.0 1.4 collective-permute-start.17
  88.4 1.9 %collective-permute-start.18 = (bf16[1024,384]{1,0:T(8,128)(2,1)S(1)}, bf16[1024,384]{1,0:T(8,128)(2,1)S(1)}, u32[]{:S(2)}, u32[]{:S(2)}) collective-permute-start(bf16[1024,384]{1,0:T(8,128)(2,1)S(1)} %get-tuple-element.66), channel_id=1, source_target_pairs={{0,6},{1,7},{2,0},{3,1},{4,2},{5,3},{6,4},{7,5},{8,14},{9,15},{10,... | collective-permute-start | bytes 2359304 | tf_op jit(solution)/shard_map/ppermute | solution.py:37
  90.3 0.0 collective-permute-done.12.b
  90.3 0.0 collective-permute-done.13.c
  90.3 0.5 collective-permute-start.15
  90.9 3.6 %collective-permute-done.15.down_other = bf16[64,384]{1,0:T(8,128)(2,1)S(1)} collective-permute-done((bf16[64,384]{1,0:T(8,128)(2,1)S(1)}, bf16[64,384]{1,0:T(8,128)(2,1)S(1)}, u32[]{:S(2)}, u32[]{:S(2)}) %collective-permute-start.15) | collective-permute-done | bytes 49184 | tf_op jit(solution)/shard_map/ppermute | solution.py:37
  94.5 2.3 %lowrank.1 = bf16[64,2048]{1,0:T(8,128)(2,1)S(1)} custom-call(bf16[64,384]{1,0:T(8,128)(2,1)S(1)} %get-tuple-element.68.down_own, bf16[64,384]{1,0:T(8,128)(2,1)S(1)} %collective-permute-done.15.down_other, bf16[512,384]{1,0:T(8,128)(2,1)S(1)} %copy-done.3, bf16[512,384]{1,0:T(8,128)(2,1)S(1)} %copy-done.4, bf16[1024,384]{1,0:T(8,128)(2,1)S(1)} %copy-done.2, ...), custom_call_target="tpu_custom_call" | custom-call | flops 201326592 | bytes 3145728 | tf_op jit(solution)/shard_map/lowrank/pallas_call | solution.py:215
  96.8 0.0 copy-start.10
  96.8 0.2 collective-permute-start.16
  97.0 2.7 %collective-permute-start.19 = (bf16[512,384]{1,0:T(8,128)(2,1)S(1)}, bf16[512,384]{1,0:T(8,128)(2,1)S(1)}, u32[]{:S(2)}, u32[]{:S(2)}) collective-permute-start(bf16[512,384]{1,0:T(8,128)(2,1)S(1)} %get-tuple-element.55), channel_id=1, source_target_pairs={{0,4},{1,5},{2,6},{3,7},{4,0},{5,1},{6,2},{7,3},{8,12},{9,13},{10,... | collective-permute-start | bytes 1179656 | tf_op jit(solution)/shard_map/ppermute | solution.py:37
  99.8 14.7 %collective-permute-done.16 = bf16[64,2048]{1,0:T(8,128)(2,1)S(1)} collective-permute-done((bf16[64,2048]{1,0:T(8,128)(2,1)S(1)}, bf16[64,2048]{1,0:T(8,128)(2,1)S(1)}, u32[]{:S(2)}, u32[]{:S(2)}) %collective-permute-start.16) | collective-permute-done | bytes 262176 | tf_op jit(solution)/shard_map/ppermute | solution.py:37
  114.5 1.2 collective-permute-start.21
  115.7 0.1 add.6
  115.8 7.8 %collective-permute-done.19.rest_0_ = bf16[512,384]{1,0:T(8,128)(2,1)S(1)} collective-permute-done((bf16[512,384]{1,0:T(8,128)(2,1)S(1)}, bf16[512,384]{1,0:T(8,128)(2,1)S(1)}, u32[]{:S(2)}, u32[]{:S(2)}) %collective-permute-start.19) | collective-permute-done | bytes 393248 | tf_op jit(solution)/shard_map/ppermute | solution.py:37
  123.6 4.1 %collective-permute-done.20.rest_1_ = bf16[512,384]{1,0:T(8,128)(2,1)S(1)} collective-permute-done((bf16[512,384]{1,0:T(8,128)(2,1)S(1)}, bf16[512,384]{1,0:T(8,128)(2,1)S(1)}, u32[]{:S(2)}, u32[]{:S(2)}) %collective-permute-start.20) | collective-permute-done | bytes 393248 | tf_op jit(solution)/shard_map/ppermute | solution.py:37
  127.7 2.2 %collective-permute-done.21.rest_2_ = bf16[512,384]{1,0:T(8,128)(2,1)S(1)} collective-permute-done((bf16[512,384]{1,0:T(8,128)(2,1)S(1)}, bf16[512,384]{1,0:T(8,128)(2,1)S(1)}, u32[]{:S(2)}, u32[]{:S(2)}) %collective-permute-start.21) | collective-permute-done | bytes 393248 | tf_op jit(solution)/shard_map/ppermute | solution.py:37
  129.9 2.9 %collective-permute-start.22 = (bf16[64,2048]{1,0:T(8,128)(2,1)S(1)}, bf16[64,2048]{1,0:T(8,128)(2,1)S(1)}, u32[]{:S(2)}, u32[]{:S(2)}) collective-permute-start(bf16[64,2048]{1,0:T(8,128)(2,1)S(1)} %add.6), channel_id=1, source_target_pairs={{0,4},{1,5},{2,6},{3,7},{4,0},{5,1},{6,2},{7,3},{8,12},{9,13},{10,... | collective-permute-start | bytes 786440 | tf_op jit(solution)/shard_map/ppermute | solution.py:37
  132.8 5.8 %collective-permute-done.22 = bf16[64,2048]{1,0:T(8,128)(2,1)S(1)} collective-permute-done((bf16[64,2048]{1,0:T(8,128)(2,1)S(1)}, bf16[64,2048]{1,0:T(8,128)(2,1)S(1)}, u32[]{:S(2)}, u32[]{:S(2)}) %collective-permute-start.22) | collective-permute-done | bytes 262176 | tf_op jit(solution)/shard_map/ppermute | solution.py:37
  138.6 0.1 add.7.t
  138.7 2.0 %home.3.rest_2_ = bf16[2,1024,384]{2,1,0:T(8,128)(2,1)} custom-call(s32[8]{0:T(128)S(1)} %copy-done.9, s32[32]{0:T(128)S(1)} %copy-done.11, bf16[512,384]{1,0:T(8,128)(2,1)S(1)} %copy-done.3, bf16[512,384]{1,0:T(8,128)(2,1)S(1)} %copy-done.7, bf16[384,3072]{1,0:T(8,128)(2,1)S(1)} %copy-done, ...), custom_call_target="tpu_custom_call" | custom-call | flops 301989888 | bytes 2359296 | tf_op jit(solution)/shard_map/home/pallas_call | solution.py:244
  140.7 3.8 %home.4.rest_3_ = bf16[2,1024,384]{2,1,0:T(8,128)(2,1)} custom-call(s32[8]{0:T(128)S(1)} %copy-done.9, s32[32]{0:T(128)S(1)} %copy-done.11, bf16[1024,384]{1,0:T(8,128)(2,1)S(1)} %copy-done.2, bf16[1024,384]{1,0:T(8,128)(2,1)} %collective-permute-done.4.other.refs_5_, bf16[384,3072]{1,0:T(8,128)(2,1)S(1)} %copy-done, ...), custom_call_target="tpu_custom_call", output_to_operand_aliasing={{}: (12, {})} | custom-call | flops 603979776 | bytes 4718592 | tf_op jit(solution)/shard_map/home/pallas_call | solution.py:244
  144.5 2.0 %home.5 = bf16[2,1024,384]{2,1,0:T(8,128)(2,1)} custom-call(s32[8]{0:T(128)S(1)} %copy-done.9, s32[32]{0:T(128)S(1)} %copy-done.11, bf16[512,384]{1,0:T(8,128)(2,1)S(1)} %copy-done.4, bf16[512,384]{1,0:T(8,128)(2,1)S(1)} %collective-permute-done.2.other.refs_4_, bf16[384,3072]{1,0:T(8,128)(2,1)S(1)} %copy-done, ...), custom_call_target="tpu_custom_call", output_to_operand_aliasing={{}: (13, {})} | custom-call | flops 301989888 | bytes 2359296 | tf_op jit(solution)/shard_map/home/pallas_call | solution.py:244
  (28 shorter events, 0.1 us)
Async XLA Ops:
  6.3 20.9 %collective-permute-start.1 = (bf16[16,2,64,384]{3,2,1,0:T(8,128)(2,1)}, bf16[16,2,64,384]{3,2,1,0:T(8,128)(2,1)S(1)}, u32[]{:S(2)}, u32[]{:S(2)}) collective-permute-start(bf16[16,2,64,384]{3,2,1,0:T(8,128)(2,1)} %choose.1), channel_id=1, source_target_pairs={{0,8},{1,9},{2,10},{3,11},{4,12},{5,13},{6,14},{7,15},{8,0},{9,1},... | collective-permute-start | bytes 4718600 | tf_op jit(solution)/shard_map/ppermute | solution.py:37
  6.3 36.1 %collective-permute-start.3 = (bf16[384,1536]{1,0:T(8,128)(2,1)}, bf16[384,1536]{1,0:T(8,128)(2,1)S(1)}, u32[]{:S(2)}, u32[]{:S(2)}) collective-permute-start(bf16[384,1536]{1,0:T(8,128)(2,1)} %cut.1), channel_id=1, source_target_pairs={{0,193},{1,64},{2,195},{3,66},{4,197},{5,68},{6,199},{7,70},{8,201... | collective-permute-start | bytes 3538952 | tf_op jit(solution)/shard_map/ppermute | solution.py:37
  13.4 13.8 %collective-permute-start = (bf16[512,384]{1,0:T(8,128)(2,1)}, bf16[512,384]{1,0:T(8,128)(2,1)S(1)}, u32[]{:S(2)}, u32[]{:S(2)}) collective-permute-start(bf16[512,384]{1,0:T(8,128)(2,1)} %attend.3.own.refs_0_), channel_id=1, source_target_pairs={{0,1},{1,0},{2,3},{3,2},{4,5},{5,4},{6,7},{7,6},{8,9},{9,8},{10,11... | collective-permute-start | bytes 1179656 | tf_op jit(solution)/shard_map/ppermute | solution.py:37
  24.4 20.8 %collective-permute-start.4 = (bf16[1024,384]{1,0:T(8,128)(2,1)}, bf16[1024,384]{1,0:T(8,128)(2,1)}, u32[]{:S(2)}, u32[]{:S(2)}) collective-permute-start(bf16[1024,384]{1,0:T(8,128)(2,1)} %attend.4.own.refs_2_), channel_id=1, source_target_pairs={{0,1},{1,0},{2,3},{3,2},{4,5},{5,4},{6,7},{7,6},{8,9},{9,8},{10,11... | collective-permute-start | bytes 2359304 | tf_op jit(solution)/shard_map/ppermute | solution.py:37
  27.2 4.5 %copy-start.5 = (bf16[512,384]{1,0:T(8,128)(2,1)}, bf16[512,384]{1,0:T(8,128)(2,1)S(1)}, u32[]{:S(2)}) copy-start(bf16[512,384]{1,0:T(8,128)(2,1)S(1)} %collective-permute-done.other.refs_3_) | copy-start | bytes 1179652
  27.2 1.2 copy-start.12
  31.7 10.7 %copy-start = (bf16[384,3072]{1,0:T(8,128)(2,1)S(1)}, bf16[384,3072]{1,0:T(8,128)(2,1)}, u32[]{:S(2)}) copy-start(bf16[384,3072]{1,0:T(8,128)(2,1)} %w_own.7) | copy-start | bytes 7077892
  31.7 10.7 %copy-start.3 = (bf16[512,384]{1,0:T(8,128)(2,1)S(1)}, bf16[512,384]{1,0:T(8,128)(2,1)}, u32[]{:S(2)}) copy-start(bf16[512,384]{1,0:T(8,128)(2,1)} %attend.3.own.refs_0_) | copy-start | bytes 1179652
  31.7 10.7 %copy-start.9 = (s32[8]{0:T(128)S(1)}, s32[8]{0:T(128)}, u32[]{:S(2)}) copy-start(s32[8]{0:T(128)} %stack.35.info.marks) | copy-start | bytes 100
  31.7 21.0 %collective-permute-start.5 = (bf16[4,2,2,64,384]{4,3,2,1,0:T(8,128)(2,1)}, bf16[4,2,2,64,384]{4,3,2,1,0:T(8,128)(2,1)}, u32[]{:S(2)}, u32[]{:S(2)}) collective-permute-start(bf16[4,2,2,64,384]{4,3,2,1,0:T(8,128)(2,1)} %get-tuple-element.42), channel_id=1, source_target_pairs={{0,32},{1,33},{2,34},{3,35},{4,36},{5,37},{6,38},{7,39},{8,40},{9,... | collective-permute-start | bytes 2359304 | tf_op jit(solution)/shard_map/ppermute | solution.py:37
  40.0 5.2 %copy-start.2 = (bf16[1024,384]{1,0:T(8,128)(2,1)S(1)}, bf16[1024,384]{1,0:T(8,128)(2,1)}, u32[]{:S(2)}) copy-start(bf16[1024,384]{1,0:T(8,128)(2,1)} %attend.4.own.refs_2_) | copy-start | bytes 2359300
  40.0 22.1 %collective-permute-start.2 = (bf16[512,384]{1,0:T(8,128)(2,1)}, bf16[512,384]{1,0:T(8,128)(2,1)S(1)}, u32[]{:S(2)}, u32[]{:S(2)}) collective-permute-start(bf16[512,384]{1,0:T(8,128)(2,1)} %attend.5.own.refs_1_), channel_id=1, source_target_pairs={{0,1},{1,0},{2,3},{3,2},{4,5},{5,4},{6,7},{7,6},{8,9},{9,8},{10,11... | collective-permute-start | bytes 1179656 | tf_op jit(solution)/shard_map/ppermute | solution.py:37
  42.4 1.0 copy-start.6
  45.2 7.6 %copy-start.8 = (bf16[4,2,2,64,384]{4,3,2,1,0:T(8,128)(2,1)S(1)}, bf16[4,2,2,64,384]{4,3,2,1,0:T(8,128)(2,1)}, u32[]{:S(2)}) copy-start(bf16[4,2,2,64,384]{4,3,2,1,0:T(8,128)(2,1)} %get-tuple-element.52) | copy-start | bytes 2359300
  47.9 19.1 %copy-start.4 = (bf16[512,384]{1,0:T(8,128)(2,1)S(1)}, bf16[512,384]{1,0:T(8,128)(2,1)}, u32[]{:S(2)}) copy-start(bf16[512,384]{1,0:T(8,128)(2,1)} %attend.5.own.refs_1_) | copy-start | bytes 1179652
  54.0 9.9 %collective-permute-start.6 = (bf16[4,1,2,64,384]{4,3,2,0,1:T(8,128)(2,1)S(1)}, bf16[4,1,2,64,384]{4,3,2,0,1:T(8,128)(2,1)S(1)}, u32[]{:S(2)}, u32[]{:S(2)}) collective-permute-start(bf16[4,1,2,64,384]{4,3,2,0,1:T(8,128)(2,1)S(1)} %bitcast.17), channel_id=1, source_target_pairs={{0,16},{1,17},{2,18},{3,19},{4,20},{5,21},{6,22},{7,23},{8,24},{9,... | collective-permute-start | bytes 1179656 | tf_op jit(solution)/shard_map/ppermute | solution.py:37
  55.6 13.7 %collective-permute-start.7 = (bf16[512,384]{1,0:T(8,128)(2,1)S(1)}, bf16[512,384]{1,0:T(8,128)(2,1)S(1)}, u32[]{:S(2)}, u32[]{:S(2)}) collective-permute-start(bf16[512,384]{1,0:T(8,128)(2,1)S(1)} %get-tuple-element.45), channel_id=1, source_target_pairs={{0,4},{1,5},{2,6},{3,7},{4,0},{5,1},{6,2},{7,3},{8,12},{9,13},{10,... | collective-permute-start | bytes 1179656 | tf_op jit(solution)/shard_map/ppermute | solution.py:37
  58.8 18.0 %collective-permute-start.8 = (bf16[512,384]{1,0:T(8,128)(2,1)S(1)}, bf16[512,384]{1,0:T(8,128)(2,1)S(1)}, u32[]{:S(2)}, u32[]{:S(2)}) collective-permute-start(bf16[512,384]{1,0:T(8,128)(2,1)S(1)} %get-tuple-element.46), channel_id=1, source_target_pairs={{0,2},{1,3},{2,4},{3,5},{4,6},{5,7},{6,0},{7,1},{8,10},{9,11},{10,... | collective-permute-start | bytes 1179656 | tf_op jit(solution)/shard_map/ppermute | solution.py:37
  59.5 20.1 %collective-permute-start.9 = (bf16[512,384]{1,0:T(8,128)(2,1)S(1)}, bf16[512,384]{1,0:T(8,128)(2,1)S(1)}, u32[]{:S(2)}, u32[]{:S(2)}) collective-permute-start(bf16[512,384]{1,0:T(8,128)(2,1)S(1)} %get-tuple-element.47), channel_id=1, source_target_pairs={{0,6},{1,7},{2,0},{3,1},{4,2},{5,3},{6,4},{7,5},{8,14},{9,15},{10,... | collective-permute-start | bytes 1179656 | tf_op jit(solution)/shard_map/ppermute | solution.py:37
  62.1 21.4 %collective-permute-start.10 = (bf16[512,384]{1,0:T(8,128)(2,1)S(1)}, bf16[512,384]{1,0:T(8,128)(2,1)S(1)}, u32[]{:S(2)}, u32[]{:S(2)}) collective-permute-start(bf16[512,384]{1,0:T(8,128)(2,1)S(1)} %get-tuple-element.49), channel_id=1, source_target_pairs={{0,2},{1,3},{2,4},{3,5},{4,6},{5,7},{6,0},{7,1},{8,10},{9,11},{10,... | collective-permute-start | bytes 1179656 | tf_op jit(solution)/shard_map/ppermute | solution.py:37
  63.9 20.0 %collective-permute-start.11 = (bf16[512,384]{1,0:T(8,128)(2,1)S(1)}, bf16[512,384]{1,0:T(8,128)(2,1)S(1)}, u32[]{:S(2)}, u32[]{:S(2)}) collective-permute-start(bf16[512,384]{1,0:T(8,128)(2,1)S(1)} %get-tuple-element.50), channel_id=1, source_target_pairs={{0,6},{1,7},{2,0},{3,1},{4,2},{5,3},{6,4},{7,5},{8,14},{9,15},{10,... | collective-permute-start | bytes 1179656 | tf_op jit(solution)/shard_map/ppermute | solution.py:37
  69.3 20.9 %collective-permute-start.12 = (bf16[2,64,384]{2,1,0:T(8,128)(2,1)S(1)}, bf16[2,64,384]{2,1,0:T(8,128)(2,1)S(1)}, u32[]{:S(2)}, u32[]{:S(2)}) collective-permute-start(bf16[2,64,384]{2,1,0:T(8,128)(2,1)S(1)} %get-tuple-element.61), channel_id=1, source_target_pairs={{0,64},{1,65},{2,66},{3,67},{4,68},{5,69},{6,70},{7,71},{8,72},{9,... | collective-permute-start | bytes 294920 | tf_op jit(solution)/shard_map/ppermute | solution.py:37
  76.8 13.5 %collective-permute-start.13 = (bf16[2,64,384]{2,1,0:T(8,128)(2,1)S(1)}, bf16[2,64,384]{2,1,0:T(8,128)(2,1)S(1)}, u32[]{:S(2)}, u32[]{:S(2)}) collective-permute-start(bf16[2,64,384]{2,1,0:T(8,128)(2,1)S(1)} %get-tuple-element.62), channel_id=1, source_target_pairs={{0,128},{1,129},{2,130},{3,131},{4,132},{5,133},{6,134},{7,135},{8... | collective-permute-start | bytes 294920 | tf_op jit(solution)/shard_map/ppermute | solution.py:37
  79.6 10.7 %collective-permute-start.14 = (bf16[2,64,384]{2,1,0:T(8,128)(2,1)S(1)}, bf16[2,64,384]{2,1,0:T(8,128)(2,1)S(1)}, u32[]{:S(2)}, u32[]{:S(2)}) collective-permute-start(bf16[2,64,384]{2,1,0:T(8,128)(2,1)S(1)} %get-tuple-element.63), channel_id=1, source_target_pairs={{0,192},{1,193},{2,194},{3,195},{4,196},{5,197},{6,198},{7,199},{8... | collective-permute-start | bytes 294920 | tf_op jit(solution)/shard_map/ppermute | solution.py:37
  82.2 12.3 %copy-start.7 = (bf16[512,384]{1,0:T(8,128)(2,1)S(1)}, bf16[512,384]{1,0:T(8,128)(2,1)}, u32[]{:S(2)}) copy-start(bf16[512,384]{1,0:T(8,128)(2,1)} %copy-done.5) | copy-start | bytes 1179652
  87.0 43.0 %collective-permute-start.17 = (bf16[1024,384]{1,0:T(8,128)(2,1)S(1)}, bf16[1024,384]{1,0:T(8,128)(2,1)S(1)}, u32[]{:S(2)}, u32[]{:S(2)}) collective-permute-start(bf16[1024,384]{1,0:T(8,128)(2,1)S(1)} %get-tuple-element.65), channel_id=1, source_target_pairs={{0,2},{1,3},{2,4},{3,5},{4,6},{5,7},{6,0},{7,1},{8,10},{9,11},{10,... | collective-permute-start | bytes 2359304 | tf_op jit(solution)/shard_map/ppermute | solution.py:37
  88.4 41.5 %collective-permute-start.18 = (bf16[1024,384]{1,0:T(8,128)(2,1)S(1)}, bf16[1024,384]{1,0:T(8,128)(2,1)S(1)}, u32[]{:S(2)}, u32[]{:S(2)}) collective-permute-start(bf16[1024,384]{1,0:T(8,128)(2,1)S(1)} %get-tuple-element.66), channel_id=1, source_target_pairs={{0,6},{1,7},{2,0},{3,1},{4,2},{5,3},{6,4},{7,5},{8,14},{9,15},{10,... | collective-permute-start | bytes 2359304 | tf_op jit(solution)/shard_map/ppermute | solution.py:37
  90.3 4.2 %collective-permute-start.15 = (bf16[64,384]{1,0:T(8,128)(2,1)S(1)}, bf16[64,384]{1,0:T(8,128)(2,1)S(1)}, u32[]{:S(2)}, u32[]{:S(2)}) collective-permute-start(bf16[64,384]{1,0:T(8,128)(2,1)S(1)} %get-tuple-element.68.down_own), channel_id=1, source_target_pairs={{0,1},{1,0},{2,3},{3,2},{4,5},{5,4},{6,7},{7,6},{8,9},{9,8},{10,11... | collective-permute-start | bytes 147464 | tf_op jit(solution)/shard_map/ppermute | solution.py:37
  94.5 44.2 %copy-start.11 = (s32[32]{0:T(128)S(1)}, s32[32]{0:T(128)}, u32[]{:S(2)}) copy-start(s32[32]{0:T(128)} %counts.5) | copy-start | bytes 388
  96.8 41.9 %copy-start.1 = (bf16[2,1024,384]{2,1,0:T(8,128)(2,1)S(1)}, bf16[2,1024,384]{2,1,0:T(8,128)(2,1)}, u32[]{:S(2)}) copy-start(bf16[2,1024,384]{2,1,0:T(8,128)(2,1)} %residual.5) | copy-start | bytes 4718596
  96.8 41.9 %copy-start.10 = (bf16[2,384]{1,0:T(2,128)(2,1)S(1)}, bf16[2,384]{1,0:T(2,128)(2,1)}, u32[]{:S(2)}) copy-start(bf16[2,384]{1,0:T(2,128)(2,1)} %gate.5) | copy-start | bytes 4612
  96.8 17.7 %collective-permute-start.16 = (bf16[64,2048]{1,0:T(8,128)(2,1)S(1)}, bf16[64,2048]{1,0:T(8,128)(2,1)S(1)}, u32[]{:S(2)}, u32[]{:S(2)}) collective-permute-start(bf16[64,2048]{1,0:T(8,128)(2,1)S(1)} %lowrank.1), channel_id=1, source_target_pairs={{0,2},{1,3},{2,0},{3,1},{4,6},{5,7},{6,4},{7,5},{8,10},{9,11},{10,... | collective-permute-start | bytes 786440 | tf_op jit(solution)/shard_map/ppermute | solution.py:37
  97.0 26.6 %collective-permute-start.19 = (bf16[512,384]{1,0:T(8,128)(2,1)S(1)}, bf16[512,384]{1,0:T(8,128)(2,1)S(1)}, u32[]{:S(2)}, u32[]{:S(2)}) collective-permute-start(bf16[512,384]{1,0:T(8,128)(2,1)S(1)} %get-tuple-element.55), channel_id=1, source_target_pairs={{0,4},{1,5},{2,6},{3,7},{4,0},{5,1},{6,2},{7,3},{8,12},{9,13},{10,... | collective-permute-start | bytes 1179656 | tf_op jit(solution)/shard_map/ppermute | solution.py:37
  99.7 28.0 %collective-permute-start.20 = (bf16[512,384]{1,0:T(8,128)(2,1)S(1)}, bf16[512,384]{1,0:T(8,128)(2,1)S(1)}, u32[]{:S(2)}, u32[]{:S(2)}) collective-permute-start(bf16[512,384]{1,0:T(8,128)(2,1)S(1)} %get-tuple-element.56), channel_id=1, source_target_pairs={{0,2},{1,3},{2,4},{3,5},{4,6},{5,7},{6,0},{7,1},{8,10},{9,11},{10,... | collective-permute-start | bytes 1179656 | tf_op jit(solution)/shard_map/ppermute | solution.py:37
  114.5 15.4 %collective-permute-start.21 = (bf16[512,384]{1,0:T(8,128)(2,1)S(1)}, bf16[512,384]{1,0:T(8,128)(2,1)S(1)}, u32[]{:S(2)}, u32[]{:S(2)}) collective-permute-start(bf16[512,384]{1,0:T(8,128)(2,1)S(1)} %get-tuple-element.57), channel_id=1, source_target_pairs={{0,6},{1,7},{2,0},{3,1},{4,2},{5,3},{6,4},{7,5},{8,14},{9,15},{10,... | collective-permute-start | bytes 1179656 | tf_op jit(solution)/shard_map/ppermute | solution.py:37
  129.9 8.7 %collective-permute-start.22 = (bf16[64,2048]{1,0:T(8,128)(2,1)S(1)}, bf16[64,2048]{1,0:T(8,128)(2,1)S(1)}, u32[]{:S(2)}, u32[]{:S(2)}) collective-permute-start(bf16[64,2048]{1,0:T(8,128)(2,1)S(1)} %add.6), channel_id=1, source_target_pairs={{0,4},{1,5},{2,6},{3,7},{4,0},{5,1},{6,2},{7,3},{8,12},{9,13},{10,... | collective-permute-start | bytes 786440 | tf_op jit(solution)/shard_map/ppermute | solution.py:37
